TPU v7x, 32 devices: a whole 2x2x4 slice. The times are simulated.
32 devices in a mesh: parts: 2 (over x), space: 16 (over z, y, core).
Axes of the slice: x: 2, y: 2, z: 4, core: 2. Of those that a mesh axis runs over, the one named last changes fastest.
Arguments:
- volume: bfloat16 [64, 16, 16, 128], P(('parts', 'space')), parts along dimension 0, may hold values from -6 to 6
- first_filter: bfloat16 [3, 3, 3, 128, 128], replicated, may hold values from -0.109375 to 0.109375
- second_filter: bfloat16 [3, 3, 3, 128, 128], replicated, may hold values from -0.109375 to 0.109375
- cotangent: bfloat16 [64, 16, 16, 128], P(('parts', 'space')), parts along dimension 0, may hold values from -0.06591797 to 0.06591797
Outputs:
- response: bfloat16 [64, 16, 16, 128], P(('parts', 'space')), parts along dimension 0
- first_grad: float32 [256, 3, 3, 3, 128], P(('parts', 'space')), parts along dimension 0
- second_grad: float32 [256, 3, 3, 3, 128], P(('parts', 'space')), parts along dimension 0
There are 2 independent parts, one for each index of `parts`. A program takes and returns all parts, laid end to end along the dimension named above; an argument that names none is the same for every part. Nothing has to cross between parts.
All inputs are finite; a program needn't handle non-finite values.
Results may differ from a plain program's by a relative error of at most 0.0049.
Values may be sent and summed in bfloat16 or wider, within the bound.
No kernel may reach another device: no remote copies, remote signals or barrier semaphores. Data moves between devices by JAX's collectives and lax.ppermute only.
A program may use at most 64 MiB of HBM per device.

v0:
```python
import jax
import jax.numpy as jnp
from jax import lax
from jax.sharding import PartitionSpec as P


def padded_2(shard, sides, width):
    for axis, dim in sides:
        size, length = (lax.axis_size(axis), shard.shape[dim])
        up = [(i, (i + 1) % size) for i in range(size - 1)]
        down = [(j, i) for i, j in up]
        last = lax.slice_in_dim(shard, length - width, length, axis=dim)
        first = lax.slice_in_dim(shard, 0, width, axis=dim)
        before = lax.ppermute(last, axis, up)
        after = lax.ppermute(first, axis, down)
        shard = jnp.concatenate([before, shard, after], axis=dim)
    return shard


def spread(field):
    return jnp.pad(field, ((0, 0), (1, 1), (1, 1), (0, 0)))


def convolve(padded, weight):
    depth = padded.shape[0] - 2
    width = padded.shape[1] - 2
    height = padded.shape[2] - 2
    inner = padded.shape[3]
    total = jnp.zeros((depth * width * height, weight.shape[4]), jnp.float32)
    for plane in range(3):
        for column in range(3):
            slab = jnp.concatenate(
                [
                    padded[plane : plane + depth, column : column + width, lane : lane + height, :]
                    for lane in range(3)
                ],
                axis=-1,
            )
            total = total + jnp.dot(
                slab.reshape(-1, 3 * inner),
                weight[plane, column].reshape(3 * inner, -1),
                preferred_element_type=jnp.float32,
            )
    return total.reshape(depth, width, height, -1)


def weight_term(padded, grads, count):
    depth, width, height, outer = grads.shape
    flat = grads.reshape(-1, outer)
    blocks = []
    for plane in range(3):
        for column in range(3):
            slab = jnp.concatenate(
                [
                    padded[plane : plane + depth, column : column + width, lane : lane + height, :]
                    for lane in range(3)
                ],
                axis=-1,
            )
            term = lax.dot_general(
                slab.reshape(-1, 3 * count),
                flat,
                (((0,), (0,)), ((), ())),
                preferred_element_type=jnp.float32,
            )
            blocks.append(term.reshape(3, count, outer))
    stacked = jnp.stack(blocks, 0).reshape(3, 3, 3, count, outer)
    return jnp.transpose(stacked, (3, 0, 1, 2, 4))


def flipped(weight):
    return jnp.swapaxes(jnp.flip(weight, (0, 1, 2)), 3, 4)


def per_device(volume, first_filter, second_filter, cotangent):
    rim_in = padded_2(volume, (("space", 0),), 1)
    rim_cot = None
    padded_in = spread(rim_in)
    hidden = convolve(padded_in, first_filter)
    activated = jax.nn.silu(hidden).astype(jnp.bfloat16)
    padded_act = spread(padded_2(activated, (("space", 0),), 1))
    response = convolve(padded_act, second_filter).astype(jnp.bfloat16)
    rim_cot = padded_2(cotangent, (("space", 0),), 1)
    padded_cot = spread(rim_cot)
    act_grad = convolve(padded_cot, flipped(second_filter))
    sigma = jax.nn.sigmoid(hidden)
    hidden_grad = (act_grad * sigma * (1.0 + hidden * (1.0 - sigma))).astype(jnp.bfloat16)
    channels = volume.shape[3]
    second_local = weight_term(padded_act, cotangent, channels)
    first_local = weight_term(padded_in, hidden_grad, channels)
    second_grad = lax.psum_scatter(second_local, "space", scatter_dimension=0, tiled=True)
    first_grad = lax.psum_scatter(first_local, "space", scatter_dimension=0, tiled=True)
    return (response, first_grad, second_grad)


def solution(mesh):
    return jax.shard_map(
        per_device,
        mesh=mesh,
        in_specs=(
            P(("parts", "space"), None, None, None),
            P(),
            P(),
            P(("parts", "space"), None, None, None),
        ),
        out_specs=(
            P(("parts", "space"), None, None, None),
            P(("parts", "space"), None, None, None, None),
            P(("parts", "space"), None, None, None, None),
        ),
        check_vma=False,
    )
```

profile of v0, /device:TPU:0, one launch (start us, length us, event | category | flops | bytes accessed | tf_op | source)
XLA Modules:
  0.0 195.9 jit_solution(6003647268394256088)
XLA Ops:
  8.1 2.4 %collective-permute-start = (bf16[1,16,16,128]{3,2,1,0:T(8,128)(2,1)S(1)}, bf16[1,16,16,128]{3,2,1,0:T(8,128)(2,1)S(1)}, u32[]{:S(2)}, u32[]{:S(2)}) collective-permute-start(bf16[1,16,16,128]{3,2,1,0:T(8,128)(2,1)S(1)} %get-tuple-element.115), channel_id=1, source_target_pairs={{0,1},{1,2},{2,3},{3,4},{4,5},{5,6},{6,7},{7,8},{8,9},{9,10},{10,1... | collective-permute-start | bytes 196616 | tf_op jit(solution)/shard_map/ppermute | solution.py:14
  10.5 1.3 collective-permute-start.1
  12.7 5.2 %collective-permute-start.4 = (bf16[1,16,16,128]{3,2,1,0:T(8,128)(2,1)S(1)}, bf16[1,16,16,128]{3,2,1,0:T(8,128)(2,1)S(1)}, u32[]{:S(2)}, u32[]{:S(2)}) collective-permute-start(bf16[1,16,16,128]{3,2,1,0:T(8,128)(2,1)S(1)} %get-tuple-element.105), channel_id=1, source_target_pairs={{0,1},{1,2},{2,3},{3,4},{4,5},{5,6},{6,7},{7,8},{8,9},{9,10},{10,1... | collective-permute-start | bytes 196616 | tf_op jit(solution)/shard_map/ppermute | solution.py:14
  17.8 1.3 collective-permute-start.5
  19.1 2.0 %copy.26 = bf16[3,3,3,128,128]{3,4,2,1,0:T(8,128)(2,1)S(1)} copy(bf16[3,3,3,128,128]{4,3,2,1,0:T(8,128)(2,1)} %param.6) | data formatting | bytes 1769472 | tf_op args[2]
  21.2 1.0 fusion.46
  23.7 1.4 fusion.49
  27.2 1.1 fusion.53
  29.4 1.0 copy.32
  31.4 1.0 copy.29
  33.3 2.3 %fusion.43 = (bf16[2,16,16,384]{3,2,1,0:T(8,128)(2,1)S(1)}, bf16[2,16,16,384]{3,2,1,0:T(8,128)(2,1)}, bf16[2,16,16,384]{3,2,1,0:T(8,128)(2,1)S(1)}, bf16[2,16,16,384]{3,2,1,0:T(8,128)(2,1)S(1)}) fusion(bf16[1,16,16,128]{3,2,1,0:T(8,128)(2,1)} %copy-done.71, bf16[2,16,16,128]{3,2,1,0:T(8,128)(2,1)S(1)} %copy-done.25, ...), kind=kLoop, calls=%fused_computation.99 | loop fusion | flops 5505024 | bytes 3014656 | tf_op jit(solution)/shard_map/concatenate | solution.py:32
  35.7 1.0 copy.25
  36.6 1.9 fusion.58
  39.4 0.9 copy.30
  40.4 1.0 copy.27
  41.3 1.3 convolution_add_fusion.23
  42.6 1.2 convolution_add_fusion.22
  45.8 4.3 %collective-permute-start.2 = (bf16[1,16,16,128]{3,2,1,0:T(8,128)(2,1)S(1)}, bf16[1,16,16,128]{3,2,1,0:T(8,128)(2,1)S(1)}, u32[]{:S(2)}, u32[]{:S(2)}) collective-permute-start(bf16[1,16,16,128]{3,2,1,0:T(8,128)(2,1)S(1)} %get-tuple-element.110), channel_id=1, source_target_pairs={{0,1},{1,2},{2,3},{3,4},{4,5},{5,6},{6,7},{7,8},{8,9},{9,10},{10,1... | collective-permute-start | bytes 196616 | tf_op jit(solution)/shard_map/ppermute | solution.py:14
  50.1 1.3 collective-permute-start.3
  58.5 1.2 copy-done.8
  60.7 1.1 fusion.51
  62.8 1.0 pad_maximum_fusion.19
  64.8 1.0 copy.41
  68.7 2.1 %fusion.39 = (bf16[2,16,16,384]{3,2,1,0:T(8,128)(2,1)S(1)}, bf16[2,16,16,384]{3,2,1,0:T(8,128)(2,1)S(1)}, bf16[2,16,16,384]{3,2,1,0:T(8,128)(2,1)}) fusion(bf16[1,16,16,128]{3,2,1,0:T(8,128)(2,1)} %copy-done.69, bf16[2,16,16,128]{3,2,1,0:T(8,128)(2,1)S(1)} %multiply_convert_fusion, bf16[2,16,16,128]{3,2,1,0:T(8,128)(2,1)} %get-tuple-element.56, ...), kind=kLoop, calls=%fused_computation.93 | loop fusion | flops 4325376 | bytes 2228224 | tf_op jit(solution)/shard_map/concatenate | solution.py:32
  70.9 1.0 copy.42
  72.8 1.9 copy.36
  74.8 1.4 fusion.11
  76.1 1.3 fusion.10
  77.5 1.3 fusion.9
  80.5 1.2 copy-done.9
  85.7 39.8 %reduce-scatter.3.cloned.1.call-done = f32[8,3,3,3,128]{4,0,3,2,1:T(8,128)} async-done(((f32[128,3,3,3,128]{4,0,3,2,1:T(8,128)}), f32[8,3,3,3,128]{4,0,3,2,1:T(8,128)}) %reduce-scatter.3.cloned.1.call-update) | async-done | bytes 110608 | tf_op jit(solution)/shard_map/reduce_scatter | solution.py:92
  125.5 63.5 %reduce-scatter.5.cloned.1.call-done = f32[8,3,3,3,128]{4,0,3,2,1:T(8,128)} async-done(((f32[128,3,3,3,128]{4,0,3,2,1:T(8,128)}), f32[8,3,3,3,128]{4,0,3,2,1:T(8,128)}) %reduce-scatter.5.cloned.1.call-update) | async-done | bytes 110608 | tf_op jit(solution)/shard_map/reduce_scatter | solution.py:91
  (228 shorter events, 30.1 us)
Async XLA Ops:
  7.2 118.4 %reduce-scatter.3.cloned.1.call-start = ((), (), s32[]{:S(2)}) async-start(), calls=%async_computation.2 | async-start | bytes 1880064 | tf_op jit(solution)/shard_map/reduce_scatter | solution.py:92
  8.1 18.0 %collective-permute-start = (bf16[1,16,16,128]{3,2,1,0:T(8,128)(2,1)S(1)}, bf16[1,16,16,128]{3,2,1,0:T(8,128)(2,1)S(1)}, u32[]{:S(2)}, u32[]{:S(2)}) collective-permute-start(bf16[1,16,16,128]{3,2,1,0:T(8,128)(2,1)S(1)} %get-tuple-element.115), channel_id=1, source_target_pairs={{0,1},{1,2},{2,3},{3,4},{4,5},{5,6},{6,7},{7,8},{8,9},{9,10},{10,1... | collective-permute-start | bytes 196616 | tf_op jit(solution)/shard_map/ppermute | solution.py:14
  10.5 15.6 %collective-permute-start.1 = (bf16[1,16,16,128]{3,2,1,0:T(8,128)(2,1)S(1)}, bf16[1,16,16,128]{3,2,1,0:T(8,128)(2,1)S(1)}, u32[]{:S(2)}, u32[]{:S(2)}) collective-permute-start(bf16[1,16,16,128]{3,2,1,0:T(8,128)(2,1)S(1)} %get-tuple-element.116), channel_id=1, source_target_pairs={{1,0},{2,1},{3,2},{4,3},{5,4},{6,5},{7,6},{8,7},{9,8},{10,9},{11,1... | collective-permute-start | bytes 196616 | tf_op jit(solution)/shard_map/ppermute | solution.py:15
  12.7 10.9 %collective-permute-start.4 = (bf16[1,16,16,128]{3,2,1,0:T(8,128)(2,1)S(1)}, bf16[1,16,16,128]{3,2,1,0:T(8,128)(2,1)S(1)}, u32[]{:S(2)}, u32[]{:S(2)}) collective-permute-start(bf16[1,16,16,128]{3,2,1,0:T(8,128)(2,1)S(1)} %get-tuple-element.105), channel_id=1, source_target_pairs={{0,1},{1,2},{2,3},{3,4},{4,5},{5,6},{6,7},{7,8},{8,9},{9,10},{10,1... | collective-permute-start | bytes 196616 | tf_op jit(solution)/shard_map/ppermute | solution.py:14
  17.8 5.7 %collective-permute-start.5 = (bf16[1,16,16,128]{3,2,1,0:T(8,128)(2,1)S(1)}, bf16[1,16,16,128]{3,2,1,0:T(8,128)(2,1)S(1)}, u32[]{:S(2)}, u32[]{:S(2)}) collective-permute-start(bf16[1,16,16,128]{3,2,1,0:T(8,128)(2,1)S(1)} %get-tuple-element.106), channel_id=1, source_target_pairs={{1,0},{2,1},{3,2},{4,3},{5,4},{6,5},{7,6},{8,7},{9,8},{10,9},{11,1... | collective-permute-start | bytes 196616 | tf_op jit(solution)/shard_map/ppermute | solution.py:15
  39.4 4.4 %copy-start.63 = (bf16[1,1,3,128,128]{4,3,2,1,0:T(8,128)(2,1)S(1)}, bf16[1,1,3,128,128]{4,3,2,1,0:T(8,128)(2,1)}, u32[]{:S(2)}) copy-start(bf16[1,1,3,128,128]{4,3,2,1,0:T(8,128)(2,1)} %get-tuple-element.25) | copy-start | bytes 294916
  41.3 2.8 %copy-start.62 = (bf16[1,1,3,128,128]{4,3,2,1,0:T(8,128)(2,1)S(1)}, bf16[1,1,3,128,128]{4,3,2,1,0:T(8,128)(2,1)}, u32[]{:S(2)}) copy-start(bf16[1,1,3,128,128]{4,3,2,1,0:T(8,128)(2,1)} %get-tuple-element.24) | copy-start | bytes 294916
  44.7 6.7 %copy-start.43 = (bf16[2,16,16,128]{3,2,1,0:T(8,128)(2,1)S(1)}, bf16[2,16,16,128]{3,2,1,0:T(8,128)(2,1)}, u32[]{:S(2)}) copy-start(bf16[2,16,16,128]{3,2,1,0:T(8,128)(2,1)} %get-tuple-element.30) | copy-start | bytes 393220
  44.7 6.7 %copy-start.44 = (bf16[2,16,16,128]{3,2,1,0:T(8,128)(2,1)S(1)}, bf16[2,16,16,128]{3,2,1,0:T(8,128)(2,1)}, u32[]{:S(2)}) copy-start(bf16[2,16,16,128]{3,2,1,0:T(8,128)(2,1)} %get-tuple-element.31) | copy-start | bytes 393220
  44.7 6.7 %copy-start.46 = (bf16[2,16,16,128]{3,2,1,0:T(8,128)(2,1)S(1)}, bf16[2,16,16,128]{3,2,1,0:T(8,128)(2,1)}, u32[]{:S(2)}) copy-start(bf16[2,16,16,128]{3,2,1,0:T(8,128)(2,1)} %get-tuple-element.49) | copy-start | bytes 393220
  44.7 6.7 %copy-start.47 = (bf16[2,16,16,128]{3,2,1,0:T(8,128)(2,1)S(1)}, bf16[2,16,16,128]{3,2,1,0:T(8,128)(2,1)}, u32[]{:S(2)}) copy-start(bf16[2,16,16,128]{3,2,1,0:T(8,128)(2,1)} %get-tuple-element.51) | copy-start | bytes 393220
  44.8 6.7 %copy-start.48 = (bf16[2,16,16,128]{3,2,1,0:T(8,128)(2,1)S(1)}, bf16[2,16,16,128]{3,2,1,0:T(8,128)(2,1)}, u32[]{:S(2)}) copy-start(bf16[2,16,16,128]{3,2,1,0:T(8,128)(2,1)} %get-tuple-element.52) | copy-start | bytes 393220
  44.8 6.7 %copy-start.49 = (bf16[2,16,16,128]{3,2,1,0:T(8,128)(2,1)S(1)}, bf16[2,16,16,128]{3,2,1,0:T(8,128)(2,1)}, u32[]{:S(2)}) copy-start(bf16[2,16,16,128]{3,2,1,0:T(8,128)(2,1)} %get-tuple-element.53) | copy-start | bytes 393220
  45.3 6.2 %copy-start.50 = (bf16[1,1,3,128,128]{4,3,2,1,0:T(8,128)(2,1)S(1)}, bf16[1,1,3,128,128]{4,3,2,1,0:T(8,128)(2,1)}, u32[]{:S(2)}) copy-start(bf16[1,1,3,128,128]{4,3,2,1,0:T(8,128)(2,1)} %get-tuple-element.11) | copy-start | bytes 294916
  45.3 6.5 %copy-start.38 = (bf16[2,16,16,128]{3,2,1,0:T(8,128)(2,1)S(1)}, bf16[2,16,16,128]{3,2,1,0:T(8,128)(2,1)}, u32[]{:S(2)}) copy-start(bf16[2,16,16,128]{3,2,1,0:T(8,128)(2,1)} %get-tuple-element.32) | copy-start | bytes 393220
  45.4 6.5 %copy-start.39 = (bf16[2,16,16,128]{3,2,1,0:T(8,128)(2,1)S(1)}, bf16[2,16,16,128]{3,2,1,0:T(8,128)(2,1)}, u32[]{:S(2)}) copy-start(bf16[2,16,16,128]{3,2,1,0:T(8,128)(2,1)} %get-tuple-element.33) | copy-start | bytes 393220
  45.4 6.5 %copy-start.40 = (bf16[2,16,16,128]{3,2,1,0:T(8,128)(2,1)S(1)}, bf16[2,16,16,128]{3,2,1,0:T(8,128)(2,1)}, u32[]{:S(2)}) copy-start(bf16[2,16,16,128]{3,2,1,0:T(8,128)(2,1)} %get-tuple-element.40) | copy-start | bytes 393220
  45.4 6.5 %copy-start.41 = (bf16[2,16,16,128]{3,2,1,0:T(8,128)(2,1)S(1)}, bf16[2,16,16,128]{3,2,1,0:T(8,128)(2,1)}, u32[]{:S(2)}) copy-start(bf16[2,16,16,128]{3,2,1,0:T(8,128)(2,1)} %get-tuple-element.41) | copy-start | bytes 393220
  45.4 6.5 %copy-start.42 = (bf16[2,16,16,128]{3,2,1,0:T(8,128)(2,1)S(1)}, bf16[2,16,16,128]{3,2,1,0:T(8,128)(2,1)}, u32[]{:S(2)}) copy-start(bf16[2,16,16,128]{3,2,1,0:T(8,128)(2,1)} %get-tuple-element.48) | copy-start | bytes 393220
  45.4 6.5 %copy-start.45 = (bf16[2,16,16,128]{3,2,1,0:T(8,128)(2,1)S(1)}, bf16[2,16,16,128]{3,2,1,0:T(8,128)(2,1)}, u32[]{:S(2)}) copy-start(bf16[2,16,16,128]{3,2,1,0:T(8,128)(2,1)} %get-tuple-element.50) | copy-start | bytes 393220
  45.4 6.5 %copy-start.65 = (bf16[1,16,16,128]{3,2,1,0:T(8,128)(2,1)S(1)}, bf16[1,16,16,128]{3,2,1,0:T(8,128)(2,1)}, u32[]{:S(2)}) copy-start(bf16[1,16,16,128]{3,2,1,0:T(8,128)(2,1)} %copy-done.64) | copy-start | bytes 196612
  45.4 6.5 %copy-start.67 = (bf16[1,16,16,128]{3,2,1,0:T(8,128)(2,1)S(1)}, bf16[1,16,16,128]{3,2,1,0:T(8,128)(2,1)}, u32[]{:S(2)}) copy-start(bf16[1,16,16,128]{3,2,1,0:T(8,128)(2,1)} %copy-done.66) | copy-start | bytes 196612
  45.8 14.2 %collective-permute-start.2 = (bf16[1,16,16,128]{3,2,1,0:T(8,128)(2,1)S(1)}, bf16[1,16,16,128]{3,2,1,0:T(8,128)(2,1)S(1)}, u32[]{:S(2)}, u32[]{:S(2)}) collective-permute-start(bf16[1,16,16,128]{3,2,1,0:T(8,128)(2,1)S(1)} %get-tuple-element.110), channel_id=1, source_target_pairs={{0,1},{1,2},{2,3},{3,4},{4,5},{5,6},{6,7},{7,8},{8,9},{9,10},{10,1... | collective-permute-start | bytes 196616 | tf_op jit(solution)/shard_map/ppermute | solution.py:14
  50.1 9.9 %collective-permute-start.3 = (bf16[1,16,16,128]{3,2,1,0:T(8,128)(2,1)S(1)}, bf16[1,16,16,128]{3,2,1,0:T(8,128)(2,1)S(1)}, u32[]{:S(2)}, u32[]{:S(2)}) collective-permute-start(bf16[1,16,16,128]{3,2,1,0:T(8,128)(2,1)S(1)} %get-tuple-element.111), channel_id=1, source_target_pairs={{1,0},{2,1},{3,2},{4,3},{5,4},{6,5},{7,6},{8,7},{9,8},{10,9},{11,1... | collective-permute-start | bytes 196616 | tf_op jit(solution)/shard_map/ppermute | solution.py:15
  59.7 129.3 %reduce-scatter.5.cloned.1.call-start = ((), (), s32[]{:S(2)}) async-start(), calls=%async_computation.3 | async-start | bytes 1880064 | tf_op jit(solution)/shard_map/reduce_scatter | solution.py:91
  70.8 6.6 %copy-start.2 = (bf16[2,16,16,384]{3,2,1,0:T(8,128)(2,1)}, bf16[2,16,16,384]{3,2,1,0:T(8,128)(2,1)S(1)}, u32[]{:S(2)}) copy-start(bf16[2,16,16,384]{3,2,1,0:T(8,128)(2,1)S(1)} %get-tuple-element.107) | copy-start | bytes 1179652
  70.8 6.6 %copy-start.4 = (bf16[2,16,16,384]{3,2,1,0:T(8,128)(2,1)}, bf16[2,16,16,384]{3,2,1,0:T(8,128)(2,1)S(1)}, u32[]{:S(2)}) copy-start(bf16[2,16,16,384]{3,2,1,0:T(8,128)(2,1)S(1)} %get-tuple-element.108) | copy-start | bytes 1179652
  74.7 4.0 %copy-start.22 = (bf16[512,384]{0,1:T(8,128)(2,1)S(1)}, bf16[512,384]{0,1:T(8,128)(2,1)}, u32[]{:S(2)}) copy-start(bf16[512,384]{0,1:T(8,128)(2,1)} %copy.38) | copy-start | bytes 1179652
  74.7 4.3 %copy-start.24 = (bf16[512,384]{0,1:T(8,128)(2,1)S(1)}, bf16[512,384]{0,1:T(8,128)(2,1)}, u32[]{:S(2)}) copy-start(bf16[512,384]{0,1:T(8,128)(2,1)} %copy.39) | copy-start | bytes 1179652
  74.7 4.6 %copy-start.21 = (bf16[512,384]{0,1:T(8,128)(2,1)S(1)}, bf16[512,384]{0,1:T(8,128)(2,1)}, u32[]{:S(2)}) copy-start(bf16[512,384]{0,1:T(8,128)(2,1)} %copy.40) | copy-start | bytes 1179652
  76.1 3.5 %copy-start.20 = (bf16[512,384]{0,1:T(8,128)(2,1)S(1)}, bf16[512,384]{0,1:T(8,128)(2,1)}, u32[]{:S(2)}) copy-start(bf16[512,384]{0,1:T(8,128)(2,1)} %copy.41) | copy-start | bytes 1179652
  77.5 2.4 %copy-start.23 = (bf16[512,384]{0,1:T(8,128)(2,1)S(1)}, bf16[512,384]{0,1:T(8,128)(2,1)}, u32[]{:S(2)}) copy-start(bf16[512,384]{0,1:T(8,128)(2,1)} %copy.42) | copy-start | bytes 1179652
  (49 other events, 61.9 us)
Sparse Core Ops, SparseCore 0:
  59.8 65.6 reduce-scatter.2
  129.9 59.1 reduce-scatter.4
where the time goes:
time: 197 us; the launch traced here: 196 us
  waiting for transfers between devices  103 us (52%)
  local copies, waits for them, and re-layouts  35.1 us (18%)
  matrix products  19.1 us (10%)
  starting transfers between devices  15.9 us (8%)
  between operations  15.4 us (8%)
  other arithmetic  6.97 us (4%)
    reduce_scatter x1, waiting for transfers between devices, per_device(): lax.psum_scatter(second_local, 'space', scatter_dimension=0, tiled=True)  63.5 us
    reduce_scatter x1, waiting for transfers between devices, per_device(): lax.psum_scatter(first_local, 'space', scatter_dimension=0, tiled=True)  39.8 us
    reshape x18, local copies, waits for them, and re-layouts, convolve(): slab.reshape(-1, 3 * inner)  18.1 us
    ppermute x3, starting transfers between devices, padded_2(): before = lax.ppermute(last, axis, up)  11.8 us
    dot_general x27, matrix products, convolve(): jnp.dot(slab.reshape(-1, 3 * inner), weight[plane, column].reshape(3 * in...  11.3 us
    dot_general x18, matrix products, weight_term(): lax.dot_general(slab.reshape(-1, 3 * count), flat, (((0,), (0,)), ((), ()...  7.83 us
    unnamed x147, local copies, waits for them, and re-layouts  7.69 us
    concatenate x15, other arithmetic, convolve(): jnp.concatenate([padded[plane:plane + depth, column:column + width, lane:...  6.39 us
  transfers between devices with their start and end apart: 8, of which 2 were waited for; matrix products, arithmetic and copies ran while one was open for 18% of the time, Pallas kernels for 0%

commit v1 on v0

v1 whole, which is shorter than its diff:
```python
import functools

import jax
import jax.numpy as jnp
from jax import lax
from jax.experimental import pallas as pl
from jax.experimental.pallas import tpu as pltpu
from jax.sharding import PartitionSpec as P

F32 = jnp.float32
BF16 = jnp.bfloat16
VMEM_BYTES = 40 * 2**20


def call(body, out_shape, scratch, flops, moved, name):
    return pl.pallas_call(
        body,
        out_shape=out_shape,
        scratch_shapes=scratch,
        name=name,
        compiler_params=pltpu.CompilerParams(vmem_limit_bytes=VMEM_BYTES),
        cost_estimate=pl.CostEstimate(flops=flops, bytes_accessed=moved, transcendentals=0),
    )


def place(index, size):
    return lax.rem(index, 2), lax.rem(index // 2, 2), index // 4


def edge_rows(wide):
    planes, rows, lanes, channels = wide.shape
    zero = jnp.zeros((planes, 1, lanes, channels), wide.dtype)
    wide[:, 0:1] = zero
    wide[:, rows - 1 : rows] = zero


def moved_lanes(plane):
    length = plane.shape[1]
    at = lax.broadcasted_iota(jnp.int32, plane.shape, 1)
    before = jnp.where(at == 0, 0.0, pltpu.roll(plane, 1, 1))
    after = jnp.where(at == length - 1, 0.0, pltpu.roll(plane, length - 1, 1))
    return before, after


def widen(wide, at, plane):
    rows, _, channels = plane.shape
    before, after = moved_lanes(plane.astype(F32))
    wide[at, 1 : rows + 1, :, 0:channels] = before.astype(BF16)
    wide[at, 1 : rows + 1, :, channels : 2 * channels] = plane.astype(BF16)
    wide[at, 1 : rows + 1, :, 2 * channels : 3 * channels] = after.astype(BF16)


def patch(wide, plane, planes, column):
    rows, lanes, channels = wide.shape[1] - 2, wide.shape[2], wide.shape[3]
    return wide[plane : plane + planes, column : column + rows].reshape(planes * rows * lanes, channels)


def convolve(wide, weight, planes):
    total = None
    for plane in range(3):
        for column in range(3):
            kernel = weight[plane, column]
            term = jnp.dot(
                patch(wide, plane, planes, column),
                kernel.reshape(-1, kernel.shape[-1]),
                preferred_element_type=F32,
            )
            total = term if total is None else total + term
    return total


def convolve_back(wide, weight, planes):
    channels = weight.shape[4]
    total = None
    for plane in range(3):
        for column in range(3):
            block = patch(wide, plane, planes, column)
            for lane in range(3):
                term = lax.dot_general(
                    block[:, lane * channels : (lane + 1) * channels],
                    weight[2 - plane, 2 - column, 2 - lane],
                    (((1,), (1,)), ((), ())),
                    preferred_element_type=F32,
                )
                total = term if total is None else total + term
    return total


def hidden_kernel(size, own, sib, cross, cot, cot_sib, cot_cross, first, second, out, vol_wide, cot_wide):
    core, _, _ = place(lax.axis_index("space"), size)
    for wide, mine, near, far in ((vol_wide, own, sib, cross), (cot_wide, cot, cot_sib, cot_cross)):
        edge_rows(wide)
        widen(wide, 1, mine[0])
        widen(wide, 2, mine[1])
        widen(wide, 3 * core, far[1 - core])
        widen(wide, 3 * (1 - core), near[core])
    hidden = convolve(vol_wide, first, 2)
    sigma = jax.nn.sigmoid(hidden)
    act_grad = convolve_back(cot_wide, second, 2)
    out[0:2] = (hidden * sigma).astype(BF16).reshape(own.shape)
    out[2:4] = (act_grad * sigma * (1.0 + hidden * (1.0 - sigma))).astype(BF16).reshape(own.shape)


def response_kernel(size, act, act_sib, own, cross, first, second, out, vol_wide, act_wide):
    index = lax.axis_index("space")
    core, _, _ = place(index, size)
    edge_rows(vol_wide)
    widen(vol_wide, core, cross[0])
    widen(vol_wide, core + 1, cross[1])
    widen(vol_wide, 2 * (1 - core), own[core])
    hidden = convolve(vol_wide, first, 1)
    inside = jnp.where((index == 0) | (index == size - 1), 0.0, 1.0)
    outer = hidden * jax.nn.sigmoid(hidden) * inside
    edge_rows(act_wide)
    widen(act_wide, 1, act[0])
    widen(act_wide, 2, act[1])
    widen(act_wide, 3 * core, outer.reshape(own.shape[1:]).astype(BF16))
    widen(act_wide, 3 * (1 - core), act_sib[core])
    out[...] = convolve(act_wide, second, 2).astype(BF16).reshape(out.shape)


def channel_choice(size, channels, index):
    core, pair, z = place(index, size)
    group = size // 4
    share = channels // size
    lane = lax.broadcasted_iota(jnp.int32, (channels, channels), 1) % (channels // 2)
    row = lax.broadcasted_iota(jnp.int32, (channels, channels), 0)
    half = channels // 4
    stays = lane // half
    block = (lane % half) // share
    where_z = jnp.bitwise_xor(block, z)
    where_pair = jnp.bitwise_xor(pair, 1 - stays)
    owner = (where_z * 2 + where_pair) * 2 + core
    return jnp.where(row == owner * share + lane % share, 1.0, 0.0).astype(BF16)


def narrow(wide, at, plane, choice):
    rows, lanes, channels = plane.shape
    kept = jnp.dot(plane.reshape(rows * lanes, channels), choice, preferred_element_type=F32)
    kept = kept.reshape(rows, lanes, channels)
    before, after = moved_lanes(kept)
    lane = lax.broadcasted_iota(jnp.int32, kept.shape, 2)
    wide[at, 1 : rows + 1, :, 0:channels] = jnp.where(lane < channels // 2, before, kept).astype(BF16)
    wide[at, 1 : rows + 1, :, channels : 2 * channels] = after.astype(BF16)


def weight_kernel(size, shifted_left, *refs):
    (own, sib, cross, cross_sib, four_own, four_sib, send, keep, wide, turned) = refs
    index = lax.axis_index("space")
    core, _, _ = place(index, size)
    channels = own.shape[-1]
    voxels = own.shape[1] * own.shape[2]
    choice = channel_choice(size, channels, index)
    edge_rows(wide)
    if shifted_left:
        for i in range(2):
            narrow(wide, 1 + i + 2 * core, own[i], choice)
            narrow(wide, 3 + i - 2 * core, sib[i], choice)
            turned[i + 2 * core] = four_own[i].reshape(voxels, channels).astype(F32).T.astype(BF16)
            turned[2 + i - 2 * core] = four_sib[i].reshape(voxels, channels).astype(F32).T.astype(BF16)
        narrow(wide, 5 * core, cross[1 - core], choice)
        narrow(wide, 5 * (1 - core), cross_sib[core], choice)
    else:
        for i in range(2):
            narrow(wide, i + 2 * core, four_own[i], choice)
            narrow(wide, 2 + i - 2 * core, four_sib[i], choice)
            turned[1 + i + 2 * core] = own[i].reshape(voxels, channels).astype(F32).T.astype(BF16)
            turned[3 + i - 2 * core] = sib[i].reshape(voxels, channels).astype(F32).T.astype(BF16)
        turned[5 * core] = cross[1 - core].reshape(voxels, channels).astype(F32).T.astype(BF16)
        turned[5 * (1 - core)] = cross_sib[core].reshape(voxels, channels).astype(F32).T.astype(BF16)
    half = channels // 4
    for column in range(3):
        blocks = [None, None, None]
        for at in range(wide.shape[0]):
            right = patch(wide, at, 1, column)
            if shifted_left:
                pairs = [(a, at - a) for a in range(3) if 0 <= at - a < 4]
            else:
                pairs = [(a, at - a + 2) for a in range(3)]
            left = jnp.concatenate([turned[p] for _, p in pairs], axis=0)
            term = jnp.dot(left, right, preferred_element_type=F32)
            for i, (a, _) in enumerate(pairs):
                piece = term[i * channels : (i + 1) * channels]
                blocks[a] = piece if blocks[a] is None else blocks[a] + piece
        for a in range(3):
            first = blocks[a][:, :channels].T
            second = blocks[a][:, channels:].T
            tap = (a * 3 + column) * 3
            for lane, rows in enumerate((first[: 2 * half], first[2 * half :], second[: 2 * half])):
                send[tap + lane] = rows[:half].astype(BF16)
                keep[tap + lane] = rows[half:]


def pair_sum_kernel(share, keep, got, own, *sends):
    total = keep[...] + got[...].astype(F32)
    taps, _, channels = total.shape
    for q in range(len(sends) + 1):
        block = total[:, q * share : (q + 1) * share].reshape(taps * share, channels)
        if q == 0:
            own[...] = block
        else:
            rows = sends[q - 1].shape[0]
            pad = jnp.zeros((rows - taps * share, channels), F32)
            sends[q - 1][...] = jnp.concatenate([block, pad], axis=0).astype(BF16)


def last_sum_kernel(*refs):
    own, gots, out = refs[0], refs[1:-1], refs[-1]
    rows = own.shape[0]
    total = own[...]
    for got in gots:
        total = total + got[...].astype(F32)[:rows]
    out[...] = total


def per_device(size, volume, first_filter, second_filter, cotangent):
    channels = volume.shape[3]
    share = channels // size
    group = size // 4
    planes, width, height, _ = volume.shape
    voxels = planes * width * height
    slab = volume.size * 2
    unit = 2 * voxels * 27 * channels * channels

    def pairs(move):
        return [(i, move(i)) for i in range(size)]

    across = [(i, i + 1) for i in range(1, size - 1, 2)]
    across = across + [(j, i) for i, j in across]
    sibling = pairs(lambda i: i ^ 1)

    def send(array, moves):
        return lax.ppermute(array, "space", moves)

    vol_cross = send(volume, across)
    vol_sib = send(volume, sibling)
    cot_cross = send(cotangent, across)
    cot_sib = send(cotangent, sibling)

    def wide(count, wide_channels):
        return pltpu.VMEM((count, width + 2, height, wide_channels), BF16)

    both = call(
        functools.partial(hidden_kernel, size),
        jax.ShapeDtypeStruct((2 * planes, width, height, channels), BF16),
        [wide(4, 3 * channels), wide(4, 3 * channels)],
        2 * unit,
        8 * slab + 4 * first_filter.size,
        "hidden",
    )(volume, vol_sib, vol_cross, cotangent, cot_sib, cot_cross, first_filter, second_filter)
    both_sib = send(both, sibling)
    vol_far = send(vol_cross, sibling)
    cot_far = send(cot_cross, sibling)

    response = call(
        functools.partial(response_kernel, size),
        jax.ShapeDtypeStruct(volume.shape, BF16),
        [wide(3, 3 * channels), wide(4, 3 * channels)],
        3 * unit // 2,
        6 * slab + 4 * first_filter.size,
        "response",
    )(both[:planes], both_sib[:planes], volume, vol_cross, first_filter, second_filter)

    def filter_grad(shifted_left, operands, name):
        return call(
            functools.partial(weight_kernel, size, shifted_left),
            (
                jax.ShapeDtypeStruct((27, channels // 4, channels), BF16),
                jax.ShapeDtypeStruct((27, channels // 4, channels), F32),
            ),
            [
                wide(6 if shifted_left else 4, 2 * channels),
                pltpu.VMEM((4 if shifted_left else 6, channels, width * height), BF16),
            ],
            unit,
            6 * slab,
            name,
        )(*operands)

    def pair_sum(keep, got, name):
        if share % 8:
            total = (keep + got.astype(F32)).reshape(27, group, share, channels)
            blocks = [total[:, q].reshape(27 * share, channels) for q in range(group)]
            return [blocks[0]] + [b.astype(BF16) for b in blocks[1:]]
        rows = 27 * share
        padded = -(-rows // 16) * 16
        return call(
            functools.partial(pair_sum_kernel, share),
            (jax.ShapeDtypeStruct((rows, channels), F32),)
            + (jax.ShapeDtypeStruct((padded, channels), BF16),) * (group - 1),
            [],
            keep.size,
            8 * keep.size,
            name,
        )(keep, got)

    def spread_out(blocks):
        return [
            send(block, pairs(lambda i: (((i // 4) ^ q) * 4) + i % 4))
            for q, block in enumerate(blocks[1:], 1)
        ]

    def last_sum(own, gots, name):
        if share % 8:
            total = own
            for got in gots:
                total = total + got.astype(F32)
        else:
            total = call(
                last_sum_kernel, jax.ShapeDtypeStruct(own.shape, F32), [], own.size, 16 * own.size, name
            )(own, *gots)
        return jnp.transpose(total.reshape(3, 3, 3, share, channels), (3, 0, 1, 2, 4))

    pair = pairs(lambda i: i ^ 2)
    act, act_sib = both[:planes], both_sib[:planes]
    grad, grad_sib = both[planes:], both_sib[planes:]
    send_2, keep_2 = filter_grad(False, (cotangent, cot_sib, cot_cross, cot_far, act, act_sib), "second_grad")
    got_2 = send(send_2, pair)
    send_1, keep_1 = filter_grad(True, (volume, vol_sib, vol_cross, vol_far, grad, grad_sib), "first_grad")
    got_1 = send(send_1, pair)
    blocks_2 = pair_sum(keep_2, got_2, "second_pair_sum")
    gots_2 = spread_out(blocks_2)
    blocks_1 = pair_sum(keep_1, got_1, "first_pair_sum")
    gots_1 = spread_out(blocks_1)
    second_grad = last_sum(blocks_2[0], gots_2, "second_last_sum")
    first_grad = last_sum(blocks_1[0], gots_1, "first_last_sum")
    return response, first_grad, second_grad


def solution(mesh):
    size = mesh.shape["space"]
    return jax.shard_map(
        functools.partial(per_device, size),
        mesh=mesh,
        in_specs=(
            P(("parts", "space"), None, None, None),
            P(),
            P(),
            P(("parts", "space"), None, None, None),
        ),
        out_specs=(
            P(("parts", "space"), None, None, None),
            P(("parts", "space"), None, None, None, None),
            P(("parts", "space"), None, None, None, None),
        ),
        check_vma=False,
    )
```

time: 197 us -> 46.7 us (0.24)
  waiting for transfers between devices: 103 us -> 9.8 us
  local copies, waits for them, and re-layouts: 35.1 us -> 4.19 us
  matrix products: 19.1 us -> 0 us
  between operations: 15.4 us -> 0.73 us
  Pallas kernels: 0 us -> 8.96 us
  other arithmetic: 6.97 us -> 0 us
  starting transfers between devices: 15.9 us -> 22.8 us
    reduce_scatter x2 -> x0, waiting for transfers between devices: 103 us -> none  [the longest x1 63.5 us: per_device(): lax.psum_scatter(second_local, 'space', scatter_dimension=0, tiled=True)]
    dot_general x45 -> x0, matrix products: 19.1 us -> none  [the longest x27 11.3 us: convolve(): jnp.dot(slab.reshape(-1, 3 * inner), weight[plane, column].reshape(3 * in...]
    reshape x18 -> x0, local copies, waits for them, and re-layouts: 18.1 us -> none  [convolve(): slab.reshape(-1, 3 * inner)]
    ppermute x6 -> x15, waiting for transfers between devices: 0.02 us -> 9.8 us  [send(): return lax.ppermute(array, 'space', moves)]
    slice x12 -> x2, local copies, waits for them, and re-layouts: 9.26 us -> 0.04 us  [per_device(): grad, grad_sib = (both[planes:], both_sib[planes:])]
    pallas_call x0 -> x8, Pallas kernels: none -> 8.96 us  [the longest x2 2.7 us: filter_grad(): call(functools.partial(weight_kernel, size, shifted_left), (jax.ShapeDtyp...]
    ppermute x6 -> x15, starting transfers between devices: 15.7 us -> 22.8 us  [send(): return lax.ppermute(array, 'space', moves)]
    concatenate x18 -> x0, other arithmetic: 6.89 us -> none  [the longest x15 6.39 us: convolve(): jnp.concatenate([padded[plane:plane + depth, column:column + width, lane:...]
  transfers between devices with their start and end apart: 8 -> 15, of which waited for: 2 -> 7; matrix products, arithmetic and copies ran while one was open for 18% -> 0% of each run, Pallas kernels for 0% -> 13%
where the time goes in v1:
time: 46.7 us; the launch traced here: 46.4 us
  starting transfers between devices  22.8 us (49%)
  waiting for transfers between devices  9.8 us (21%)
  Pallas kernels  8.96 us (19%)
  local copies, waits for them, and re-layouts  4.19 us (9%)
  between operations  0.73 us (2%)
    ppermute x15, starting transfers between devices, send(): return lax.ppermute(array, 'space', moves)  22.8 us
    ppermute x15, waiting for transfers between devices, send(): return lax.ppermute(array, 'space', moves)  9.8 us
    unnamed x14, local copies, waits for them, and re-layouts  4.16 us
    pallas_call x2, Pallas kernels, filter_grad(): call(functools.partial(weight_kernel, size, shifted_left), (jax.ShapeDtyp...  2.7 us
    pallas_call x1, Pallas kernels, per_device(): call(functools.partial(response_kernel, size), jax.ShapeDtypeStruct(volum...  2.56 us
    pallas_call x1, Pallas kernels, per_device(): call(functools.partial(hidden_kernel, size), jax.ShapeDtypeStruct((2 * pl...  2.23 us
    pallas_call x2, Pallas kernels, last_sum(): call(last_sum_kernel, jax.ShapeDtypeStruct(own.shape, F32), [], own.size,...  1.35 us
  transfers between devices with their start and end apart: 15, of which 7 were waited for; matrix products, arithmetic and copies ran while one was open for 0% of the time, Pallas kernels for 13%

profile of v1, /device:TPU:0, one launch (start us, length us, event | category | flops | bytes accessed | tf_op | source)
XLA Modules:
  0.0 46.4 jit_solution(9549883067372617245)
XLA Ops:
  0.6 0.7 %collective-permute-start.1 = (bf16[2,16,16,128]{3,2,1,0:T(8,128)(2,1)}, bf16[2,16,16,128]{3,2,1,0:T(8,128)(2,1)S(1)}, u32[]{:S(2)}, u32[]{:S(2)}) collective-permute-start(bf16[2,16,16,128]{3,2,1,0:T(8,128)(2,1)} %refs_0_.2), channel_id=1, source_target_pairs={{1,2},{3,4},{5,6},{7,8},{9,10},{11,12},{13,14},{2,1},{4,3},{6,5},{... | collective-permute-start | bytes 393224 | tf_op jit(solution)/shard_map/ppermute | solution.py:233
  1.3 0.7 %collective-permute-start.3 = (bf16[2,16,16,128]{3,2,1,0:T(8,128)(2,1)}, bf16[2,16,16,128]{3,2,1,0:T(8,128)(2,1)S(1)}, u32[]{:S(2)}, u32[]{:S(2)}) collective-permute-start(bf16[2,16,16,128]{3,2,1,0:T(8,128)(2,1)} %refs_0_.3), channel_id=1, source_target_pairs={{1,2},{3,4},{5,6},{7,8},{9,10},{11,12},{13,14},{2,1},{4,3},{6,5},{... | collective-permute-start | bytes 393224 | tf_op jit(solution)/shard_map/ppermute | solution.py:233
  2.0 5.6 %collective-permute-start = (bf16[2,16,16,128]{3,2,1,0:T(8,128)(2,1)}, bf16[2,16,16,128]{3,2,1,0:T(8,128)(2,1)S(1)}, u32[]{:S(2)}, u32[]{:S(2)}) collective-permute-start(bf16[2,16,16,128]{3,2,1,0:T(8,128)(2,1)} %refs_0_.2), channel_id=1, source_target_pairs={{0,1},{1,0},{2,3},{3,2},{4,5},{5,4},{6,7},{7,6},{8,9},{9,8},{10,11... | collective-permute-start | bytes 393224 | tf_op jit(solution)/shard_map/ppermute | solution.py:233
  7.6 0.1 collective-permute-start.2
  7.7 1.1 %collective-permute-done.sib.refs_1_ = bf16[2,16,16,128]{3,2,1,0:T(8,128)(2,1)S(1)} collective-permute-done((bf16[2,16,16,128]{3,2,1,0:T(8,128)(2,1)}, bf16[2,16,16,128]{3,2,1,0:T(8,128)(2,1)S(1)}, u32[]{:S(2)}, u32[]{:S(2)}) %collective-permute-start) | collective-permute-done | bytes 131104 | tf_op jit(solution)/shard_map/ppermute | solution.py:233
  8.8 0.4 collective-permute-done.2.cot_sib.refs_1_
  9.2 1.2 %copy-done = bf16[3,3,3,128,128]{4,3,2,1,0:T(8,128)(2,1)S(1)} copy-done((bf16[3,3,3,128,128]{4,3,2,1,0:T(8,128)(2,1)S(1)}, bf16[3,3,3,128,128]{4,3,2,1,0:T(8,128)(2,1)}, u32[]{:S(2)}) %copy-start) | copy-done | bytes 884760
  10.4 1.2 %copy-done.2 = bf16[3,3,3,128,128]{4,3,2,1,0:T(8,128)(2,1)S(1)} copy-done((bf16[3,3,3,128,128]{4,3,2,1,0:T(8,128)(2,1)S(1)}, bf16[3,3,3,128,128]{4,3,2,1,0:T(8,128)(2,1)}, u32[]{:S(2)}) %copy-start.2) | copy-done | bytes 884760
  11.5 0.9 %copy-done.4 = bf16[2,16,16,128]{3,2,1,0:T(8,128)(2,1)S(1)} copy-done((bf16[2,16,16,128]{3,2,1,0:T(8,128)(2,1)S(1)}, bf16[2,16,16,128]{3,2,1,0:T(8,128)(2,1)}, u32[]{:S(2)}) %copy-start.4) | copy-done | bytes 131096
  12.4 0.9 %copy-done.5 = bf16[2,16,16,128]{3,2,1,0:T(8,128)(2,1)S(1)} copy-done((bf16[2,16,16,128]{3,2,1,0:T(8,128)(2,1)S(1)}, bf16[2,16,16,128]{3,2,1,0:T(8,128)(2,1)}, u32[]{:S(2)}) %copy-start.5) | copy-done | bytes 131096
  13.3 2.2 %hidden.1 = bf16[4,16,16,128]{3,2,1,0:T(8,128)(2,1)S(1)} custom-call(bf16[2,16,16,128]{3,2,1,0:T(8,128)(2,1)S(1)} %copy-done.5, bf16[2,16,16,128]{3,2,1,0:T(8,128)(2,1)S(1)} %collective-permute-done.sib.refs_1_, bf16[2,16,16,128]{3,2,1,0:T(8,128)(2,1)S(1)} %collective-permute-done.1.cross.refs_2_, bf16[2,16,16,128]{3,2,1,0:T(8,128)(2,1)S(1)} %copy-done.4, ...), custom_call_target="tpu_custom_call" | custom-call | flops 905969664 | bytes 2818048 | tf_op jit(solution)/shard_map/hidden/pallas_call | solution.py:243
  15.6 3.0 %collective-permute-start.4 = (bf16[4,16,16,128]{3,2,1,0:T(8,128)(2,1)S(1)}, bf16[4,16,16,128]{3,2,1,0:T(8,128)(2,1)S(1)}, u32[]{:S(2)}, u32[]{:S(2)}) collective-permute-start(bf16[4,16,16,128]{3,2,1,0:T(8,128)(2,1)S(1)} %hidden.1), channel_id=1, source_target_pairs={{0,1},{1,0},{2,3},{3,2},{4,5},{5,4},{6,7},{7,6},{8,9},{9,8},{10,11... | collective-permute-start | bytes 786440 | tf_op jit(solution)/shard_map/ppermute | solution.py:233
  18.6 0.1 collective-permute-start.10
  18.7 0.4 collective-permute-start.5
  19.1 0.6 %collective-permute-done.4 = bf16[4,16,16,128]{3,2,1,0:T(8,128)(2,1)S(1)} collective-permute-done((bf16[4,16,16,128]{3,2,1,0:T(8,128)(2,1)S(1)}, bf16[4,16,16,128]{3,2,1,0:T(8,128)(2,1)S(1)}, u32[]{:S(2)}, u32[]{:S(2)}) %collective-permute-start.4) | collective-permute-done | bytes 262176 | tf_op jit(solution)/shard_map/ppermute | solution.py:233
  19.8 0.2 collective-permute-done.10.refs_3_
  19.9 1.4 %second_grad.1 = (bf16[27,32,128]{2,1,0:T(8,128)(2,1)S(1)}, f32[27,32,128]{2,1,0:T(8,128)S(1)}) custom-call(bf16[2,16,16,128]{3,2,1,0:T(8,128)(2,1)S(1)} %copy-done.4, bf16[2,16,16,128]{3,2,1,0:T(8,128)(2,1)S(1)} %collective-permute-done.2.cot_sib.refs_1_, bf16[2,16,16,128]{3,2,1,0:T(8,128)(2,1)S(1)} %collective-permute-done.3.cot_cross.refs_2_, ...), custom_call_target="tpu_custom_call" | custom-call | flops 452984832 | bytes 786432 | tf_op jit(solution)/shard_map/second_grad/pallas_call | solution.py:265
  21.3 2.5 %collective-permute-start.11 = (bf16[27,32,128]{2,1,0:T(8,128)(2,1)S(1)}, bf16[27,32,128]{2,1,0:T(8,128)(2,1)S(1)}, u32[]{:S(2)}, u32[]{:S(2)}) collective-permute-start(bf16[27,32,128]{2,1,0:T(8,128)(2,1)S(1)} %get-tuple-element.22), channel_id=1, source_target_pairs={{0,2},{1,3},{2,0},{3,1},{4,6},{5,7},{6,4},{7,5},{8,10},{9,11},{10,... | collective-permute-start | bytes 663560 | tf_op jit(solution)/shard_map/ppermute | solution.py:233
  23.8 1.3 %first_grad.1 = (bf16[27,32,128]{2,1,0:T(8,128)(2,1)S(1)}, f32[27,32,128]{2,1,0:T(8,128)S(1)}) custom-call(bf16[2,16,16,128]{3,2,1,0:T(8,128)(2,1)S(1)} %copy-done.5, bf16[2,16,16,128]{3,2,1,0:T(8,128)(2,1)S(1)} %collective-permute-done.sib.refs_1_, bf16[2,16,16,128]{3,2,1,0:T(8,128)(2,1)S(1)} %collective-permute-done.1.cross.refs_2_, ...), custom_call_target="tpu_custom_call" | custom-call | flops 452984832 | bytes 786432 | tf_op jit(solution)/shard_map/first_grad/pallas_call | solution.py:265
  25.2 0.1 collective-permute-start.6
  25.2 4.8 %collective-permute-done.11.got = bf16[27,32,128]{2,1,0:T(8,128)(2,1)S(1)} collective-permute-done((bf16[27,32,128]{2,1,0:T(8,128)(2,1)S(1)}, bf16[27,32,128]{2,1,0:T(8,128)(2,1)S(1)}, u32[]{:S(2)}, u32[]{:S(2)}) %collective-permute-start.11) | collective-permute-done | bytes 221216 | tf_op jit(solution)/shard_map/ppermute | solution.py:233
  30.1 0.1 second_pair_sum.1
  30.1 2.5 %collective-permute-start.12 = (bf16[224,128]{1,0:T(8,128)(2,1)S(1)}, bf16[224,128]{1,0:T(8,128)(2,1)S(1)}, u32[]{:S(2)}, u32[]{:S(2)}) collective-permute-start(bf16[224,128]{1,0:T(8,128)(2,1)S(1)} %get-tuple-element.24), channel_id=1, source_target_pairs={{0,4},{1,5},{2,6},{3,7},{4,0},{5,1},{6,2},{7,3},{8,12},{9,13},{10,... | collective-permute-start | bytes 172040 | tf_op jit(solution)/shard_map/ppermute | solution.py:233
  32.7 2.6 %collective-permute-start.13 = (bf16[224,128]{1,0:T(8,128)(2,1)S(1)}, bf16[224,128]{1,0:T(8,128)(2,1)S(1)}, u32[]{:S(2)}, u32[]{:S(2)}) collective-permute-start(bf16[224,128]{1,0:T(8,128)(2,1)S(1)} %get-tuple-element.25), channel_id=1, source_target_pairs={{0,8},{1,9},{2,10},{3,11},{4,12},{5,13},{6,14},{7,15},{8,0},{9,1},... | collective-permute-start | bytes 172040 | tf_op jit(solution)/shard_map/ppermute | solution.py:233
  35.3 0.1 first_pair_sum.1
  35.3 1.5 %collective-permute-start.7 = (bf16[224,128]{1,0:T(8,128)(2,1)S(1)}, bf16[224,128]{1,0:T(8,128)(2,1)S(1)}, u32[]{:S(2)}, u32[]{:S(2)}) collective-permute-start(bf16[224,128]{1,0:T(8,128)(2,1)S(1)} %get-tuple-element.18), channel_id=1, source_target_pairs={{0,4},{1,5},{2,6},{3,7},{4,0},{5,1},{6,2},{7,3},{8,12},{9,13},{10,... | collective-permute-start | bytes 172040 | tf_op jit(solution)/shard_map/ppermute | solution.py:233
  36.9 2.9 %collective-permute-start.8 = (bf16[224,128]{1,0:T(8,128)(2,1)S(1)}, bf16[224,128]{1,0:T(8,128)(2,1)S(1)}, u32[]{:S(2)}, u32[]{:S(2)}) collective-permute-start(bf16[224,128]{1,0:T(8,128)(2,1)S(1)} %get-tuple-element.19), channel_id=1, source_target_pairs={{0,8},{1,9},{2,10},{3,11},{4,12},{5,13},{6,14},{7,15},{8,0},{9,1},... | collective-permute-start | bytes 172040 | tf_op jit(solution)/shard_map/ppermute | solution.py:233
  39.8 2.6 %response.1 = bf16[2,16,16,128]{3,2,1,0:T(8,128)(2,1)} custom-call(bf16[2,16,16,128]{3,2,1,0:T(8,128)(2,1)S(1)} %get-tuple-element.30.act.refs_4_, bf16[2,16,16,128]{3,2,1,0:T(8,128)(2,1)S(1)} %get-tuple-element.28.act_sib.refs_5_, bf16[2,16,16,128]{3,2,1,0:T(8,128)(2,1)S(1)} %copy-done.6, bf16[2,16,16,128]{3,2,1,0:T(8,128)(2,1)S(1)} %collective-permute-done.1.cross.refs_2_, ...), custom_call_target="tpu_custom_call" | custom-call | flops 679477248 | bytes 2555904 | tf_op jit(solution)/shard_map/response/pallas_call | solution.py:255
  42.4 0.7 %second_last_sum.1 = f32[216,128]{1,0:T(8,128)} custom-call(f32[216,128]{1,0:T(8,128)S(1)} %get-tuple-element.23.refs_0_, bf16[224,128]{1,0:T(8,128)(2,1)S(1)} %collective-permute-done.12.refs_1_, bf16[224,128]{1,0:T(8,128)(2,1)S(1)} %collective-permute-done.13.refs_2_, bf16[224,128]{1,0:T(8,128)(2,1)S(1)} %collective-permute-done.14.refs_3_), custom_call_target="tpu_custom_call" | custom-call | flops 27648 | bytes 442368 | tf_op jit(solution)/shard_map/second_last_sum/pallas_call | solution.py:309
  43.1 0.9 %collective-permute-done.8.refs_2_ = bf16[224,128]{1,0:T(8,128)(2,1)S(1)} collective-permute-done((bf16[224,128]{1,0:T(8,128)(2,1)S(1)}, bf16[224,128]{1,0:T(8,128)(2,1)S(1)}, u32[]{:S(2)}, u32[]{:S(2)}) %collective-permute-start.8) | collective-permute-done | bytes 57376 | tf_op jit(solution)/shard_map/ppermute | solution.py:233
  43.9 1.8 %collective-permute-done.9.refs_3_ = bf16[224,128]{1,0:T(8,128)(2,1)S(1)} collective-permute-done((bf16[224,128]{1,0:T(8,128)(2,1)S(1)}, bf16[224,128]{1,0:T(8,128)(2,1)S(1)}, u32[]{:S(2)}, u32[]{:S(2)}) %collective-permute-start.9) | collective-permute-done | bytes 57376 | tf_op jit(solution)/shard_map/ppermute | solution.py:233
  45.8 0.7 %first_last_sum.1 = f32[216,128]{1,0:T(8,128)} custom-call(f32[216,128]{1,0:T(8,128)S(1)} %get-tuple-element.17.refs_0_, bf16[224,128]{1,0:T(8,128)(2,1)S(1)} %collective-permute-done.7.refs_1_, bf16[224,128]{1,0:T(8,128)(2,1)S(1)} %collective-permute-done.8.refs_2_, bf16[224,128]{1,0:T(8,128)(2,1)S(1)} %collective-permute-done.9.refs_3_), custom_call_target="tpu_custom_call" | custom-call | flops 27648 | bytes 442368 | tf_op jit(solution)/shard_map/first_last_sum/pallas_call | solution.py:309
  (22 shorter events, 0.1 us)
Async XLA Ops:
  0.6 7.1 %collective-permute-start.1 = (bf16[2,16,16,128]{3,2,1,0:T(8,128)(2,1)}, bf16[2,16,16,128]{3,2,1,0:T(8,128)(2,1)S(1)}, u32[]{:S(2)}, u32[]{:S(2)}) collective-permute-start(bf16[2,16,16,128]{3,2,1,0:T(8,128)(2,1)} %refs_0_.2), channel_id=1, source_target_pairs={{1,2},{3,4},{5,6},{7,8},{9,10},{11,12},{13,14},{2,1},{4,3},{6,5},{... | collective-permute-start | bytes 393224 | tf_op jit(solution)/shard_map/ppermute | solution.py:233
  1.3 6.4 %collective-permute-start.3 = (bf16[2,16,16,128]{3,2,1,0:T(8,128)(2,1)}, bf16[2,16,16,128]{3,2,1,0:T(8,128)(2,1)S(1)}, u32[]{:S(2)}, u32[]{:S(2)}) collective-permute-start(bf16[2,16,16,128]{3,2,1,0:T(8,128)(2,1)} %refs_0_.3), channel_id=1, source_target_pairs={{1,2},{3,4},{5,6},{7,8},{9,10},{11,12},{13,14},{2,1},{4,3},{6,5},{... | collective-permute-start | bytes 393224 | tf_op jit(solution)/shard_map/ppermute | solution.py:233
  2.0 6.8 %collective-permute-start = (bf16[2,16,16,128]{3,2,1,0:T(8,128)(2,1)}, bf16[2,16,16,128]{3,2,1,0:T(8,128)(2,1)S(1)}, u32[]{:S(2)}, u32[]{:S(2)}) collective-permute-start(bf16[2,16,16,128]{3,2,1,0:T(8,128)(2,1)} %refs_0_.2), channel_id=1, source_target_pairs={{0,1},{1,0},{2,3},{3,2},{4,5},{5,4},{6,7},{7,6},{8,9},{9,8},{10,11... | collective-permute-start | bytes 393224 | tf_op jit(solution)/shard_map/ppermute | solution.py:233
  7.6 1.6 %collective-permute-start.2 = (bf16[2,16,16,128]{3,2,1,0:T(8,128)(2,1)}, bf16[2,16,16,128]{3,2,1,0:T(8,128)(2,1)S(1)}, u32[]{:S(2)}, u32[]{:S(2)}) collective-permute-start(bf16[2,16,16,128]{3,2,1,0:T(8,128)(2,1)} %refs_0_.3), channel_id=1, source_target_pairs={{0,1},{1,0},{2,3},{3,2},{4,5},{5,4},{6,7},{7,6},{8,9},{9,8},{10,11... | collective-permute-start | bytes 393224 | tf_op jit(solution)/shard_map/ppermute | solution.py:233
  9.2 1.2 %copy-start = (bf16[3,3,3,128,128]{4,3,2,1,0:T(8,128)(2,1)S(1)}, bf16[3,3,3,128,128]{4,3,2,1,0:T(8,128)(2,1)}, u32[]{:S(2)}) copy-start(bf16[3,3,3,128,128]{4,3,2,1,0:T(8,128)(2,1)} %first.3) | copy-start | bytes 2654212
  10.4 1.2 %copy-start.2 = (bf16[3,3,3,128,128]{4,3,2,1,0:T(8,128)(2,1)S(1)}, bf16[3,3,3,128,128]{4,3,2,1,0:T(8,128)(2,1)}, u32[]{:S(2)}) copy-start(bf16[3,3,3,128,128]{4,3,2,1,0:T(8,128)(2,1)} %second.3) | copy-start | bytes 2654212
  11.5 0.9 %copy-start.4 = (bf16[2,16,16,128]{3,2,1,0:T(8,128)(2,1)S(1)}, bf16[2,16,16,128]{3,2,1,0:T(8,128)(2,1)}, u32[]{:S(2)}) copy-start(bf16[2,16,16,128]{3,2,1,0:T(8,128)(2,1)} %refs_0_.3) | copy-start | bytes 393220
  12.4 0.9 %copy-start.5 = (bf16[2,16,16,128]{3,2,1,0:T(8,128)(2,1)S(1)}, bf16[2,16,16,128]{3,2,1,0:T(8,128)(2,1)}, u32[]{:S(2)}) copy-start(bf16[2,16,16,128]{3,2,1,0:T(8,128)(2,1)} %refs_0_.2) | copy-start | bytes 393220
  15.6 4.2 %collective-permute-start.4 = (bf16[4,16,16,128]{3,2,1,0:T(8,128)(2,1)S(1)}, bf16[4,16,16,128]{3,2,1,0:T(8,128)(2,1)S(1)}, u32[]{:S(2)}, u32[]{:S(2)}) collective-permute-start(bf16[4,16,16,128]{3,2,1,0:T(8,128)(2,1)S(1)} %hidden.1), channel_id=1, source_target_pairs={{0,1},{1,0},{2,3},{3,2},{4,5},{5,4},{6,7},{7,6},{8,9},{9,8},{10,11... | collective-permute-start | bytes 786440 | tf_op jit(solution)/shard_map/ppermute | solution.py:233
  18.6 1.3 %collective-permute-start.10 = (bf16[2,16,16,128]{3,2,1,0:T(8,128)(2,1)S(1)}, bf16[2,16,16,128]{3,2,1,0:T(8,128)(2,1)S(1)}, u32[]{:S(2)}, u32[]{:S(2)}) collective-permute-start(bf16[2,16,16,128]{3,2,1,0:T(8,128)(2,1)S(1)} %collective-permute-done.3.cot_cross.refs_2_), channel_id=1, source_target_pairs={{0,1},{1,0},{2,3},{3,2},{4,5},{5,4},{6,7},{7,6},{8,9},{9,8},{10,11... | collective-permute-start | bytes 393224 | tf_op jit(solution)/shard_map/ppermute | solution.py:233
  18.7 5.2 %collective-permute-start.5 = (bf16[2,16,16,128]{3,2,1,0:T(8,128)(2,1)S(1)}, bf16[2,16,16,128]{3,2,1,0:T(8,128)(2,1)S(1)}, u32[]{:S(2)}, u32[]{:S(2)}) collective-permute-start(bf16[2,16,16,128]{3,2,1,0:T(8,128)(2,1)S(1)} %collective-permute-done.1.cross.refs_2_), channel_id=1, source_target_pairs={{0,1},{1,0},{2,3},{3,2},{4,5},{5,4},{6,7},{7,6},{8,9},{9,8},{10,11... | collective-permute-start | bytes 393224 | tf_op jit(solution)/shard_map/ppermute | solution.py:233
  21.3 8.8 %collective-permute-start.11 = (bf16[27,32,128]{2,1,0:T(8,128)(2,1)S(1)}, bf16[27,32,128]{2,1,0:T(8,128)(2,1)S(1)}, u32[]{:S(2)}, u32[]{:S(2)}) collective-permute-start(bf16[27,32,128]{2,1,0:T(8,128)(2,1)S(1)} %get-tuple-element.22), channel_id=1, source_target_pairs={{0,2},{1,3},{2,0},{3,1},{4,6},{5,7},{6,4},{7,5},{8,10},{9,11},{10,... | collective-permute-start | bytes 663560 | tf_op jit(solution)/shard_map/ppermute | solution.py:233
  23.8 16.0 %copy-start.3 = (bf16[3,3,3,128,128]{4,3,2,1,0:T(8,128)(2,1)S(1)}, bf16[3,3,3,128,128]{4,3,2,1,0:T(8,128)(2,1)}, u32[]{:S(2)}) copy-start(bf16[3,3,3,128,128]{4,3,2,1,0:T(8,128)(2,1)} %second.3) | copy-start | bytes 2654212
  25.2 14.6 %copy-start.1 = (bf16[3,3,3,128,128]{4,3,2,1,0:T(8,128)(2,1)S(1)}, bf16[3,3,3,128,128]{4,3,2,1,0:T(8,128)(2,1)}, u32[]{:S(2)}) copy-start(bf16[3,3,3,128,128]{4,3,2,1,0:T(8,128)(2,1)} %first.3) | copy-start | bytes 2654212
  25.2 10.1 %collective-permute-start.6 = (bf16[27,32,128]{2,1,0:T(8,128)(2,1)S(1)}, bf16[27,32,128]{2,1,0:T(8,128)(2,1)S(1)}, u32[]{:S(2)}, u32[]{:S(2)}) collective-permute-start(bf16[27,32,128]{2,1,0:T(8,128)(2,1)S(1)} %get-tuple-element.16), channel_id=1, source_target_pairs={{0,2},{1,3},{2,0},{3,1},{4,6},{5,7},{6,4},{7,5},{8,10},{9,11},{10,... | collective-permute-start | bytes 663560 | tf_op jit(solution)/shard_map/ppermute | solution.py:233
  30.1 9.7 %collective-permute-start.12 = (bf16[224,128]{1,0:T(8,128)(2,1)S(1)}, bf16[224,128]{1,0:T(8,128)(2,1)S(1)}, u32[]{:S(2)}, u32[]{:S(2)}) collective-permute-start(bf16[224,128]{1,0:T(8,128)(2,1)S(1)} %get-tuple-element.24), channel_id=1, source_target_pairs={{0,4},{1,5},{2,6},{3,7},{4,0},{5,1},{6,2},{7,3},{8,12},{9,13},{10,... | collective-permute-start | bytes 172040 | tf_op jit(solution)/shard_map/ppermute | solution.py:233
  32.7 9.7 %collective-permute-start.13 = (bf16[224,128]{1,0:T(8,128)(2,1)S(1)}, bf16[224,128]{1,0:T(8,128)(2,1)S(1)}, u32[]{:S(2)}, u32[]{:S(2)}) collective-permute-start(bf16[224,128]{1,0:T(8,128)(2,1)S(1)} %get-tuple-element.25), channel_id=1, source_target_pairs={{0,8},{1,9},{2,10},{3,11},{4,12},{5,13},{6,14},{7,15},{8,0},{9,1},... | collective-permute-start | bytes 172040 | tf_op jit(solution)/shard_map/ppermute | solution.py:233
  35.3 7.1 %collective-permute-start.14 = (bf16[224,128]{1,0:T(8,128)(2,1)S(1)}, bf16[224,128]{1,0:T(8,128)(2,1)S(1)}, u32[]{:S(2)}, u32[]{:S(2)}) collective-permute-start(bf16[224,128]{1,0:T(8,128)(2,1)S(1)} %get-tuple-element.26), channel_id=1, source_target_pairs={{0,12},{1,13},{2,14},{3,15},{4,8},{5,9},{6,10},{7,11},{8,4},{9,5},... | collective-permute-start | bytes 172040 | tf_op jit(solution)/shard_map/ppermute | solution.py:233
  35.3 4.5 %copy-start.6 = (bf16[2,16,16,128]{3,2,1,0:T(8,128)(2,1)S(1)}, bf16[2,16,16,128]{3,2,1,0:T(8,128)(2,1)}, u32[]{:S(2)}) copy-start(bf16[2,16,16,128]{3,2,1,0:T(8,128)(2,1)} %refs_0_.2) | copy-start | bytes 393220
  35.3 7.7 %collective-permute-start.7 = (bf16[224,128]{1,0:T(8,128)(2,1)S(1)}, bf16[224,128]{1,0:T(8,128)(2,1)S(1)}, u32[]{:S(2)}, u32[]{:S(2)}) collective-permute-start(bf16[224,128]{1,0:T(8,128)(2,1)S(1)} %get-tuple-element.18), channel_id=1, source_target_pairs={{0,4},{1,5},{2,6},{3,7},{4,0},{5,1},{6,2},{7,3},{8,12},{9,13},{10,... | collective-permute-start | bytes 172040 | tf_op jit(solution)/shard_map/ppermute | solution.py:233
  36.9 7.1 %collective-permute-start.8 = (bf16[224,128]{1,0:T(8,128)(2,1)S(1)}, bf16[224,128]{1,0:T(8,128)(2,1)S(1)}, u32[]{:S(2)}, u32[]{:S(2)}) collective-permute-start(bf16[224,128]{1,0:T(8,128)(2,1)S(1)} %get-tuple-element.19), channel_id=1, source_target_pairs={{0,8},{1,9},{2,10},{3,11},{4,12},{5,13},{6,14},{7,15},{8,0},{9,1},... | collective-permute-start | bytes 172040 | tf_op jit(solution)/shard_map/ppermute | solution.py:233
  39.8 6.0 %collective-permute-start.9 = (bf16[224,128]{1,0:T(8,128)(2,1)S(1)}, bf16[224,128]{1,0:T(8,128)(2,1)S(1)}, u32[]{:S(2)}, u32[]{:S(2)}) collective-permute-start(bf16[224,128]{1,0:T(8,128)(2,1)S(1)} %get-tuple-element.20), channel_id=1, source_target_pairs={{0,12},{1,13},{2,14},{3,15},{4,8},{5,9},{6,10},{7,11},{8,4},{9,5},... | collective-permute-start | bytes 172040 | tf_op jit(solution)/shard_map/ppermute | solution.py:233

commit v2 on v1

--- a/solution.py
+++ b/solution.py
@@ -86,37 +86,59 @@
     return total
 
 
-def hidden_kernel(size, own, sib, cross, cot, cot_sib, cot_cross, first, second, out, vol_wide, cot_wide):
+def inner_kernel(size, vol, sib, cot, cot_sib, first, second, part, back, vol_wide, cot_wide):
     core, _, _ = place(lax.axis_index("space"), size)
-    for wide, mine, near, far in ((vol_wide, own, sib, cross), (cot_wide, cot, cot_sib, cot_cross)):
+    for wide, mine, near in ((vol_wide, vol, sib), (cot_wide, cot, cot_sib)):
         edge_rows(wide)
         widen(wide, 1, mine[0])
         widen(wide, 2, mine[1])
-        widen(wide, 3 * core, far[1 - core])
         widen(wide, 3 * (1 - core), near[core])
-    hidden = convolve(vol_wide, first, 2)
-    sigma = jax.nn.sigmoid(hidden)
-    act_grad = convolve_back(cot_wide, second, 2)
-    out[0:2] = (hidden * sigma).astype(BF16).reshape(own.shape)
-    out[2:4] = (act_grad * sigma * (1.0 + hidden * (1.0 - sigma))).astype(BF16).reshape(own.shape)
-
-
-def response_kernel(size, act, act_sib, own, cross, first, second, out, vol_wide, act_wide):
+        wide[3 * core] = jnp.zeros(wide.shape[1:], BF16)
+    part[...] = convolve(vol_wide, first, 2).reshape(part.shape)
+    back[...] = convolve_back(cot_wide, second, 2).reshape(back.shape)
+
+
+def hidden_kernel(size, part, back, cross, first, second, out, wide):
+    core, _, _ = place(lax.axis_index("space"), size)
+    edge_rows(wide)
+    widen(wide, 0, cross[0])
+    widen(wide, 1, cross[1])
+    channels = cross.shape[-1]
+    grown, grown_back = part[core], back[core]
+    for column in range(3):
+        block = patch(wide, 0, 1, column)
+        kernel = first[2 * core, column]
+        grown = grown + jnp.dot(block, kernel.reshape(-1, channels), preferred_element_type=F32)
+        block = patch(wide, 1, 1, column)
+        for lane in range(3):
+            grown_back = grown_back + lax.dot_general(
+                block[:, lane * channels : (lane + 1) * channels],
+                second[2 - 2 * core, 2 - column, 2 - lane],
+                (((1,), (1,)), ((), ())),
+                preferred_element_type=F32,
+            )
+    for at, hidden, act_grad in ((core, grown, grown_back), (1 - core, part[1 - core], back[1 - core])):
+        sigma = jax.nn.sigmoid(hidden)
+        out[at] = (hidden * sigma).astype(BF16).reshape(out.shape[1:])
+        out[2 + at] = (act_grad * sigma * (1.0 + hidden * (1.0 - sigma))).astype(BF16).reshape(out.shape[1:])
+
+
+def response_kernel(size, both, both_sib, vol, cross, first, second, out, vol_wide, wide):
     index = lax.axis_index("space")
     core, _, _ = place(index, size)
     edge_rows(vol_wide)
-    widen(vol_wide, core, cross[0])
-    widen(vol_wide, core + 1, cross[1])
-    widen(vol_wide, 2 * (1 - core), own[core])
+    widen(vol_wide, 1, cross[0])
+    widen(vol_wide, 2 * core, cross[2])
+    widen(vol_wide, 2 * (1 - core), vol[core])
     hidden = convolve(vol_wide, first, 1)
     inside = jnp.where((index == 0) | (index == size - 1), 0.0, 1.0)
     outer = hidden * jax.nn.sigmoid(hidden) * inside
-    edge_rows(act_wide)
-    widen(act_wide, 1, act[0])
-    widen(act_wide, 2, act[1])
-    widen(act_wide, 3 * core, outer.reshape(own.shape[1:]).astype(BF16))
-    widen(act_wide, 3 * (1 - core), act_sib[core])
-    out[...] = convolve(act_wide, second, 2).astype(BF16).reshape(out.shape)
+    edge_rows(wide)
+    widen(wide, 1, both[0])
+    widen(wide, 2, both[1])
+    widen(wide, 3 * core, outer.reshape(out.shape[1:]).astype(BF16))
+    widen(wide, 3 * (1 - core), both_sib[core])
+    out[...] = convolve(wide, second, 2).astype(BF16).reshape(out.shape)
 
 
 def channel_choice(size, channels, index):
@@ -145,29 +167,33 @@
 
 
 def weight_kernel(size, shifted_left, *refs):
-    (own, sib, cross, cross_sib, four_own, four_sib, send, keep, wide, turned) = refs
+    (own, sib, cross, cross_sib, both, both_sib, send, keep, wide, turned) = refs
     index = lax.axis_index("space")
     core, _, _ = place(index, size)
     channels = own.shape[-1]
     voxels = own.shape[1] * own.shape[2]
     choice = channel_choice(size, channels, index)
     edge_rows(wide)
+    outer = 0 if shifted_left else 1
+    half_at = 2 if shifted_left else 0
+    four_own = [both[half_at + i] for i in range(2)]
+    four_sib = [both_sib[half_at + i] for i in range(2)]
     if shifted_left:
         for i in range(2):
             narrow(wide, 1 + i + 2 * core, own[i], choice)
             narrow(wide, 3 + i - 2 * core, sib[i], choice)
             turned[i + 2 * core] = four_own[i].reshape(voxels, channels).astype(F32).T.astype(BF16)
             turned[2 + i - 2 * core] = four_sib[i].reshape(voxels, channels).astype(F32).T.astype(BF16)
-        narrow(wide, 5 * core, cross[1 - core], choice)
-        narrow(wide, 5 * (1 - core), cross_sib[core], choice)
+        narrow(wide, 5 * core, cross[outer], choice)
+        narrow(wide, 5 * (1 - core), cross_sib[outer], choice)
     else:
         for i in range(2):
             narrow(wide, i + 2 * core, four_own[i], choice)
             narrow(wide, 2 + i - 2 * core, four_sib[i], choice)
             turned[1 + i + 2 * core] = own[i].reshape(voxels, channels).astype(F32).T.astype(BF16)
             turned[3 + i - 2 * core] = sib[i].reshape(voxels, channels).astype(F32).T.astype(BF16)
-        turned[5 * core] = cross[1 - core].reshape(voxels, channels).astype(F32).T.astype(BF16)
-        turned[5 * (1 - core)] = cross_sib[core].reshape(voxels, channels).astype(F32).T.astype(BF16)
+        turned[5 * core] = cross[outer].reshape(voxels, channels).astype(F32).T.astype(BF16)
+        turned[5 * (1 - core)] = cross_sib[outer].reshape(voxels, channels).astype(F32).T.astype(BF16)
     half = channels // 4
     for column in range(3):
         blocks = [None, None, None]
@@ -232,34 +258,50 @@
     def send(array, moves):
         return lax.ppermute(array, "space", moves)
 
-    vol_cross = send(volume, across)
-    vol_sib = send(volume, sibling)
-    cot_cross = send(cotangent, across)
-    cot_sib = send(cotangent, sibling)
-
     def wide(count, wide_channels):
         return pltpu.VMEM((count, width + 2, height, wide_channels), BF16)
 
+    slab_type = jax.ShapeDtypeStruct(volume.shape, BF16)
+    sums_type = jax.ShapeDtypeStruct((planes, width * height, channels), F32)
+    filter_type = jax.ShapeDtypeStruct(first_filter.shape, BF16)
+    weights = 2 * first_filter.size
+
+    core = lax.rem(lax.axis_index("space"), 2)
+    edge = jnp.stack(
+        [
+            lax.dynamic_index_in_dim(array, at, 0, False)
+            for array, at in ((volume, core), (cotangent, core), (volume, 1 - core))
+        ]
+    )
+    cross = send(edge, across)
+    vol_sib = send(volume, sibling)
+    cot_sib = send(cotangent, sibling)
+    part, back = call(
+        functools.partial(inner_kernel, size),
+        (sums_type, sums_type),
+        [wide(4, 3 * channels), wide(4, 3 * channels)],
+        2 * unit,
+        8 * slab + 2 * weights,
+        "inner",
+    )(volume, vol_sib, cotangent, cot_sib, first_filter, second_filter)
     both = call(
         functools.partial(hidden_kernel, size),
         jax.ShapeDtypeStruct((2 * planes, width, height, channels), BF16),
-        [wide(4, 3 * channels), wide(4, 3 * channels)],
-        2 * unit,
-        8 * slab + 4 * first_filter.size,
+        [wide(2, 3 * channels)],
+        unit // 3,
+        8 * slab + 2 * weights,
         "hidden",
-    )(volume, vol_sib, vol_cross, cotangent, cot_sib, cot_cross, first_filter, second_filter)
+    )(part, back, cross, first_filter, second_filter)
     both_sib = send(both, sibling)
-    vol_far = send(vol_cross, sibling)
-    cot_far = send(cot_cross, sibling)
-
+    cross_far = send(cross, sibling)
     response = call(
         functools.partial(response_kernel, size),
-        jax.ShapeDtypeStruct(volume.shape, BF16),
+        slab_type,
         [wide(3, 3 * channels), wide(4, 3 * channels)],
         3 * unit // 2,
-        6 * slab + 4 * first_filter.size,
+        6 * slab + 2 * weights,
         "response",
-    )(both[:planes], both_sib[:planes], volume, vol_cross, first_filter, second_filter)
+    )(both, both_sib, volume, cross, first_filter, second_filter)
 
     def filter_grad(shifted_left, operands, name):
         return call(
@@ -312,12 +354,11 @@
         return jnp.transpose(total.reshape(3, 3, 3, share, channels), (3, 0, 1, 2, 4))
 
     pair = pairs(lambda i: i ^ 2)
-    act, act_sib = both[:planes], both_sib[:planes]
-    grad, grad_sib = both[planes:], both_sib[planes:]
-    send_2, keep_2 = filter_grad(False, (cotangent, cot_sib, cot_cross, cot_far, act, act_sib), "second_grad")
+    send_2, keep_2 = filter_grad(False, (cotangent, cot_sib, cross, cross_far, both, both_sib), "second_grad")
     got_2 = send(send_2, pair)
-    send_1, keep_1 = filter_grad(True, (volume, vol_sib, vol_cross, vol_far, grad, grad_sib), "first_grad")
+    send_1, keep_1 = filter_grad(True, (volume, vol_sib, cross, cross_far, both, both_sib), "first_grad")
     got_1 = send(send_1, pair)
+    got_2, response = lax.optimization_barrier((got_2, response))
     blocks_2 = pair_sum(keep_2, got_2, "second_pair_sum")
     gots_2 = spread_out(blocks_2)
     blocks_1 = pair_sum(keep_1, got_1, "first_pair_sum")

time: 46.7 us -> 40.3 us (0.86)
  starting transfers between devices: 22.8 us -> 17.8 us
  local copies, waits for them, and re-layouts: 4.19 us -> 3.23 us
  waiting for transfers between devices: 9.8 us -> 8.96 us
    ppermute x15 -> x13, starting transfers between devices: 22.8 us -> 17.8 us  [send(): return lax.ppermute(array, 'space', moves)]
    pallas_call x1 -> x2, Pallas kernels: 2.56 us -> 4.63 us  [the longest x1 2.51 us: per_device(): call(functools.partial(response_kernel, size), slab_type, [wide(3, 3 * ch...]
    unnamed x14 -> x12, local copies, waits for them, and re-layouts: 4.16 us -> 2.38 us
    pallas_call x1, Pallas kernels: 2.23 us -> 0.51 us  [per_device(): call(functools.partial(hidden_kernel, size), jax.ShapeDtypeStruct((2 * pl...]
    dynamic_slice x0 -> x2, local copies, waits for them, and re-layouts: none -> 0.85 us  [per_device(): lax.dynamic_index_in_dim(array, at, 0, False)]
    ppermute x15 -> x13, waiting for transfers between devices: 9.8 us -> 8.96 us  [send(): return lax.ppermute(array, 'space', moves)]
  transfers between devices with their start and end apart: 15 -> 13, of which waited for: 7 -> 5; matrix products, arithmetic and copies ran while one was open for 0% -> 2% of each run, Pallas kernels for 13% -> 17%
where the time goes in v2:
time: 40.3 us; the launch traced here: 40.1 us
  starting transfers between devices  17.8 us (44%)
  Pallas kernels  9.31 us (23%)
  waiting for transfers between devices  8.96 us (22%)
  local copies, waits for them, and re-layouts  3.23 us (8%)
  between operations  0.75 us (2%)
    ppermute x13, starting transfers between devices, send(): return lax.ppermute(array, 'space', moves)  17.8 us
    ppermute x13, waiting for transfers between devices, send(): return lax.ppermute(array, 'space', moves)  8.96 us
    pallas_call x2, Pallas kernels, filter_grad(): call(functools.partial(weight_kernel, size, shifted_left), (jax.ShapeDtyp...  2.7 us
    pallas_call x1, Pallas kernels, per_device(): call(functools.partial(response_kernel, size), slab_type, [wide(3, 3 * ch...  2.51 us
    unnamed x12, local copies, waits for them, and re-layouts  2.38 us
    pallas_call x1, Pallas kernels, per_device(): call(functools.partial(inner_kernel, size), (sums_type, sums_type), [wide...  2.13 us
    pallas_call x2, Pallas kernels, last_sum(): call(last_sum_kernel, jax.ShapeDtypeStruct(own.shape, F32), [], own.size,...  1.35 us
    dynamic_slice x2, local copies, waits for them, and re-layouts, per_device(): lax.dynamic_index_in_dim(array, at, 0, False)  0.85 us
  transfers between devices with their start and end apart: 13, of which 5 were waited for; matrix products, arithmetic and copies ran while one was open for 2% of the time, Pallas kernels for 17%

profile of v2, /device:TPU:0, one launch (start us, length us, event | category | flops | bytes accessed | tf_op | source)
XLA Modules:
  0.0 40.1 jit_solution(4720723834230099126)
XLA Ops:
  0.6 0.5 %collective-permute-start = (bf16[2,16,16,128]{3,2,1,0:T(8,128)(2,1)}, bf16[2,16,16,128]{3,2,1,0:T(8,128)(2,1)S(1)}, u32[]{:S(2)}, u32[]{:S(2)}) collective-permute-start(bf16[2,16,16,128]{3,2,1,0:T(8,128)(2,1)} %refs_0_.2), channel_id=1, source_target_pairs={{0,1},{1,0},{2,3},{3,2},{4,5},{5,4},{6,7},{7,6},{8,9},{9,8},{10,11... | collective-permute-start | bytes 393224 | tf_op jit(solution)/shard_map/ppermute | solution.py:259
  1.2 0.1 collective-permute-start.3
  1.2 0.8 %constant_dynamic-slice_fusion.1 = bf16[1,16,16,128]{3,2,1,0:T(8,128)(2,1)S(1)} fusion(bf16[2,16,16,128]{3,2,1,0:T(8,128)(2,1)} %refs_0_.2, s32[]{:T(128)S(6)} %select_n.8), kind=kLoop, calls=%fused_computation.2 | loop fusion | bytes 131076 | tf_op jit(solution)/shard_map/jit(dynamic_index_in_dim)/dynamic_slice | solution.py:272
  2.1 0.0 copy-start.5
  2.1 0.8 %collective-permute-start.1 = (bf16[3,16,16,128]{3,2,1,0:T(8,128)(2,1)S(1)}, bf16[3,16,16,128]{3,2,1,0:T(8,128)(2,1)S(1)}, u32[]{:S(2)}, u32[]{:S(2)}) collective-permute-start(bf16[3,16,16,128]{3,2,1,0:T(8,128)(2,1)S(1)} %pad_maximum_fusion), channel_id=1, source_target_pairs={{1,2},{3,4},{5,6},{7,8},{9,10},{11,12},{13,14},{2,1},{4,3},{6,5},{... | collective-permute-start | bytes 589832 | tf_op jit(solution)/shard_map/ppermute | solution.py:259
  3.0 0.0 collective-permute-done.cot_sib.refs_1_
  3.0 0.0 copy-done.5
  3.0 1.2 %copy-done = bf16[3,3,3,128,128]{4,3,2,1,0:T(8,128)(2,1)S(1)} copy-done((bf16[3,3,3,128,128]{4,3,2,1,0:T(8,128)(2,1)S(1)}, bf16[3,3,3,128,128]{4,3,2,1,0:T(8,128)(2,1)}, u32[]{:S(2)}) %copy-start) | copy-done | bytes 884760
  4.2 1.2 %copy-done.2 = bf16[3,3,3,128,128]{4,3,2,1,0:T(8,128)(2,1)S(1)} copy-done((bf16[3,3,3,128,128]{4,3,2,1,0:T(8,128)(2,1)S(1)}, bf16[3,3,3,128,128]{4,3,2,1,0:T(8,128)(2,1)}, u32[]{:S(2)}) %copy-start.2) | copy-done | bytes 884760
  5.3 2.1 %inner.1 = (f32[2,256,128]{2,1,0:T(8,128)S(1)}, f32[2,256,128]{2,1,0:T(8,128)S(1)}) custom-call(bf16[2,16,16,128]{3,2,1,0:T(8,128)(2,1)S(1)} %copy-done.4, bf16[2,16,16,128]{3,2,1,0:T(8,128)(2,1)S(1)} %collective-permute-done.3.sib.refs_1_, bf16[2,16,16,128]{3,2,1,0:T(8,128)(2,1)S(1)} %copy-done.5, ...), custom_call_target="tpu_custom_call" | custom-call | flops 905969664 | bytes 2818048 | tf_op jit(solution)/shard_map/inner/pallas_call | solution.py:279
  7.5 0.5 %hidden.1.refs_4_.both = bf16[4,16,16,128]{3,2,1,0:T(8,128)(2,1)S(1)} custom-call(f32[2,256,128]{2,1,0:T(8,128)S(1)} %get-tuple-element.19.part, f32[2,256,128]{2,1,0:T(8,128)S(1)} %get-tuple-element.20.back, bf16[3,16,16,128]{3,2,1,0:T(8,128)(2,1)S(1)} %collective-permute-done.1.cross.refs_2_, bf16[3,3,3,128,128]{4,3,2,1,0:T(8,128)(2,1)S(1)} %copy-done.1, ...), custom_call_target="tpu_custom_call" | custom-call | flops 150994944 | bytes 2818048 | tf_op jit(solution)/shard_map/hidden/pallas_call | solution.py:287
  8.0 4.5 %collective-permute-start.4 = (bf16[4,16,16,128]{3,2,1,0:T(8,128)(2,1)S(1)}, bf16[4,16,16,128]{3,2,1,0:T(8,128)(2,1)S(1)}, u32[]{:S(2)}, u32[]{:S(2)}) collective-permute-start(bf16[4,16,16,128]{3,2,1,0:T(8,128)(2,1)S(1)} %hidden.1.refs_4_.both), channel_id=1, source_target_pairs={{0,1},{1,0},{2,3},{3,2},{4,5},{5,4},{6,7},{7,6},{8,9},{9,8},{10,11... | collective-permute-start | bytes 786440 | tf_op jit(solution)/shard_map/ppermute | solution.py:259
  12.5 0.1 collective-permute-start.2
  12.6 1.4 %collective-permute-done.2.refs_3_ = bf16[3,16,16,128]{3,2,1,0:T(8,128)(2,1)S(1)} collective-permute-done((bf16[3,16,16,128]{3,2,1,0:T(8,128)(2,1)S(1)}, bf16[3,16,16,128]{3,2,1,0:T(8,128)(2,1)S(1)}, u32[]{:S(2)}, u32[]{:S(2)}) %collective-permute-start.2) | collective-permute-done | bytes 196640 | tf_op jit(solution)/shard_map/ppermute | solution.py:259
  14.0 1.4 %second_grad.1 = (bf16[27,32,128]{2,1,0:T(8,128)(2,1)S(1)}, f32[27,32,128]{2,1,0:T(8,128)S(1)}) custom-call(bf16[2,16,16,128]{3,2,1,0:T(8,128)(2,1)S(1)} %copy-done.5, bf16[2,16,16,128]{3,2,1,0:T(8,128)(2,1)S(1)} %collective-permute-done.cot_sib.refs_1_, bf16[3,16,16,128]{3,2,1,0:T(8,128)(2,1)S(1)} %collective-permute-done.1.cross.refs_2_, ...), custom_call_target="tpu_custom_call" | custom-call | flops 452984832 | bytes 786432 | tf_op jit(solution)/shard_map/second_grad/pallas_call | solution.py:307
  15.4 2.8 %collective-permute-start.5 = (bf16[27,32,128]{2,1,0:T(8,128)(2,1)S(1)}, bf16[27,32,128]{2,1,0:T(8,128)(2,1)S(1)}, u32[]{:S(2)}, u32[]{:S(2)}) collective-permute-start(bf16[27,32,128]{2,1,0:T(8,128)(2,1)S(1)} %get-tuple-element.21), channel_id=1, source_target_pairs={{0,2},{1,3},{2,0},{3,1},{4,6},{5,7},{6,4},{7,5},{8,10},{9,11},{10,... | collective-permute-start | bytes 663560 | tf_op jit(solution)/shard_map/ppermute | solution.py:259
  18.2 1.3 %first_grad.1 = (bf16[27,32,128]{2,1,0:T(8,128)(2,1)S(1)}, f32[27,32,128]{2,1,0:T(8,128)S(1)}) custom-call(bf16[2,16,16,128]{3,2,1,0:T(8,128)(2,1)S(1)} %copy-done.4, bf16[2,16,16,128]{3,2,1,0:T(8,128)(2,1)S(1)} %collective-permute-done.3.sib.refs_1_, bf16[3,16,16,128]{3,2,1,0:T(8,128)(2,1)S(1)} %collective-permute-done.1.cross.refs_2_, ...), custom_call_target="tpu_custom_call" | custom-call | flops 452984832 | bytes 786432 | tf_op jit(solution)/shard_map/first_grad/pallas_call | solution.py:307
  19.5 0.1 collective-permute-start.6
  19.6 2.5 %response.1 = bf16[2,16,16,128]{3,2,1,0:T(8,128)(2,1)} custom-call(bf16[4,16,16,128]{3,2,1,0:T(8,128)(2,1)S(1)} %hidden.1.refs_4_.both, bf16[4,16,16,128]{3,2,1,0:T(8,128)(2,1)S(1)} %collective-permute-done.4.refs_5_.both_sib, bf16[2,16,16,128]{3,2,1,0:T(8,128)(2,1)S(1)} %copy-done.4, bf16[3,16,16,128]{3,2,1,0:T(8,128)(2,1)S(1)} %collective-permute-done.1.cross.refs_2_, ...), custom_call_target="tpu_custom_call" | custom-call | flops 679477248 | bytes 2555904 | tf_op jit(solution)/shard_map/response/pallas_call | solution.py:297
  22.1 2.3 %collective-permute-done.5.got = bf16[27,32,128]{2,1,0:T(8,128)(2,1)S(1)} collective-permute-done((bf16[27,32,128]{2,1,0:T(8,128)(2,1)S(1)}, bf16[27,32,128]{2,1,0:T(8,128)(2,1)S(1)}, u32[]{:S(2)}, u32[]{:S(2)}) %collective-permute-start.5) | collective-permute-done | bytes 221216 | tf_op jit(solution)/shard_map/ppermute | solution.py:259
  24.4 0.1 second_pair_sum.1
  24.4 1.9 %collective-permute-start.10 = (bf16[224,128]{1,0:T(8,128)(2,1)S(1)}, bf16[224,128]{1,0:T(8,128)(2,1)S(1)}, u32[]{:S(2)}, u32[]{:S(2)}) collective-permute-start(bf16[224,128]{1,0:T(8,128)(2,1)S(1)} %get-tuple-element.32), channel_id=1, source_target_pairs={{0,4},{1,5},{2,6},{3,7},{4,0},{5,1},{6,2},{7,3},{8,12},{9,13},{10,... | collective-permute-start | bytes 172040 | tf_op jit(solution)/shard_map/ppermute | solution.py:259
  26.3 2.6 %collective-permute-start.11 = (bf16[224,128]{1,0:T(8,128)(2,1)S(1)}, bf16[224,128]{1,0:T(8,128)(2,1)S(1)}, u32[]{:S(2)}, u32[]{:S(2)}) collective-permute-start(bf16[224,128]{1,0:T(8,128)(2,1)S(1)} %get-tuple-element.33), channel_id=1, source_target_pairs={{0,8},{1,9},{2,10},{3,11},{4,12},{5,13},{6,14},{7,15},{8,0},{9,1},... | collective-permute-start | bytes 172040 | tf_op jit(solution)/shard_map/ppermute | solution.py:259
  28.9 0.1 first_pair_sum.1
  29.0 1.5 %collective-permute-start.7 = (bf16[224,128]{1,0:T(8,128)(2,1)S(1)}, bf16[224,128]{1,0:T(8,128)(2,1)S(1)}, u32[]{:S(2)}, u32[]{:S(2)}) collective-permute-start(bf16[224,128]{1,0:T(8,128)(2,1)S(1)} %get-tuple-element.26), channel_id=1, source_target_pairs={{0,4},{1,5},{2,6},{3,7},{4,0},{5,1},{6,2},{7,3},{8,12},{9,13},{10,... | collective-permute-start | bytes 172040 | tf_op jit(solution)/shard_map/ppermute | solution.py:259
  30.5 2.9 %collective-permute-start.8 = (bf16[224,128]{1,0:T(8,128)(2,1)S(1)}, bf16[224,128]{1,0:T(8,128)(2,1)S(1)}, u32[]{:S(2)}, u32[]{:S(2)}) collective-permute-start(bf16[224,128]{1,0:T(8,128)(2,1)S(1)} %get-tuple-element.27), channel_id=1, source_target_pairs={{0,8},{1,9},{2,10},{3,11},{4,12},{5,13},{6,14},{7,15},{8,0},{9,1},... | collective-permute-start | bytes 172040 | tf_op jit(solution)/shard_map/ppermute | solution.py:259
  33.4 0.0 collective-permute-start.9
  33.4 1.6 %collective-permute-done.12.refs_3_ = bf16[224,128]{1,0:T(8,128)(2,1)S(1)} collective-permute-done((bf16[224,128]{1,0:T(8,128)(2,1)S(1)}, bf16[224,128]{1,0:T(8,128)(2,1)S(1)}, u32[]{:S(2)}, u32[]{:S(2)}) %collective-permute-start.12) | collective-permute-done | bytes 57376 | tf_op jit(solution)/shard_map/ppermute | solution.py:259
  35.1 0.7 %second_last_sum.1 = f32[216,128]{1,0:T(8,128)} custom-call(f32[216,128]{1,0:T(8,128)S(1)} %get-tuple-element.31.refs_0_, bf16[224,128]{1,0:T(8,128)(2,1)S(1)} %collective-permute-done.10.refs_1_, bf16[224,128]{1,0:T(8,128)(2,1)S(1)} %collective-permute-done.11.refs_2_, bf16[224,128]{1,0:T(8,128)(2,1)S(1)} %collective-permute-done.12.refs_3_), custom_call_target="tpu_custom_call" | custom-call | flops 27648 | bytes 442368 | tf_op jit(solution)/shard_map/second_last_sum/pallas_call | solution.py:351
  35.8 1.8 %collective-permute-done.8.refs_2_ = bf16[224,128]{1,0:T(8,128)(2,1)S(1)} collective-permute-done((bf16[224,128]{1,0:T(8,128)(2,1)S(1)}, bf16[224,128]{1,0:T(8,128)(2,1)S(1)}, u32[]{:S(2)}, u32[]{:S(2)}) %collective-permute-start.8) | collective-permute-done | bytes 57376 | tf_op jit(solution)/shard_map/ppermute | solution.py:259
  37.6 1.8 %collective-permute-done.9.refs_3_ = bf16[224,128]{1,0:T(8,128)(2,1)S(1)} collective-permute-done((bf16[224,128]{1,0:T(8,128)(2,1)S(1)}, bf16[224,128]{1,0:T(8,128)(2,1)S(1)}, u32[]{:S(2)}, u32[]{:S(2)}) %collective-permute-start.9) | collective-permute-done | bytes 57376 | tf_op jit(solution)/shard_map/ppermute | solution.py:259
  39.4 0.7 %first_last_sum.1 = f32[216,128]{1,0:T(8,128)} custom-call(f32[216,128]{1,0:T(8,128)S(1)} %get-tuple-element.25.refs_0_, bf16[224,128]{1,0:T(8,128)(2,1)S(1)} %collective-permute-done.7.refs_1_, bf16[224,128]{1,0:T(8,128)(2,1)S(1)} %collective-permute-done.8.refs_2_, bf16[224,128]{1,0:T(8,128)(2,1)S(1)} %collective-permute-done.9.refs_3_), custom_call_target="tpu_custom_call" | custom-call | flops 27648 | bytes 442368 | tf_op jit(solution)/shard_map/first_last_sum/pallas_call | solution.py:351
  (18 shorter events, 0.1 us)
Async XLA Ops:
  0.6 1.5 %copy-start.4 = (bf16[2,16,16,128]{3,2,1,0:T(8,128)(2,1)S(1)}, bf16[2,16,16,128]{3,2,1,0:T(8,128)(2,1)}, u32[]{:S(2)}) copy-start(bf16[2,16,16,128]{3,2,1,0:T(8,128)(2,1)} %refs_0_.3) | copy-start | bytes 393220
  0.6 2.3 %collective-permute-start = (bf16[2,16,16,128]{3,2,1,0:T(8,128)(2,1)}, bf16[2,16,16,128]{3,2,1,0:T(8,128)(2,1)S(1)}, u32[]{:S(2)}, u32[]{:S(2)}) collective-permute-start(bf16[2,16,16,128]{3,2,1,0:T(8,128)(2,1)} %refs_0_.2), channel_id=1, source_target_pairs={{0,1},{1,0},{2,3},{3,2},{4,5},{5,4},{6,7},{7,6},{8,9},{9,8},{10,11... | collective-permute-start | bytes 393224 | tf_op jit(solution)/shard_map/ppermute | solution.py:259
  1.2 1.8 %collective-permute-start.3 = (bf16[2,16,16,128]{3,2,1,0:T(8,128)(2,1)}, bf16[2,16,16,128]{3,2,1,0:T(8,128)(2,1)S(1)}, u32[]{:S(2)}, u32[]{:S(2)}) collective-permute-start(bf16[2,16,16,128]{3,2,1,0:T(8,128)(2,1)} %refs_0_.3), channel_id=1, source_target_pairs={{0,1},{1,0},{2,3},{3,2},{4,5},{5,4},{6,7},{7,6},{8,9},{9,8},{10,11... | collective-permute-start | bytes 393224 | tf_op jit(solution)/shard_map/ppermute | solution.py:259
  2.1 0.9 %copy-start.5 = (bf16[2,16,16,128]{3,2,1,0:T(8,128)(2,1)S(1)}, bf16[2,16,16,128]{3,2,1,0:T(8,128)(2,1)}, u32[]{:S(2)}) copy-start(bf16[2,16,16,128]{3,2,1,0:T(8,128)(2,1)} %refs_0_.2) | copy-start | bytes 393220
  2.1 5.3 %collective-permute-start.1 = (bf16[3,16,16,128]{3,2,1,0:T(8,128)(2,1)S(1)}, bf16[3,16,16,128]{3,2,1,0:T(8,128)(2,1)S(1)}, u32[]{:S(2)}, u32[]{:S(2)}) collective-permute-start(bf16[3,16,16,128]{3,2,1,0:T(8,128)(2,1)S(1)} %pad_maximum_fusion), channel_id=1, source_target_pairs={{1,2},{3,4},{5,6},{7,8},{9,10},{11,12},{13,14},{2,1},{4,3},{6,5},{... | collective-permute-start | bytes 589832 | tf_op jit(solution)/shard_map/ppermute | solution.py:259
  3.0 1.2 %copy-start = (bf16[3,3,3,128,128]{4,3,2,1,0:T(8,128)(2,1)S(1)}, bf16[3,3,3,128,128]{4,3,2,1,0:T(8,128)(2,1)}, u32[]{:S(2)}) copy-start(bf16[3,3,3,128,128]{4,3,2,1,0:T(8,128)(2,1)} %first.5) | copy-start | bytes 2654212
  4.2 1.2 %copy-start.2 = (bf16[3,3,3,128,128]{4,3,2,1,0:T(8,128)(2,1)S(1)}, bf16[3,3,3,128,128]{4,3,2,1,0:T(8,128)(2,1)}, u32[]{:S(2)}) copy-start(bf16[3,3,3,128,128]{4,3,2,1,0:T(8,128)(2,1)} %second.5) | copy-start | bytes 2654212
  5.3 2.1 %copy-start.1 = (bf16[3,3,3,128,128]{4,3,2,1,0:T(8,128)(2,1)S(1)}, bf16[3,3,3,128,128]{4,3,2,1,0:T(8,128)(2,1)}, u32[]{:S(2)}) copy-start(bf16[3,3,3,128,128]{4,3,2,1,0:T(8,128)(2,1)} %first.5) | copy-start | bytes 2654212
  5.3 2.2 %copy-start.3 = (bf16[3,3,3,128,128]{4,3,2,1,0:T(8,128)(2,1)S(1)}, bf16[3,3,3,128,128]{4,3,2,1,0:T(8,128)(2,1)}, u32[]{:S(2)}) copy-start(bf16[3,3,3,128,128]{4,3,2,1,0:T(8,128)(2,1)} %second.5) | copy-start | bytes 2654212
  8.0 6.0 %collective-permute-start.4 = (bf16[4,16,16,128]{3,2,1,0:T(8,128)(2,1)S(1)}, bf16[4,16,16,128]{3,2,1,0:T(8,128)(2,1)S(1)}, u32[]{:S(2)}, u32[]{:S(2)}) collective-permute-start(bf16[4,16,16,128]{3,2,1,0:T(8,128)(2,1)S(1)} %hidden.1.refs_4_.both), channel_id=1, source_target_pairs={{0,1},{1,0},{2,3},{3,2},{4,5},{5,4},{6,7},{7,6},{8,9},{9,8},{10,11... | collective-permute-start | bytes 786440 | tf_op jit(solution)/shard_map/ppermute | solution.py:259
  12.5 1.4 %collective-permute-start.2 = (bf16[3,16,16,128]{3,2,1,0:T(8,128)(2,1)S(1)}, bf16[3,16,16,128]{3,2,1,0:T(8,128)(2,1)S(1)}, u32[]{:S(2)}, u32[]{:S(2)}) collective-permute-start(bf16[3,16,16,128]{3,2,1,0:T(8,128)(2,1)S(1)} %collective-permute-done.1.cross.refs_2_), channel_id=1, source_target_pairs={{0,1},{1,0},{2,3},{3,2},{4,5},{5,4},{6,7},{7,6},{8,9},{9,8},{10,11... | collective-permute-start | bytes 589832 | tf_op jit(solution)/shard_map/ppermute | solution.py:259
  15.4 9.0 %collective-permute-start.5 = (bf16[27,32,128]{2,1,0:T(8,128)(2,1)S(1)}, bf16[27,32,128]{2,1,0:T(8,128)(2,1)S(1)}, u32[]{:S(2)}, u32[]{:S(2)}) collective-permute-start(bf16[27,32,128]{2,1,0:T(8,128)(2,1)S(1)} %get-tuple-element.21), channel_id=1, source_target_pairs={{0,2},{1,3},{2,0},{3,1},{4,6},{5,7},{6,4},{7,5},{8,10},{9,11},{10,... | collective-permute-start | bytes 663560 | tf_op jit(solution)/shard_map/ppermute | solution.py:259
  19.5 9.4 %collective-permute-start.6 = (bf16[27,32,128]{2,1,0:T(8,128)(2,1)S(1)}, bf16[27,32,128]{2,1,0:T(8,128)(2,1)S(1)}, u32[]{:S(2)}, u32[]{:S(2)}) collective-permute-start(bf16[27,32,128]{2,1,0:T(8,128)(2,1)S(1)} %get-tuple-element.24), channel_id=1, source_target_pairs={{0,2},{1,3},{2,0},{3,1},{4,6},{5,7},{6,4},{7,5},{8,10},{9,11},{10,... | collective-permute-start | bytes 663560 | tf_op jit(solution)/shard_map/ppermute | solution.py:259
  24.4 9.0 %collective-permute-start.10 = (bf16[224,128]{1,0:T(8,128)(2,1)S(1)}, bf16[224,128]{1,0:T(8,128)(2,1)S(1)}, u32[]{:S(2)}, u32[]{:S(2)}) collective-permute-start(bf16[224,128]{1,0:T(8,128)(2,1)S(1)} %get-tuple-element.32), channel_id=1, source_target_pairs={{0,4},{1,5},{2,6},{3,7},{4,0},{5,1},{6,2},{7,3},{8,12},{9,13},{10,... | collective-permute-start | bytes 172040 | tf_op jit(solution)/shard_map/ppermute | solution.py:259
  26.3 7.1 %collective-permute-start.11 = (bf16[224,128]{1,0:T(8,128)(2,1)S(1)}, bf16[224,128]{1,0:T(8,128)(2,1)S(1)}, u32[]{:S(2)}, u32[]{:S(2)}) collective-permute-start(bf16[224,128]{1,0:T(8,128)(2,1)S(1)} %get-tuple-element.33), channel_id=1, source_target_pairs={{0,8},{1,9},{2,10},{3,11},{4,12},{5,13},{6,14},{7,15},{8,0},{9,1},... | collective-permute-start | bytes 172040 | tf_op jit(solution)/shard_map/ppermute | solution.py:259
  28.9 6.2 %collective-permute-start.12 = (bf16[224,128]{1,0:T(8,128)(2,1)S(1)}, bf16[224,128]{1,0:T(8,128)(2,1)S(1)}, u32[]{:S(2)}, u32[]{:S(2)}) collective-permute-start(bf16[224,128]{1,0:T(8,128)(2,1)S(1)} %get-tuple-element.34), channel_id=1, source_target_pairs={{0,12},{1,13},{2,14},{3,15},{4,8},{5,9},{6,10},{7,11},{8,4},{9,5},... | collective-permute-start | bytes 172040 | tf_op jit(solution)/shard_map/ppermute | solution.py:259
  29.0 6.8 %collective-permute-start.7 = (bf16[224,128]{1,0:T(8,128)(2,1)S(1)}, bf16[224,128]{1,0:T(8,128)(2,1)S(1)}, u32[]{:S(2)}, u32[]{:S(2)}) collective-permute-start(bf16[224,128]{1,0:T(8,128)(2,1)S(1)} %get-tuple-element.26), channel_id=1, source_target_pairs={{0,4},{1,5},{2,6},{3,7},{4,0},{5,1},{6,2},{7,3},{8,12},{9,13},{10,... | collective-permute-start | bytes 172040 | tf_op jit(solution)/shard_map/ppermute | solution.py:259
  30.5 7.1 %collective-permute-start.8 = (bf16[224,128]{1,0:T(8,128)(2,1)S(1)}, bf16[224,128]{1,0:T(8,128)(2,1)S(1)}, u32[]{:S(2)}, u32[]{:S(2)}) collective-permute-start(bf16[224,128]{1,0:T(8,128)(2,1)S(1)} %get-tuple-element.27), channel_id=1, source_target_pairs={{0,8},{1,9},{2,10},{3,11},{4,12},{5,13},{6,14},{7,15},{8,0},{9,1},... | collective-permute-start | bytes 172040 | tf_op jit(solution)/shard_map/ppermute | solution.py:259
  33.4 6.0 %collective-permute-start.9 = (bf16[224,128]{1,0:T(8,128)(2,1)S(1)}, bf16[224,128]{1,0:T(8,128)(2,1)S(1)}, u32[]{:S(2)}, u32[]{:S(2)}) collective-permute-start(bf16[224,128]{1,0:T(8,128)(2,1)S(1)} %get-tuple-element.28), channel_id=1, source_target_pairs={{0,12},{1,13},{2,14},{3,15},{4,8},{5,9},{6,10},{7,11},{8,4},{9,5},... | collective-permute-start | bytes 172040 | tf_op jit(solution)/shard_map/ppermute | solution.py:259

commit v3 on v1

v3 whole, which is shorter than its diff:
```python
import functools

import jax
import jax.numpy as jnp
from jax import lax
from jax.experimental import pallas as pl
from jax.experimental.pallas import tpu as pltpu
from jax.sharding import PartitionSpec as P

F32 = jnp.float32
BF16 = jnp.bfloat16
VMEM_BYTES = 40 * 2**20


def call(body, out_shape, scratch, name):
    return pl.pallas_call(
        body,
        out_shape=out_shape,
        scratch_shapes=scratch,
        name=name,
        compiler_params=pltpu.CompilerParams(vmem_limit_bytes=VMEM_BYTES),
        cost_estimate=pl.CostEstimate(flops=0, bytes_accessed=0, transcendentals=0),
    )


def core_of(size):
    index = lax.axis_index("space")
    return index, lax.rem(index, 2)


def within(index, size):
    return jnp.where((index == 0) | (index == size - 1), 0.0, 1.0)


def edge_rows(wide):
    planes, rows, lanes, channels = wide.shape
    zero = jnp.zeros((planes, 1, lanes, channels), wide.dtype)
    wide[:, 0:1] = zero
    wide[:, rows - 1 : rows] = zero


def moved_lanes(plane):
    length = plane.shape[1]
    at = lax.broadcasted_iota(jnp.int32, plane.shape, 1)
    before = jnp.where(at == 0, 0.0, pltpu.roll(plane, 1, 1))
    after = jnp.where(at == length - 1, 0.0, pltpu.roll(plane, length - 1, 1))
    return before, after


def widen(wide, at, plane):
    rows, _, channels = plane.shape
    before, after = moved_lanes(plane.astype(F32))
    wide[at, 1 : rows + 1, :, 0:channels] = before.astype(BF16)
    wide[at, 1 : rows + 1, :, channels : 2 * channels] = plane.astype(BF16)
    wide[at, 1 : rows + 1, :, 2 * channels : 3 * channels] = after.astype(BF16)


def patch(wide, plane, planes, column):
    rows, lanes, channels = wide.shape[1] - 2, wide.shape[2], wide.shape[3]
    return wide[plane : plane + planes, column : column + rows].reshape(planes * rows * lanes, channels)


def convolve(wide, weight, planes):
    total = None
    for plane in range(3):
        for column in range(3):
            kernel = weight[plane, column]
            term = jnp.dot(
                patch(wide, plane, planes, column),
                kernel.reshape(-1, kernel.shape[-1]),
                preferred_element_type=F32,
            )
            total = term if total is None else total + term
    return total


def convolve_back(wide, weight, planes):
    channels = weight.shape[4]
    total = None
    for plane in range(3):
        for column in range(3):
            block = patch(wide, plane, planes, column)
            for lane in range(3):
                term = lax.dot_general(
                    block[:, lane * channels : (lane + 1) * channels],
                    weight[2 - plane, 2 - column, 2 - lane],
                    (((1,), (1,)), ((), ())),
                    preferred_element_type=F32,
                )
                total = term if total is None else total + term
    return total


def inner_kernel(size, vol, sib, first, part, wide):
    _, core = core_of(size)
    edge_rows(wide)
    widen(wide, 1, vol[0])
    widen(wide, 2, vol[1])
    widen(wide, 3 * (1 - core), sib[core])
    wide[3 * core] = jnp.zeros(wide.shape[1:], BF16)
    part[...] = convolve(wide, first, 2).reshape(part.shape)


def hidden_kernel(size, part, cross, first, hidden, act, wide):
    index, core = core_of(size)
    edge_rows(wide)
    widen(wide, 0, cross[0].astype(F32) * within(index, size))
    grown = part[core]
    for column in range(3):
        kernel = first[2 * core, column]
        grown = grown + jnp.dot(
            patch(wide, 0, 1, column), kernel.reshape(-1, kernel.shape[-1]), preferred_element_type=F32
        )
    for at, held in ((core, grown), (1 - core, part[1 - core])):
        hidden[at] = held
        act[at] = (held * jax.nn.sigmoid(held)).astype(BF16).reshape(act.shape[1:])


def hidden_grad_kernel(size, hidden, cot, sib, cross, second, out, wide):
    index, core = core_of(size)
    edge_rows(wide)
    widen(wide, 1, cot[0])
    widen(wide, 2, cot[1])
    widen(wide, 3 * (1 - core), sib[core])
    widen(wide, 3 * core, cross[1].astype(F32) * within(index, size))
    act_grad = convolve_back(wide, second, 2)
    held = hidden[...].reshape(act_grad.shape)
    sigma = jax.nn.sigmoid(held)
    out[...] = (act_grad * sigma * (1.0 + held * (1.0 - sigma))).astype(BF16).reshape(out.shape)


def response_kernel(size, act, sib, vol, cross, first, second, out, vol_wide, wide):
    index, core = core_of(size)
    edge_rows(vol_wide)
    widen(vol_wide, 1, cross[0])
    widen(vol_wide, 2 * core, cross[2])
    widen(vol_wide, 2 * (1 - core), vol[core])
    hidden = convolve(vol_wide, first, 1)
    outer = hidden * jax.nn.sigmoid(hidden) * within(index, size)
    edge_rows(wide)
    widen(wide, 1, act[0])
    widen(wide, 2, act[1])
    widen(wide, 3 * core, outer.reshape(out.shape[1:]).astype(BF16))
    widen(wide, 3 * (1 - core), sib[core])
    out[...] = convolve(wide, second, 2).astype(BF16).reshape(out.shape)


def channel_choice(size, channels, index):
    share = channels // size
    lane = lax.broadcasted_iota(jnp.int32, (channels, channels), 1) % (channels // 2)
    row = lax.broadcasted_iota(jnp.int32, (channels, channels), 0)
    eighth = channels // 8
    move = lane // eighth * 2 + lane % eighth // share * 8
    owner = jnp.bitwise_xor(move, index)
    return jnp.where(row == owner * share + lane % share, 1.0, 0.0).astype(BF16)


def narrow(wide, at, plane, choice):
    rows, lanes, channels = plane.shape
    kept = jnp.dot(plane.astype(BF16).reshape(rows * lanes, channels), choice, preferred_element_type=F32)
    kept = kept.reshape(rows, lanes, channels)
    before, after = moved_lanes(kept)
    lane = lax.broadcasted_iota(jnp.int32, kept.shape, 2)
    wide[at, 1 : rows + 1, :, 0:channels] = jnp.where(lane < channels // 2, before, kept).astype(BF16)
    wide[at, 1 : rows + 1, :, channels : 2 * channels] = after.astype(BF16)


def turn(plane):
    return plane.reshape(-1, plane.shape[-1]).astype(F32).T.astype(BF16)


def weight_kernel(size, which, own, sib, cross, cross_sib, four, four_sib, keep, *refs):
    sends, wide, turned = refs[:-2], refs[-2], refs[-1]
    index, core = core_of(size)
    channels = own.shape[-1]
    choice = channel_choice(size, channels, index)
    edge_rows(wide)

    def six(at, plane):
        if which:
            turned[at] = turn(plane)
        else:
            narrow(wide, at, plane, choice)

    for i in range(2):
        six(1 + i + 2 * core, own[i])
        six(3 + i - 2 * core, sib[i])
        for at, plane in ((i + 2 * core, four[i]), (2 + i - 2 * core, four_sib[i])):
            if which:
                narrow(wide, at, plane, choice)
            else:
                turned[at] = turn(plane)
    six(5 * core, cross[which].astype(F32) * within(index, size))
    six(5 * (1 - core), cross_sib[which].astype(F32) * within(jnp.bitwise_xor(index, 1), size))
    half = channels // 2
    block = half // 4
    for column in range(3):
        sums = [None, None, None]
        for at in range(wide.shape[0]):
            pairs = [(a, at - a + 2 * which) for a in range(3)]
            pairs = [(a, p) for a, p in pairs if 0 <= p < turned.shape[0]]
            left = jnp.concatenate([turned[p] for _, p in pairs], axis=0)
            term = jnp.dot(left, patch(wide, at, 1, column), preferred_element_type=F32)
            for i, (a, _) in enumerate(pairs):
                piece = term[i * channels : (i + 1) * channels]
                sums[a] = piece if sums[a] is None else sums[a] + piece
        for a in range(3):
            first = sums[a][:, :channels].T
            second = sums[a][:, channels:].T
            tap = (a * 3 + column) * 3
            for lane, rows in enumerate((first[:half], first[half:], second[:half])):
                keep[tap + lane] = rows[:block]
                for d, target in enumerate(sends, 1):
                    target[tap + lane] = rows[d * block : (d + 1) * block].astype(BF16)


def near_sum_kernel(share, keep, got_a, got_b, got_c, own, *sends):
    total = keep[...]
    for got in (got_a, got_b, got_c):
        total = total + got[...].astype(F32)
    taps, _, channels = total.shape
    for q in range(len(sends) + 1):
        block = total[:, q * share : (q + 1) * share].reshape(taps * share, channels)
        if q == 0:
            own[...] = block
        else:
            rows = sends[q - 1].shape[0]
            pad = jnp.zeros((rows - taps * share, channels), F32)
            sends[q - 1][...] = jnp.concatenate([block, pad], axis=0).astype(BF16)


def last_sum_kernel(*refs):
    own, gots, out = refs[0], refs[1:-1], refs[-1]
    rows = own.shape[0]
    total = own[...]
    for got in gots:
        total = total + got[...].astype(F32)[:rows]
    out[...] = total


def per_device(parts, size, volume, first_filter, second_filter, cotangent):
    channels = volume.shape[3]
    share = channels // size
    far = size // 8
    planes, width, height, _ = volume.shape

    def pairs(move):
        return [(i, move(i)) for i in range(size)]

    links = [(part * size + i, part * size + i + 1) for part in range(parts) for i in range(1, size - 1, 2)]
    links = links + [
        (part * size + i, (part + 1) * size + i) for part in range(0, parts, 2) for i in (0, size - 1)
    ]
    across = links + [(j, i) for i, j in links]
    sibling = pairs(lambda i: i ^ 1)

    def send(array, moves):
        return lax.ppermute(array, "space", moves)

    def send_across(array):
        return lax.ppermute(array, ("parts", "space"), across)

    def wide(count, wide_channels):
        return pltpu.VMEM((count, width + 2, height, wide_channels), BF16)

    slab_type = jax.ShapeDtypeStruct(volume.shape, BF16)
    sums_type = jax.ShapeDtypeStruct((planes, width * height, channels), F32)
    filter_type = jax.ShapeDtypeStruct(first_filter.shape, BF16)

    def hop(move):
        return pairs(lambda i: i ^ move)

    core = lax.rem(lax.axis_index("space"), 2)
    edge = jnp.where(
        core == 0,
        jnp.stack([volume[0], cotangent[0], volume[1]]),
        jnp.stack([volume[1], cotangent[1], volume[0]]),
    )
    edge, late_volume, late_cotangent = lax.optimization_barrier((edge, volume, cotangent))
    cross = send_across(edge)
    vol_sib = send(late_volume, sibling)
    cot_sib = send(late_cotangent, sibling)

    def wide(count, wide_channels):
        return pltpu.VMEM((count, width + 2, height, wide_channels), BF16)

    slab_type = jax.ShapeDtypeStruct(volume.shape, BF16)
    sums_type = jax.ShapeDtypeStruct((planes, width * height, channels), F32)

    vol_sib, cot_sib = lax.optimization_barrier((vol_sib, cot_sib))
    part = call(
        functools.partial(inner_kernel, size),
        sums_type,
        [wide(4, 3 * channels)],
        "inner",
    )(volume, vol_sib, first_filter)
    cross, part = lax.optimization_barrier((cross, part))
    hidden, act = call(
        functools.partial(hidden_kernel, size),
        (sums_type, slab_type),
        [wide(1, 3 * channels)],
        "hidden",
    )(part, cross, first_filter)
    act_sib = send(act, sibling)
    late_cross, hidden = lax.optimization_barrier((cross, hidden))
    cross_far = send(late_cross, sibling)
    grad = call(
        functools.partial(hidden_grad_kernel, size),
        slab_type,
        [wide(4, 3 * channels)],
        "hidden_grad",
    )(hidden, cotangent, cot_sib, cross, second_filter)
    grad_sib = send(grad, sibling)

    block_type = jax.ShapeDtypeStruct((27, channels // 8, channels), BF16)
    keep_type = jax.ShapeDtypeStruct(block_type.shape, F32)

    def filter_grad(which, operands, name):
        keep, *blocks = call(
            functools.partial(weight_kernel, size, which),
            (keep_type,) + (block_type,) * 3,
            [
                wide(4 if which else 6, 2 * channels),
                pltpu.VMEM((6 if which else 4, channels, width * height), BF16),
            ],
            name,
        )(*operands)
        return keep, [send(blocks[d - 1], hop(2 * d)) for d in (3, 1, 2)]

    def near_sum(keep, gots, name):
        if share % 8:
            total = (keep + sum(got.astype(F32) for got in gots)).reshape(27, far, share, channels)
            blocks = [total[:, q].reshape(27 * share, channels) for q in range(far)]
            return [blocks[0]] + [b.astype(BF16) for b in blocks[1:]]
        rows = 27 * share
        padded = -(-rows // 16) * 16
        return call(
            functools.partial(near_sum_kernel, share),
            (jax.ShapeDtypeStruct((rows, channels), F32),)
            + (jax.ShapeDtypeStruct((padded, channels), BF16),) * (far - 1),
            [],
            name,
        )(keep, *gots)

    def far_hop(blocks):
        return [send(block, hop(8 * q)) for q, block in enumerate(blocks[1:], 1)]

    def last_sum(own, gots, name):
        if share % 8:
            total = own
            for got in gots:
                total = total + got.astype(F32)
        else:
            total = call(
                last_sum_kernel, jax.ShapeDtypeStruct(own.shape, F32), [], name
            )(own, *gots)
        return jnp.transpose(total.reshape(3, 3, 3, share, channels), (3, 0, 1, 2, 4))

    keep_2, gots_2 = filter_grad(1, (cotangent, cot_sib, cross, cross_far, act, act_sib), "second_grad")
    grad_sib, keep_2 = lax.optimization_barrier((grad_sib, keep_2))
    keep_1, gots_1 = filter_grad(0, (volume, vol_sib, cross, cross_far, grad, grad_sib), "first_grad")
    blocks_2 = near_sum(keep_2, gots_2, "second_near_sum")
    gots_2 = far_hop(blocks_2)
    late_act, _ = lax.optimization_barrier((act, blocks_2[0]))
    response = call(
        functools.partial(response_kernel, size),
        slab_type,
        [wide(3, 3 * channels), wide(4, 3 * channels)],
        "response",
    )(late_act, act_sib, volume, cross, first_filter, second_filter)
    keep_1, response = lax.optimization_barrier((keep_1, response))
    blocks_1 = near_sum(keep_1, gots_1, "first_near_sum")
    gots_1 = far_hop(blocks_1)
    second_grad = last_sum(blocks_2[0], gots_2, "second_last_sum")
    first_grad = last_sum(blocks_1[0], gots_1, "first_last_sum")
    return response, first_grad, second_grad


def solution(mesh):
    size = mesh.shape["space"]
    return jax.shard_map(
        functools.partial(per_device, mesh.shape["parts"], size),
        mesh=mesh,
        in_specs=(
            P(("parts", "space"), None, None, None),
            P(),
            P(),
            P(("parts", "space"), None, None, None),
        ),
        out_specs=(
            P(("parts", "space"), None, None, None),
            P(("parts", "space"), None, None, None, None),
            P(("parts", "space"), None, None, None, None),
        ),
        check_vma=False,
    )
```

time: 46.7 us -> 34.5 us (0.74)
  waiting for transfers between devices: 9.8 us -> 3.96 us
  starting transfers between devices: 22.8 us -> 18.3 us
  local copies, waits for them, and re-layouts: 4.19 us -> 1.96 us
    ppermute x15 -> x13, starting transfers between devices: 22.8 us -> 15.3 us  [send(): return lax.ppermute(array, 'space', moves)]
    ppermute x15 -> x13, waiting for transfers between devices: 9.8 us -> 3.96 us  [send(): return lax.ppermute(array, 'space', moves)]
    unnamed x14 -> x10, local copies, waits for them, and re-layouts: 4.16 us -> 0.93 us
    ppermute x0 -> x1, starting transfers between devices: none -> 3 us  [send_across(): return lax.ppermute(array, ('parts', 'space'), across)]
    slice x2 -> x1, local copies, waits for them, and re-layouts: 0.04 us -> 1.03 us  [per_device(): cotangent[1]]
    pallas_call x8 -> x10, Pallas kernels: 8.96 us -> 9.35 us  [the longest x2 2.69 us: filter_grad(): call(functools.partial(weight_kernel, size, which), (keep_type,) + (block...]
  transfers between devices with their start and end apart: 15 -> 14, of which waited for: 7 -> 3; matrix products, arithmetic and copies ran while one was open for 0% -> 0% of each run, Pallas kernels for 13% -> 24%
where the time goes in v3:
time: 34.5 us; the launch traced here: 34.4 us
  starting transfers between devices  18.3 us (53%)
  Pallas kernels  9.35 us (27%)
  waiting for transfers between devices  3.96 us (11%)
  local copies, waits for them, and re-layouts  1.96 us (6%)
  between operations  0.74 us (2%)
    ppermute x13, starting transfers between devices, send(): return lax.ppermute(array, 'space', moves)  15.3 us
    ppermute x13, waiting for transfers between devices, send(): return lax.ppermute(array, 'space', moves)  3.96 us
    ppermute x1, starting transfers between devices, send_across(): return lax.ppermute(array, ('parts', 'space'), across)  3 us
    pallas_call x2, Pallas kernels, filter_grad(): call(functools.partial(weight_kernel, size, which), (keep_type,) + (block...  2.69 us
    pallas_call x1, Pallas kernels, per_device(): call(functools.partial(response_kernel, size), slab_type, [wide(3, 3 * ch...  2.51 us
    pallas_call x2, Pallas kernels, last_sum(): call(last_sum_kernel, jax.ShapeDtypeStruct(own.shape, F32), [], name)  1.32 us
    pallas_call x1, Pallas kernels, per_device(): call(functools.partial(hidden_grad_kernel, size), slab_type, [wide(4, 3 *...  1.22 us
    pallas_call x1, Pallas kernels, per_device(): call(functools.partial(inner_kernel, size), sums_type, [wide(4, 3 * chann...  1.16 us
  transfers between devices with their start and end apart: 14, of which 3 were waited for; matrix products, arithmetic and copies ran while one was open for 0% of the time, Pallas kernels for 24%

profile of v3, /device:TPU:0, one launch (start us, length us, event | category | flops | bytes accessed | tf_op | source)
XLA Modules:
  0.0 34.4 jit_solution(17779229029052920665)
XLA Ops:
  0.6 1.0 %fusion = (bf16[1,16,16,128]{3,2,1,0:T(8,128)(2,1)S(1)}, bf16[1,16,16,128]{3,2,1,0:T(8,128)(2,1)S(1)}, bf16[1,16,16,128]{3,2,1,0:T(8,128)(2,1)S(1)}, bf16[1,16,16,128]{3,2,1,0:T(8,128)(2,1)S(1)}) fusion(bf16[2,16,16,128]{3,2,1,0:T(8,128)(2,1)} %own.2, bf16[2,16,16,128]{3,2,1,0:T(8,128)(2,1)} %vol.3), kind=kLoop, calls=%fused_computation.1 | loop fusion | bytes 524288 | tf_op jit(solution)/shard_map/slice | solution.py:277
  1.7 3.0 %collective-permute-start.2 = (bf16[3,16,16,128]{3,2,1,0:T(8,128)(2,1)S(1)}, bf16[3,16,16,128]{3,2,1,0:T(8,128)(2,1)S(1)}, u32[]{:S(2)}, u32[]{:S(2)}) collective-permute-start(bf16[3,16,16,128]{3,2,1,0:T(8,128)(2,1)S(1)} %maximum_select_fusion), channel_id=1, source_target_pairs={{1,2},{3,4},{5,6},{7,8},{9,10},{11,12},{13,14},{17,18},{19,20},{21... | collective-permute-start | bytes 589832 | tf_op jit(solution)/shard_map/ppermute | solution.py:261
  4.7 0.1 collective-permute-start
  4.9 0.4 %collective-permute-start.1 = (bf16[2,16,16,128]{3,2,1,0:T(8,128)(2,1)}, bf16[2,16,16,128]{3,2,1,0:T(8,128)(2,1)S(1)}, u32[]{:S(2)}, u32[]{:S(2)}) collective-permute-start(bf16[2,16,16,128]{3,2,1,0:T(8,128)(2,1)} %own.2), channel_id=1, source_target_pairs={{0,1},{1,0},{2,3},{3,2},{4,5},{5,4},{6,7},{7,6},{8,9},{9,8},{10,11... | collective-permute-start | bytes 393224 | tf_op jit(solution)/shard_map/ppermute | solution.py:258
  5.2 1.0 %collective-permute-done.sib = bf16[2,16,16,128]{3,2,1,0:T(8,128)(2,1)S(1)} collective-permute-done((bf16[2,16,16,128]{3,2,1,0:T(8,128)(2,1)}, bf16[2,16,16,128]{3,2,1,0:T(8,128)(2,1)S(1)}, u32[]{:S(2)}, u32[]{:S(2)}) %collective-permute-start) | collective-permute-done | bytes 131104 | tf_op jit(solution)/shard_map/ppermute | solution.py:258
  6.3 0.2 collective-permute-done.1.sib
  6.5 0.9 %copy-done.2 = bf16[2,16,16,128]{3,2,1,0:T(8,128)(2,1)S(1)} copy-done((bf16[2,16,16,128]{3,2,1,0:T(8,128)(2,1)S(1)}, bf16[2,16,16,128]{3,2,1,0:T(8,128)(2,1)}, u32[]{:S(2)}) %copy-start.2) | copy-done | bytes 131096
  7.4 1.2 %inner.1.part = f32[2,256,128]{2,1,0:T(8,128)S(1)} custom-call(bf16[2,16,16,128]{3,2,1,0:T(8,128)(2,1)S(1)} %copy-done.2, bf16[2,16,16,128]{3,2,1,0:T(8,128)(2,1)S(1)} %collective-permute-done.sib, bf16[3,3,3,128,128]{4,3,2,1,0:T(8,128)(2,1)S(1)} %copy-done), custom_call_target="tpu_custom_call" | custom-call | tf_op jit(solution)/shard_map/inner/pallas_call | solution.py:291
  8.6 0.0 copy-start.1
  8.6 0.0 copy-start.4
  8.6 0.3 hidden.1
  8.9 1.1 %collective-permute-start.3 = (bf16[3,16,16,128]{3,2,1,0:T(8,128)(2,1)S(1)}, bf16[3,16,16,128]{3,2,1,0:T(8,128)(2,1)S(1)}, u32[]{:S(2)}, u32[]{:S(2)}) collective-permute-start(bf16[3,16,16,128]{3,2,1,0:T(8,128)(2,1)S(1)} %collective-permute-done.2.cross), channel_id=1, source_target_pairs={{0,1},{1,0},{2,3},{3,2},{4,5},{5,4},{6,7},{7,6},{8,9},{9,8},{10,11... | collective-permute-start | bytes 589832 | tf_op jit(solution)/shard_map/ppermute | solution.py:258
  10.0 0.1 collective-permute-start.5
  10.1 1.2 %hidden_grad.1.four = bf16[2,16,16,128]{3,2,1,0:T(8,128)(2,1)S(1)} custom-call(f32[2,256,128]{2,1,0:T(8,128)S(1)} %get-tuple-element.39.hidden, bf16[2,16,16,128]{3,2,1,0:T(8,128)(2,1)S(1)} %copy-done.4, bf16[2,16,16,128]{3,2,1,0:T(8,128)(2,1)S(1)} %collective-permute-done.1.sib, bf16[3,16,16,128]{3,2,1,0:T(8,128)(2,1)S(1)} %collective-permute-done.2.cross, ...), custom_call_target="tpu_custom_call" | custom-call | tf_op jit(solution)/shard_map/hidden_grad/pallas_call | solution.py:307
  11.3 0.5 %collective-permute-start.4 = (bf16[2,16,16,128]{3,2,1,0:T(8,128)(2,1)S(1)}, bf16[2,16,16,128]{3,2,1,0:T(8,128)(2,1)S(1)}, u32[]{:S(2)}, u32[]{:S(2)}) collective-permute-start(bf16[2,16,16,128]{3,2,1,0:T(8,128)(2,1)S(1)} %hidden_grad.1.four), channel_id=1, source_target_pairs={{0,1},{1,0},{2,3},{3,2},{4,5},{5,4},{6,7},{7,6},{8,9},{9,8},{10,11... | collective-permute-start | bytes 393224 | tf_op jit(solution)/shard_map/ppermute | solution.py:258
  11.8 0.0 collective-permute-done.5.four_sib.sib
  11.8 1.3 %second_grad.1 = (f32[27,16,128]{2,1,0:T(8,128)S(1)}, bf16[27,16,128]{2,1,0:T(8,128)(2,1)S(1)}, bf16[27,16,128]{2,1,0:T(8,128)(2,1)S(1)}, bf16[27,16,128]{2,1,0:T(8,128)(2,1)S(1)}) custom-call(bf16[2,16,16,128]{3,2,1,0:T(8,128)(2,1)S(1)} %copy-done.4, bf16[2,16,16,128]{3,2,1,0:T(8,128)(2,1)S(1)} %collective-permute-done.1.sib, ...), custom_call_target="tpu_custom_call" | custom-call | tf_op jit(solution)/shard_map/second_grad/pallas_call | solution.py:319
  13.2 3.5 %collective-permute-start.6 = (bf16[27,16,128]{2,1,0:T(8,128)(2,1)S(1)}, bf16[27,16,128]{2,1,0:T(8,128)(2,1)S(1)}, u32[]{:S(2)}, u32[]{:S(2)}) collective-permute-start(bf16[27,16,128]{2,1,0:T(8,128)(2,1)S(1)} %get-tuple-element.46), channel_id=1, source_target_pairs={{0,6},{1,7},{2,4},{3,5},{4,2},{5,3},{6,0},{7,1},{8,14},{9,15},{10,... | collective-permute-start | bytes 331784 | tf_op jit(solution)/shard_map/ppermute | solution.py:258
  16.7 0.3 collective-permute-start.7
  17.0 0.3 collective-permute-start.8
  17.3 1.4 %first_grad.1 = (f32[27,16,128]{2,1,0:T(8,128)S(1)}, bf16[27,16,128]{2,1,0:T(8,128)(2,1)S(1)}, bf16[27,16,128]{2,1,0:T(8,128)(2,1)S(1)}, bf16[27,16,128]{2,1,0:T(8,128)(2,1)S(1)}) custom-call(bf16[2,16,16,128]{3,2,1,0:T(8,128)(2,1)S(1)} %copy-done.2, bf16[2,16,16,128]{3,2,1,0:T(8,128)(2,1)S(1)} %collective-permute-done.sib, ...), custom_call_target="tpu_custom_call" | custom-call | tf_op jit(solution)/shard_map/first_grad/pallas_call | solution.py:319
  18.7 1.9 %collective-permute-start.10 = (bf16[27,16,128]{2,1,0:T(8,128)(2,1)S(1)}, bf16[27,16,128]{2,1,0:T(8,128)(2,1)S(1)}, u32[]{:S(2)}, u32[]{:S(2)}) collective-permute-start(bf16[27,16,128]{2,1,0:T(8,128)(2,1)S(1)} %get-tuple-element.54), channel_id=1, source_target_pairs={{0,2},{1,3},{2,0},{3,1},{4,6},{5,7},{6,4},{7,5},{8,10},{9,11},{10,... | collective-permute-start | bytes 331784 | tf_op jit(solution)/shard_map/ppermute | solution.py:258
  20.6 1.6 %collective-permute-start.11 = (bf16[27,16,128]{2,1,0:T(8,128)(2,1)S(1)}, bf16[27,16,128]{2,1,0:T(8,128)(2,1)S(1)}, u32[]{:S(2)}, u32[]{:S(2)}) collective-permute-start(bf16[27,16,128]{2,1,0:T(8,128)(2,1)S(1)} %get-tuple-element.55), channel_id=1, source_target_pairs={{0,4},{1,5},{2,6},{3,7},{4,0},{5,1},{6,2},{7,3},{8,12},{9,13},{10,... | collective-permute-start | bytes 331784 | tf_op jit(solution)/shard_map/ppermute | solution.py:258
  22.2 1.3 %collective-permute-start.9 = (bf16[27,16,128]{2,1,0:T(8,128)(2,1)S(1)}, bf16[27,16,128]{2,1,0:T(8,128)(2,1)S(1)}, u32[]{:S(2)}, u32[]{:S(2)}) collective-permute-start(bf16[27,16,128]{2,1,0:T(8,128)(2,1)S(1)} %get-tuple-element.53), channel_id=1, source_target_pairs={{0,6},{1,7},{2,4},{3,5},{4,2},{5,3},{6,0},{7,1},{8,14},{9,15},{10,... | collective-permute-start | bytes 331784 | tf_op jit(solution)/shard_map/ppermute | solution.py:258
  23.5 0.1 second_near_sum.1
  23.6 2.4 %collective-permute-start.13 = (bf16[224,128]{1,0:T(8,128)(2,1)S(1)}, bf16[224,128]{1,0:T(8,128)(2,1)S(1)}, u32[]{:S(2)}, u32[]{:S(2)}) collective-permute-start(bf16[224,128]{1,0:T(8,128)(2,1)S(1)} %get-tuple-element.58), channel_id=1, source_target_pairs={{0,8},{1,9},{2,10},{3,11},{4,12},{5,13},{6,14},{7,15},{8,0},{9,1},... | collective-permute-start | bytes 172040 | tf_op jit(solution)/shard_map/ppermute | solution.py:258
  26.0 2.5 %response.1 = bf16[2,16,16,128]{3,2,1,0:T(8,128)(2,1)} custom-call(bf16[2,16,16,128]{3,2,1,0:T(8,128)(2,1)S(1)} %get-tuple-element.50.four.act, bf16[2,16,16,128]{3,2,1,0:T(8,128)(2,1)S(1)} %collective-permute-done.5.four_sib.sib, bf16[2,16,16,128]{3,2,1,0:T(8,128)(2,1)S(1)} %copy-done.3, bf16[3,16,16,128]{3,2,1,0:T(8,128)(2,1)S(1)} %collective-permute-done.2.cross, ...), custom_call_target="tpu_custom_call" | custom-call | tf_op jit(solution)/shard_map/response/pallas_call | solution.py:365
  28.5 0.1 first_near_sum.1
  28.6 1.8 %collective-permute-start.12 = (bf16[224,128]{1,0:T(8,128)(2,1)S(1)}, bf16[224,128]{1,0:T(8,128)(2,1)S(1)}, u32[]{:S(2)}, u32[]{:S(2)}) collective-permute-start(bf16[224,128]{1,0:T(8,128)(2,1)S(1)} %get-tuple-element.57), channel_id=1, source_target_pairs={{0,8},{1,9},{2,10},{3,11},{4,12},{5,13},{6,14},{7,15},{8,0},{9,1},... | collective-permute-start | bytes 172040 | tf_op jit(solution)/shard_map/ppermute | solution.py:258
  30.4 0.7 %second_last_sum.1 = f32[216,128]{1,0:T(8,128)} custom-call(f32[216,128]{1,0:T(8,128)S(1)} %get-tuple-element.49.refs_0_, bf16[224,128]{1,0:T(8,128)(2,1)S(1)} %collective-permute-done.13.refs_1_), custom_call_target="tpu_custom_call" | custom-call | tf_op jit(solution)/shard_map/second_last_sum/pallas_call | solution.py:354
  31.0 2.7 %collective-permute-done.12.refs_1_ = bf16[224,128]{1,0:T(8,128)(2,1)S(1)} collective-permute-done((bf16[224,128]{1,0:T(8,128)(2,1)S(1)}, bf16[224,128]{1,0:T(8,128)(2,1)S(1)}, u32[]{:S(2)}, u32[]{:S(2)}) %collective-permute-start.12) | collective-permute-done | bytes 57376 | tf_op jit(solution)/shard_map/ppermute | solution.py:258
  33.7 0.7 %first_last_sum.1 = f32[216,128]{1,0:T(8,128)} custom-call(f32[216,128]{1,0:T(8,128)S(1)} %get-tuple-element.56.refs_0_, bf16[224,128]{1,0:T(8,128)(2,1)S(1)} %collective-permute-done.12.refs_1_), custom_call_target="tpu_custom_call" | custom-call | tf_op jit(solution)/shard_map/first_last_sum/pallas_call | solution.py:354
  (18 shorter events, 0.1 us)
Async XLA Ops:
  0.6 5.9 %copy-start = (bf16[3,3,3,128,128]{4,3,2,1,0:T(8,128)(2,1)S(1)}, bf16[3,3,3,128,128]{4,3,2,1,0:T(8,128)(2,1)}, u32[]{:S(2)}) copy-start(bf16[3,3,3,128,128]{4,3,2,1,0:T(8,128)(2,1)} %first.5) | copy-start | bytes 2654212
  1.7 6.8 %collective-permute-start.2 = (bf16[3,16,16,128]{3,2,1,0:T(8,128)(2,1)S(1)}, bf16[3,16,16,128]{3,2,1,0:T(8,128)(2,1)S(1)}, u32[]{:S(2)}, u32[]{:S(2)}) collective-permute-start(bf16[3,16,16,128]{3,2,1,0:T(8,128)(2,1)S(1)} %maximum_select_fusion), channel_id=1, source_target_pairs={{1,2},{3,4},{5,6},{7,8},{9,10},{11,12},{13,14},{17,18},{19,20},{21... | collective-permute-start | bytes 589832 | tf_op jit(solution)/shard_map/ppermute | solution.py:261
  4.7 1.6 %collective-permute-start = (bf16[2,16,16,128]{3,2,1,0:T(8,128)(2,1)}, bf16[2,16,16,128]{3,2,1,0:T(8,128)(2,1)S(1)}, u32[]{:S(2)}, u32[]{:S(2)}) collective-permute-start(bf16[2,16,16,128]{3,2,1,0:T(8,128)(2,1)} %vol.3), channel_id=1, source_target_pairs={{0,1},{1,0},{2,3},{3,2},{4,5},{5,4},{6,7},{7,6},{8,9},{9,8},{10,11... | collective-permute-start | bytes 393224 | tf_op jit(solution)/shard_map/ppermute | solution.py:258
  4.9 1.6 %collective-permute-start.1 = (bf16[2,16,16,128]{3,2,1,0:T(8,128)(2,1)}, bf16[2,16,16,128]{3,2,1,0:T(8,128)(2,1)S(1)}, u32[]{:S(2)}, u32[]{:S(2)}) collective-permute-start(bf16[2,16,16,128]{3,2,1,0:T(8,128)(2,1)} %own.2), channel_id=1, source_target_pairs={{0,1},{1,0},{2,3},{3,2},{4,5},{5,4},{6,7},{7,6},{8,9},{9,8},{10,11... | collective-permute-start | bytes 393224 | tf_op jit(solution)/shard_map/ppermute | solution.py:258
  6.5 0.9 %copy-start.2 = (bf16[2,16,16,128]{3,2,1,0:T(8,128)(2,1)S(1)}, bf16[2,16,16,128]{3,2,1,0:T(8,128)(2,1)}, u32[]{:S(2)}) copy-start(bf16[2,16,16,128]{3,2,1,0:T(8,128)(2,1)} %vol.3) | copy-start | bytes 393220
  8.6 1.5 %copy-start.1 = (bf16[3,3,3,128,128]{4,3,2,1,0:T(8,128)(2,1)S(1)}, bf16[3,3,3,128,128]{4,3,2,1,0:T(8,128)(2,1)}, u32[]{:S(2)}) copy-start(bf16[3,3,3,128,128]{4,3,2,1,0:T(8,128)(2,1)} %second.3) | copy-start | bytes 2654212
  8.6 1.5 %copy-start.4 = (bf16[2,16,16,128]{3,2,1,0:T(8,128)(2,1)S(1)}, bf16[2,16,16,128]{3,2,1,0:T(8,128)(2,1)}, u32[]{:S(2)}) copy-start(bf16[2,16,16,128]{3,2,1,0:T(8,128)(2,1)} %own.2) | copy-start | bytes 393220
  8.9 2.9 %collective-permute-start.3 = (bf16[3,16,16,128]{3,2,1,0:T(8,128)(2,1)S(1)}, bf16[3,16,16,128]{3,2,1,0:T(8,128)(2,1)S(1)}, u32[]{:S(2)}, u32[]{:S(2)}) collective-permute-start(bf16[3,16,16,128]{3,2,1,0:T(8,128)(2,1)S(1)} %collective-permute-done.2.cross), channel_id=1, source_target_pairs={{0,1},{1,0},{2,3},{3,2},{4,5},{5,4},{6,7},{7,6},{8,9},{9,8},{10,11... | collective-permute-start | bytes 589832 | tf_op jit(solution)/shard_map/ppermute | solution.py:258
  10.0 1.8 %collective-permute-start.5 = (bf16[2,16,16,128]{3,2,1,0:T(8,128)(2,1)S(1)}, bf16[2,16,16,128]{3,2,1,0:T(8,128)(2,1)S(1)}, u32[]{:S(2)}, u32[]{:S(2)}) collective-permute-start(bf16[2,16,16,128]{3,2,1,0:T(8,128)(2,1)S(1)} %get-tuple-element.50.four.act), channel_id=1, source_target_pairs={{0,1},{1,0},{2,3},{3,2},{4,5},{5,4},{6,7},{7,6},{8,9},{9,8},{10,11... | collective-permute-start | bytes 393224 | tf_op jit(solution)/shard_map/ppermute | solution.py:258
  11.3 6.0 %collective-permute-start.4 = (bf16[2,16,16,128]{3,2,1,0:T(8,128)(2,1)S(1)}, bf16[2,16,16,128]{3,2,1,0:T(8,128)(2,1)S(1)}, u32[]{:S(2)}, u32[]{:S(2)}) collective-permute-start(bf16[2,16,16,128]{3,2,1,0:T(8,128)(2,1)S(1)} %hidden_grad.1.four), channel_id=1, source_target_pairs={{0,1},{1,0},{2,3},{3,2},{4,5},{5,4},{6,7},{7,6},{8,9},{9,8},{10,11... | collective-permute-start | bytes 393224 | tf_op jit(solution)/shard_map/ppermute | solution.py:258
  13.2 9.0 %collective-permute-start.6 = (bf16[27,16,128]{2,1,0:T(8,128)(2,1)S(1)}, bf16[27,16,128]{2,1,0:T(8,128)(2,1)S(1)}, u32[]{:S(2)}, u32[]{:S(2)}) collective-permute-start(bf16[27,16,128]{2,1,0:T(8,128)(2,1)S(1)} %get-tuple-element.46), channel_id=1, source_target_pairs={{0,6},{1,7},{2,4},{3,5},{4,2},{5,3},{6,0},{7,1},{8,14},{9,15},{10,... | collective-permute-start | bytes 331784 | tf_op jit(solution)/shard_map/ppermute | solution.py:258
  16.7 6.8 %collective-permute-start.7 = (bf16[27,16,128]{2,1,0:T(8,128)(2,1)S(1)}, bf16[27,16,128]{2,1,0:T(8,128)(2,1)S(1)}, u32[]{:S(2)}, u32[]{:S(2)}) collective-permute-start(bf16[27,16,128]{2,1,0:T(8,128)(2,1)S(1)} %get-tuple-element.47), channel_id=1, source_target_pairs={{0,2},{1,3},{2,0},{3,1},{4,6},{5,7},{6,4},{7,5},{8,10},{9,11},{10,... | collective-permute-start | bytes 331784 | tf_op jit(solution)/shard_map/ppermute | solution.py:258
  17.0 6.5 %collective-permute-start.8 = (bf16[27,16,128]{2,1,0:T(8,128)(2,1)S(1)}, bf16[27,16,128]{2,1,0:T(8,128)(2,1)S(1)}, u32[]{:S(2)}, u32[]{:S(2)}) collective-permute-start(bf16[27,16,128]{2,1,0:T(8,128)(2,1)S(1)} %get-tuple-element.48), channel_id=1, source_target_pairs={{0,4},{1,5},{2,6},{3,7},{4,0},{5,1},{6,2},{7,3},{8,12},{9,13},{10,... | collective-permute-start | bytes 331784 | tf_op jit(solution)/shard_map/ppermute | solution.py:258
  18.7 9.8 %collective-permute-start.10 = (bf16[27,16,128]{2,1,0:T(8,128)(2,1)S(1)}, bf16[27,16,128]{2,1,0:T(8,128)(2,1)S(1)}, u32[]{:S(2)}, u32[]{:S(2)}) collective-permute-start(bf16[27,16,128]{2,1,0:T(8,128)(2,1)S(1)} %get-tuple-element.54), channel_id=1, source_target_pairs={{0,2},{1,3},{2,0},{3,1},{4,6},{5,7},{6,4},{7,5},{8,10},{9,11},{10,... | collective-permute-start | bytes 331784 | tf_op jit(solution)/shard_map/ppermute | solution.py:258
  20.6 7.9 %collective-permute-start.11 = (bf16[27,16,128]{2,1,0:T(8,128)(2,1)S(1)}, bf16[27,16,128]{2,1,0:T(8,128)(2,1)S(1)}, u32[]{:S(2)}, u32[]{:S(2)}) collective-permute-start(bf16[27,16,128]{2,1,0:T(8,128)(2,1)S(1)} %get-tuple-element.55), channel_id=1, source_target_pairs={{0,4},{1,5},{2,6},{3,7},{4,0},{5,1},{6,2},{7,3},{8,12},{9,13},{10,... | collective-permute-start | bytes 331784 | tf_op jit(solution)/shard_map/ppermute | solution.py:258
  22.2 3.8 %copy-start.3 = (bf16[2,16,16,128]{3,2,1,0:T(8,128)(2,1)S(1)}, bf16[2,16,16,128]{3,2,1,0:T(8,128)(2,1)}, u32[]{:S(2)}) copy-start(bf16[2,16,16,128]{3,2,1,0:T(8,128)(2,1)} %vol.3) | copy-start | bytes 393220
  22.2 6.4 %collective-permute-start.9 = (bf16[27,16,128]{2,1,0:T(8,128)(2,1)S(1)}, bf16[27,16,128]{2,1,0:T(8,128)(2,1)S(1)}, u32[]{:S(2)}, u32[]{:S(2)}) collective-permute-start(bf16[27,16,128]{2,1,0:T(8,128)(2,1)S(1)} %get-tuple-element.53), channel_id=1, source_target_pairs={{0,6},{1,7},{2,4},{3,5},{4,2},{5,3},{6,0},{7,1},{8,14},{9,15},{10,... | collective-permute-start | bytes 331784 | tf_op jit(solution)/shard_map/ppermute | solution.py:258
  23.6 6.8 %collective-permute-start.13 = (bf16[224,128]{1,0:T(8,128)(2,1)S(1)}, bf16[224,128]{1,0:T(8,128)(2,1)S(1)}, u32[]{:S(2)}, u32[]{:S(2)}) collective-permute-start(bf16[224,128]{1,0:T(8,128)(2,1)S(1)} %get-tuple-element.58), channel_id=1, source_target_pairs={{0,8},{1,9},{2,10},{3,11},{4,12},{5,13},{6,14},{7,15},{8,0},{9,1},... | collective-permute-start | bytes 172040 | tf_op jit(solution)/shard_map/ppermute | solution.py:258
  28.6 5.2 %collective-permute-start.12 = (bf16[224,128]{1,0:T(8,128)(2,1)S(1)}, bf16[224,128]{1,0:T(8,128)(2,1)S(1)}, u32[]{:S(2)}, u32[]{:S(2)}) collective-permute-start(bf16[224,128]{1,0:T(8,128)(2,1)S(1)} %get-tuple-element.57), channel_id=1, source_target_pairs={{0,8},{1,9},{2,10},{3,11},{4,12},{5,13},{6,14},{7,15},{8,0},{9,1},... | collective-permute-start | bytes 172040 | tf_op jit(solution)/shard_map/ppermute | solution.py:258

commit v4 on v3

--- a/solution.py
+++ b/solution.py
@@ -60,80 +60,88 @@
     return wide[plane : plane + planes, column : column + rows].reshape(planes * rows * lanes, channels)
 
 
-def convolve(wide, weight, planes):
+def forward(block, kernel):
     total = None
-    for plane in range(3):
-        for column in range(3):
-            kernel = weight[plane, column]
-            term = jnp.dot(
-                patch(wide, plane, planes, column),
-                kernel.reshape(-1, kernel.shape[-1]),
+    for column in range(3):
+        taps = kernel(column)
+        term = jnp.dot(block(column), taps.reshape(-1, taps.shape[-1]), preferred_element_type=F32)
+        total = term if total is None else total + term
+    return total
+
+
+def backward(block, kernel):
+    total = None
+    for column in range(3):
+        voxels, taps = block(column), kernel(2 - column)
+        channels = taps.shape[-1]
+        for lane in range(3):
+            term = lax.dot_general(
+                voxels[:, lane * channels : (lane + 1) * channels],
+                taps[2 - lane],
+                (((1,), (1,)), ((), ())),
                 preferred_element_type=F32,
             )
             total = term if total is None else total + term
     return total
 
 
-def convolve_back(wide, weight, planes):
-    channels = weight.shape[4]
+def convolve(wide, weight, planes):
     total = None
     for plane in range(3):
-        for column in range(3):
-            block = patch(wide, plane, planes, column)
-            for lane in range(3):
-                term = lax.dot_general(
-                    block[:, lane * channels : (lane + 1) * channels],
-                    weight[2 - plane, 2 - column, 2 - lane],
-                    (((1,), (1,)), ((), ())),
-                    preferred_element_type=F32,
-                )
-                total = term if total is None else total + term
+        term = forward(
+            lambda column: patch(wide, plane, planes, column), lambda column: weight[plane, column]
+        )
+        total = term if total is None else total + term
     return total
 
 
-def inner_kernel(size, vol, sib, first, part, wide):
-    _, core = core_of(size)
+def inner_kernel(back, own, weight, part, wide):
+    run = backward if back else forward
     edge_rows(wide)
-    widen(wide, 1, vol[0])
-    widen(wide, 2, vol[1])
-    widen(wide, 3 * (1 - core), sib[core])
-    wide[3 * core] = jnp.zeros(wide.shape[1:], BF16)
-    part[...] = convolve(wide, first, 2).reshape(part.shape)
-
-
-def hidden_kernel(size, part, cross, first, hidden, act, wide):
+    widen(wide, 0, own[0])
+    widen(wide, 1, own[1])
+    middle = run(lambda column: patch(wide, 0, 2, column), lambda column: weight[1, column])
+    voxels = middle.shape[0] // 2
+    for plane in range(2):
+        tap = 2 * plane if back else 2 - 2 * plane
+        side = run(lambda column: patch(wide, 1 - plane, 1, column), lambda column: weight[tap, column])
+        part[plane] = middle[plane * voxels : (plane + 1) * voxels] + side
+
+
+def neighbours(size, back, part, sib, cross, weight, wide):
     index, core = core_of(size)
+    run = backward if back else forward
     edge_rows(wide)
-    widen(wide, 0, cross[0].astype(F32) * within(index, size))
-    grown = part[core]
-    for column in range(3):
-        kernel = first[2 * core, column]
-        grown = grown + jnp.dot(
-            patch(wide, 0, 1, column), kernel.reshape(-1, kernel.shape[-1]), preferred_element_type=F32
-        )
-    for at, held in ((core, grown), (1 - core, part[1 - core])):
+    widen(wide, 0, cross.astype(F32) * within(index, size))
+    widen(wide, 1, sib[core])
+    for at, plane in ((core, 0), (1 - core, 1)):
+        tap = 2 - 2 * at if back else 2 * at
+        side = run(lambda column: patch(wide, plane, 1, column), lambda column: weight[tap, column])
+        yield at, part[at] + side
+
+
+def hidden_kernel(size, part, sib, cross, cot_cross, first, hidden, near, wide):
+    index, core = core_of(size)
+    for at, held in neighbours(size, False, part, sib, cross[1 - core], first, wide):
         hidden[at] = held
-        act[at] = (held * jax.nn.sigmoid(held)).astype(BF16).reshape(act.shape[1:])
-
-
-def hidden_grad_kernel(size, hidden, cot, sib, cross, second, out, wide):
-    index, core = core_of(size)
-    edge_rows(wide)
-    widen(wide, 1, cot[0])
-    widen(wide, 2, cot[1])
-    widen(wide, 3 * (1 - core), sib[core])
-    widen(wide, 3 * core, cross[1].astype(F32) * within(index, size))
-    act_grad = convolve_back(wide, second, 2)
-    held = hidden[...].reshape(act_grad.shape)
-    sigma = jax.nn.sigmoid(held)
-    out[...] = (act_grad * sigma * (1.0 + held * (1.0 - sigma))).astype(BF16).reshape(out.shape)
+        near[at] = (held * jax.nn.sigmoid(held)).astype(BF16).reshape(near.shape[1:])
+    for i, plane in enumerate((cross[1 - core], cot_cross[...])):
+        near[2 + i] = (plane.astype(F32) * within(index, size)).astype(BF16)
+
+
+def hidden_grad_kernel(size, hidden, part, sib, cross, second, out, wide):
+    for at, act_grad in neighbours(size, True, part, sib, cross[...], second, wide):
+        held = hidden[at]
+        sigma = jax.nn.sigmoid(held)
+        grad = act_grad * sigma * (1.0 + held * (1.0 - sigma))
+        out[at] = grad.astype(BF16).reshape(out.shape[1:])
 
 
 def response_kernel(size, act, sib, vol, cross, first, second, out, vol_wide, wide):
     index, core = core_of(size)
     edge_rows(vol_wide)
-    widen(vol_wide, 1, cross[0])
-    widen(vol_wide, 2 * core, cross[2])
+    widen(vol_wide, 1, act[2])
+    widen(vol_wide, 2 * core, cross[core])
     widen(vol_wide, 2 * (1 - core), vol[core])
     hidden = convolve(vol_wide, first, 1)
     outer = hidden * jax.nn.sigmoid(hidden) * within(index, size)
@@ -157,7 +165,7 @@
 
 def narrow(wide, at, plane, choice):
     rows, lanes, channels = plane.shape
-    kept = jnp.dot(plane.astype(BF16).reshape(rows * lanes, channels), choice, preferred_element_type=F32)
+    kept = jnp.dot(plane.reshape(rows * lanes, channels), choice, preferred_element_type=F32)
     kept = kept.reshape(rows, lanes, channels)
     before, after = moved_lanes(kept)
     lane = lax.broadcasted_iota(jnp.int32, kept.shape, 2)
@@ -169,7 +177,7 @@
     return plane.reshape(-1, plane.shape[-1]).astype(F32).T.astype(BF16)
 
 
-def weight_kernel(size, which, own, sib, cross, cross_sib, four, four_sib, keep, *refs):
+def weight_kernel(size, which, own, sib, near, near_sib, four, four_sib, keep, *refs):
     sends, wide, turned = refs[:-2], refs[-2], refs[-1]
     index, core = core_of(size)
     channels = own.shape[-1]
@@ -190,8 +198,8 @@
                 narrow(wide, at, plane, choice)
             else:
                 turned[at] = turn(plane)
-    six(5 * core, cross[which].astype(F32) * within(index, size))
-    six(5 * (1 - core), cross_sib[which].astype(F32) * within(jnp.bitwise_xor(index, 1), size))
+    six(5 * core, near[2 + which])
+    six(5 * (1 - core), near_sib[2 + which])
     half = channels // 2
     block = half // 4
     for column in range(3):
@@ -263,53 +271,40 @@
     def wide(count, wide_channels):
         return pltpu.VMEM((count, width + 2, height, wide_channels), BF16)
 
-    slab_type = jax.ShapeDtypeStruct(volume.shape, BF16)
-    sums_type = jax.ShapeDtypeStruct((planes, width * height, channels), F32)
-    filter_type = jax.ShapeDtypeStruct(first_filter.shape, BF16)
-
     def hop(move):
         return pairs(lambda i: i ^ move)
 
+    slab_type = jax.ShapeDtypeStruct(volume.shape, BF16)
+    pair_type = jax.ShapeDtypeStruct((2 * planes, width, height, channels), BF16)
+    sums_type = jax.ShapeDtypeStruct((planes, width * height, channels), F32)
+
     core = lax.rem(lax.axis_index("space"), 2)
-    edge = jnp.where(
-        core == 0,
-        jnp.stack([volume[0], cotangent[0], volume[1]]),
-        jnp.stack([volume[1], cotangent[1], volume[0]]),
+    vol_cross = send_across(volume)
+    cot_cross = send_across(jnp.where(core == 0, cotangent[0], cotangent[1]))
+    vol_sib = send(volume, sibling)
+    cot_sib = send(cotangent, sibling)
+
+    def inner(back, own, weight, name):
+        return call(functools.partial(inner_kernel, back), sums_type, [wide(2, 3 * channels)], name)(own, weight)
+
+    part = inner(False, volume, first_filter, "inner")
+    part_back = inner(True, cotangent, second_filter, "inner_back")
+    vol_cross, cot_cross, part, part_back, vol_sib, cot_sib = lax.optimization_barrier(
+        (vol_cross, cot_cross, part, part_back, vol_sib, cot_sib)
     )
-    edge, late_volume, late_cotangent = lax.optimization_barrier((edge, volume, cotangent))
-    cross = send_across(edge)
-    vol_sib = send(late_volume, sibling)
-    cot_sib = send(late_cotangent, sibling)
-
-    def wide(count, wide_channels):
-        return pltpu.VMEM((count, width + 2, height, wide_channels), BF16)
-
-    slab_type = jax.ShapeDtypeStruct(volume.shape, BF16)
-    sums_type = jax.ShapeDtypeStruct((planes, width * height, channels), F32)
-
-    vol_sib, cot_sib = lax.optimization_barrier((vol_sib, cot_sib))
-    part = call(
-        functools.partial(inner_kernel, size),
-        sums_type,
-        [wide(4, 3 * channels)],
-        "inner",
-    )(volume, vol_sib, first_filter)
-    cross, part = lax.optimization_barrier((cross, part))
-    hidden, act = call(
+    hidden, near = call(
         functools.partial(hidden_kernel, size),
-        (sums_type, slab_type),
-        [wide(1, 3 * channels)],
+        (sums_type, pair_type),
+        [wide(2, 3 * channels)],
         "hidden",
-    )(part, cross, first_filter)
-    act_sib = send(act, sibling)
-    late_cross, hidden = lax.optimization_barrier((cross, hidden))
-    cross_far = send(late_cross, sibling)
+    )(part, vol_sib, vol_cross, cot_cross, first_filter)
+    near_sib = send(near, sibling)
     grad = call(
         functools.partial(hidden_grad_kernel, size),
         slab_type,
-        [wide(4, 3 * channels)],
+        [wide(2, 3 * channels)],
         "hidden_grad",
-    )(hidden, cotangent, cot_sib, cross, second_filter)
+    )(hidden, part_back, cot_sib, cot_cross, second_filter)
     grad_sib = send(grad, sibling)
 
     block_type = jax.ShapeDtypeStruct((27, channels // 8, channels), BF16)
@@ -356,18 +351,18 @@
             )(own, *gots)
         return jnp.transpose(total.reshape(3, 3, 3, share, channels), (3, 0, 1, 2, 4))
 
-    keep_2, gots_2 = filter_grad(1, (cotangent, cot_sib, cross, cross_far, act, act_sib), "second_grad")
+    keep_2, gots_2 = filter_grad(1, (cotangent, cot_sib, near, near_sib, near, near_sib), "second_grad")
     grad_sib, keep_2 = lax.optimization_barrier((grad_sib, keep_2))
-    keep_1, gots_1 = filter_grad(0, (volume, vol_sib, cross, cross_far, grad, grad_sib), "first_grad")
+    keep_1, gots_1 = filter_grad(0, (volume, vol_sib, near, near_sib, grad, grad_sib), "first_grad")
     blocks_2 = near_sum(keep_2, gots_2, "second_near_sum")
     gots_2 = far_hop(blocks_2)
-    late_act, _ = lax.optimization_barrier((act, blocks_2[0]))
+    late_near, _ = lax.optimization_barrier((near, gots_1[0]))
     response = call(
         functools.partial(response_kernel, size),
         slab_type,
         [wide(3, 3 * channels), wide(4, 3 * channels)],
         "response",
-    )(late_act, act_sib, volume, cross, first_filter, second_filter)
+    )(late_near, near_sib, volume, vol_cross, first_filter, second_filter)
     keep_1, response = lax.optimization_barrier((keep_1, response))
     blocks_1 = near_sum(keep_1, gots_1, "first_near_sum")
     gots_1 = far_hop(blocks_1)

time: 34.5 us -> 34.1 us (0.988)
  other arithmetic: 0.04 us -> 0.88 us
  waiting for transfers between devices: 3.96 us -> 3.24 us
  starting transfers between devices: 18.3 us -> 17.9 us
    ppermute x13 -> x12, starting transfers between devices: 15.3 us -> 13.7 us  [send(): return lax.ppermute(array, 'space', moves)]
    ppermute x1 -> x2, starting transfers between devices: 3 us -> 4.12 us  [send_across(): return lax.ppermute(array, ('parts', 'space'), across)]
    slice x1 -> x0, local copies, waits for them, and re-layouts: 1.03 us -> none  [per_device(): cotangent[1]]
    unnamed x10, local copies, waits for them, and re-layouts: 0.93 us -> 1.9 us
    select_n x1, other arithmetic: 0.04 us -> 0.88 us  [per_device(): cot_cross = send_across(jnp.where(core == 0, cotangent[0], cotangent[1]))]
    ppermute x13 -> x12, waiting for transfers between devices: 3.96 us -> 3.23 us  [send(): return lax.ppermute(array, 'space', moves)]
    pallas_call x3 -> x4, Pallas kernels: 2.7 us -> 2.52 us  [the longest x2 1.55 us: inner(): call(functools.partial(inner_kernel, back), sums_type, [wide(2, 3 * chann...]
  transfers between devices with their start and end apart: 14 -> 14, of which waited for: 3 -> 3; matrix products, arithmetic and copies ran while one was open for 0% -> 3% of each run, Pallas kernels for 24% -> 24%
where the time goes in v4:
time: 34.1 us; the launch traced here: 33.8 us
  starting transfers between devices  17.9 us (52%)
  Pallas kernels  9.17 us (27%)
  waiting for transfers between devices  3.24 us (10%)
  local copies, waits for them, and re-layouts  1.9 us (6%)
  other arithmetic  0.88 us (3%)
  between operations  0.73 us (2%)
    ppermute x12, starting transfers between devices, send(): return lax.ppermute(array, 'space', moves)  13.7 us
    ppermute x2, starting transfers between devices, send_across(): return lax.ppermute(array, ('parts', 'space'), across)  4.12 us
    ppermute x12, waiting for transfers between devices, send(): return lax.ppermute(array, 'space', moves)  3.23 us
    pallas_call x2, Pallas kernels, filter_grad(): call(functools.partial(weight_kernel, size, which), (keep_type,) + (block...  2.71 us
    pallas_call x1, Pallas kernels, per_device(): call(functools.partial(response_kernel, size), slab_type, [wide(3, 3 * ch...  2.51 us
    unnamed x10, local copies, waits for them, and re-layouts  1.9 us
    pallas_call x2, Pallas kernels, inner(): call(functools.partial(inner_kernel, back), sums_type, [wide(2, 3 * chann...  1.55 us
    pallas_call x2, Pallas kernels, last_sum(): call(last_sum_kernel, jax.ShapeDtypeStruct(own.shape, F32), [], name)  1.32 us
  transfers between devices with their start and end apart: 14, of which 3 were waited for; matrix products, arithmetic and copies ran while one was open for 3% of the time, Pallas kernels for 24%

profile of v4, /device:TPU:0, one launch (start us, length us, event | category | flops | bytes accessed | tf_op | source)
XLA Modules:
  0.0 33.8 jit_solution(7223550553213472967)
XLA Ops:
  0.6 0.5 %collective-permute-start.2 = (bf16[2,16,16,128]{3,2,1,0:T(8,128)(2,1)}, bf16[2,16,16,128]{3,2,1,0:T(8,128)(2,1)S(1)}, u32[]{:S(2)}, u32[]{:S(2)}) collective-permute-start(bf16[2,16,16,128]{3,2,1,0:T(8,128)(2,1)} %vol.1), channel_id=1, source_target_pairs={{0,1},{1,0},{2,3},{3,2},{4,5},{5,4},{6,7},{7,6},{8,9},{9,8},{10,11... | collective-permute-start | bytes 393224 | tf_op jit(solution)/shard_map/ppermute | solution.py:266
  1.2 2.6 %collective-permute-start = (bf16[2,16,16,128]{3,2,1,0:T(8,128)(2,1)}, bf16[2,16,16,128]{3,2,1,0:T(8,128)(2,1)S(1)}, u32[]{:S(2)}, u32[]{:S(2)}) collective-permute-start(bf16[2,16,16,128]{3,2,1,0:T(8,128)(2,1)} %vol.1), channel_id=1, source_target_pairs={{1,2},{3,4},{5,6},{7,8},{9,10},{11,12},{13,14},{17,18},{19,20},{21... | collective-permute-start | bytes 393224 | tf_op jit(solution)/shard_map/ppermute | solution.py:269
  3.7 0.1 collective-permute-start.3
  3.9 0.9 %select_bitcast_fusion = bf16[16,16,128]{2,1,0:T(8,128)(2,1)S(1)} fusion(bf16[2,16,16,128]{3,2,1,0:T(8,128)(2,1)} %own.6, pred[]{:T(512)S(6)} %eq.3), kind=kLoop, calls=%fused_computation | loop fusion | flops 32768 | bytes 196609 | tf_op jit(solution)/shard_map/jit(_where)/select_n | solution.py:283
  4.7 1.6 %collective-permute-start.1 = (bf16[16,16,128]{2,1,0:T(8,128)(2,1)S(1)}, bf16[16,16,128]{2,1,0:T(8,128)(2,1)S(1)}, u32[]{:S(2)}, u32[]{:S(2)}) collective-permute-start(bf16[16,16,128]{2,1,0:T(8,128)(2,1)S(1)} %select_bitcast_fusion), channel_id=1, source_target_pairs={{1,2},{3,4},{5,6},{7,8},{9,10},{11,12},{13,14},{17,18},{19,20},{21... | collective-permute-start | bytes 196616 | tf_op jit(solution)/shard_map/ppermute | solution.py:269
  6.3 1.2 %copy-done = bf16[3,3,3,128,128]{4,3,2,1,0:T(8,128)(2,1)S(1)} copy-done((bf16[3,3,3,128,128]{4,3,2,1,0:T(8,128)(2,1)S(1)}, bf16[3,3,3,128,128]{4,3,2,1,0:T(8,128)(2,1)}, u32[]{:S(2)}) %copy-start) | copy-done | bytes 884760
  7.5 0.8 %inner.1.part = f32[2,256,128]{2,1,0:T(8,128)S(1)} custom-call(bf16[2,16,16,128]{3,2,1,0:T(8,128)(2,1)S(1)} %copy-done.4, bf16[3,3,3,128,128]{4,3,2,1,0:T(8,128)(2,1)S(1)} %copy-done), custom_call_target="tpu_custom_call" | custom-call | tf_op jit(solution)/shard_map/inner/pallas_call | solution.py:288
  8.3 0.4 %copy-done.2 = bf16[3,3,3,128,128]{4,3,2,1,0:T(8,128)(2,1)S(1)} copy-done((bf16[3,3,3,128,128]{4,3,2,1,0:T(8,128)(2,1)S(1)}, bf16[3,3,3,128,128]{4,3,2,1,0:T(8,128)(2,1)}, u32[]{:S(2)}) %copy-start.2) | copy-done | bytes 884760
  8.6 0.8 %inner_back.1.part = f32[2,256,128]{2,1,0:T(8,128)S(1)} custom-call(bf16[2,16,16,128]{3,2,1,0:T(8,128)(2,1)S(1)} %copy-done.3, bf16[3,3,3,128,128]{4,3,2,1,0:T(8,128)(2,1)S(1)} %copy-done.2), custom_call_target="tpu_custom_call" | custom-call | tf_op jit(solution)/shard_map/inner_back/pallas_call | solution.py:288
  9.5 0.3 copy-done.1
  9.8 0.5 %hidden.1 = (f32[2,256,128]{2,1,0:T(8,128)S(1)}, bf16[4,16,16,128]{3,2,1,0:T(8,128)(2,1)S(1)}) custom-call(f32[2,256,128]{2,1,0:T(8,128)S(1)} %inner.1.part, bf16[2,16,16,128]{3,2,1,0:T(8,128)(2,1)S(1)} %collective-permute-done.2.sib, bf16[2,16,16,128]{3,2,1,0:T(8,128)(2,1)S(1)} %collective-permute-done.cross, ...), custom_call_target="tpu_custom_call" | custom-call | tf_op jit(solution)/shard_map/hidden/pallas_call | solution.py:295
  10.3 0.2 collective-permute-start.4
  10.5 0.5 %hidden_grad.1.four = bf16[2,16,16,128]{3,2,1,0:T(8,128)(2,1)S(1)} custom-call(f32[2,256,128]{2,1,0:T(8,128)S(1)} %get-tuple-element.33.hidden, f32[2,256,128]{2,1,0:T(8,128)S(1)} %inner_back.1.part, bf16[2,16,16,128]{3,2,1,0:T(8,128)(2,1)S(1)} %collective-permute-done.3.sib, bf16[16,16,128]{2,1,0:T(8,128)(2,1)S(1)} %collective-permute-done.1.cot_cross.cross, ...), custom_call_target="tpu_custom_call" | custom-call | tf_op jit(solution)/shard_map/hidden_grad/pallas_call | solution.py:302
  11.0 0.4 %collective-permute-start.5 = (bf16[2,16,16,128]{3,2,1,0:T(8,128)(2,1)S(1)}, bf16[2,16,16,128]{3,2,1,0:T(8,128)(2,1)S(1)}, u32[]{:S(2)}, u32[]{:S(2)}) collective-permute-start(bf16[2,16,16,128]{3,2,1,0:T(8,128)(2,1)S(1)} %hidden_grad.1.four), channel_id=1, source_target_pairs={{0,1},{1,0},{2,3},{3,2},{4,5},{5,4},{6,7},{7,6},{8,9},{9,8},{10,11... | collective-permute-start | bytes 393224 | tf_op jit(solution)/shard_map/ppermute | solution.py:266
  11.4 0.5 %collective-permute-done.4.near_sib.four_sib.sib = bf16[4,16,16,128]{3,2,1,0:T(8,128)(2,1)S(1)} collective-permute-done((bf16[4,16,16,128]{3,2,1,0:T(8,128)(2,1)S(1)}, bf16[4,16,16,128]{3,2,1,0:T(8,128)(2,1)S(1)}, u32[]{:S(2)}, u32[]{:S(2)}) %collective-permute-start.4) | collective-permute-done | bytes 262176 | tf_op jit(solution)/shard_map/ppermute | solution.py:266
  11.9 1.4 %second_grad.1 = (f32[27,16,128]{2,1,0:T(8,128)S(1)}, bf16[27,16,128]{2,1,0:T(8,128)(2,1)S(1)}, bf16[27,16,128]{2,1,0:T(8,128)(2,1)S(1)}, bf16[27,16,128]{2,1,0:T(8,128)(2,1)S(1)}) custom-call(bf16[2,16,16,128]{3,2,1,0:T(8,128)(2,1)S(1)} %copy-done.3, bf16[2,16,16,128]{3,2,1,0:T(8,128)(2,1)S(1)} %collective-permute-done.3.sib, ...), custom_call_target="tpu_custom_call" | custom-call | tf_op jit(solution)/shard_map/second_grad/pallas_call | solution.py:314
  13.3 2.6 %collective-permute-start.10 = (bf16[27,16,128]{2,1,0:T(8,128)(2,1)S(1)}, bf16[27,16,128]{2,1,0:T(8,128)(2,1)S(1)}, u32[]{:S(2)}, u32[]{:S(2)}) collective-permute-start(bf16[27,16,128]{2,1,0:T(8,128)(2,1)S(1)} %get-tuple-element.48), channel_id=1, source_target_pairs={{0,6},{1,7},{2,4},{3,5},{4,2},{5,3},{6,0},{7,1},{8,14},{9,15},{10,... | collective-permute-start | bytes 331784 | tf_op jit(solution)/shard_map/ppermute | solution.py:266
  15.8 0.5 %collective-permute-start.11 = (bf16[27,16,128]{2,1,0:T(8,128)(2,1)S(1)}, bf16[27,16,128]{2,1,0:T(8,128)(2,1)S(1)}, u32[]{:S(2)}, u32[]{:S(2)}) collective-permute-start(bf16[27,16,128]{2,1,0:T(8,128)(2,1)S(1)} %get-tuple-element.49), channel_id=1, source_target_pairs={{0,2},{1,3},{2,0},{3,1},{4,6},{5,7},{6,4},{7,5},{8,10},{9,11},{10,... | collective-permute-start | bytes 331784 | tf_op jit(solution)/shard_map/ppermute | solution.py:266
  16.3 0.5 %collective-permute-start.12 = (bf16[27,16,128]{2,1,0:T(8,128)(2,1)S(1)}, bf16[27,16,128]{2,1,0:T(8,128)(2,1)S(1)}, u32[]{:S(2)}, u32[]{:S(2)}) collective-permute-start(bf16[27,16,128]{2,1,0:T(8,128)(2,1)S(1)} %get-tuple-element.50), channel_id=1, source_target_pairs={{0,4},{1,5},{2,6},{3,7},{4,0},{5,1},{6,2},{7,3},{8,12},{9,13},{10,... | collective-permute-start | bytes 331784 | tf_op jit(solution)/shard_map/ppermute | solution.py:266
  16.8 1.3 %first_grad.1 = (f32[27,16,128]{2,1,0:T(8,128)S(1)}, bf16[27,16,128]{2,1,0:T(8,128)(2,1)S(1)}, bf16[27,16,128]{2,1,0:T(8,128)(2,1)S(1)}, bf16[27,16,128]{2,1,0:T(8,128)(2,1)S(1)}) custom-call(bf16[2,16,16,128]{3,2,1,0:T(8,128)(2,1)S(1)} %copy-done.4, bf16[2,16,16,128]{3,2,1,0:T(8,128)(2,1)S(1)} %collective-permute-done.2.sib, ...), custom_call_target="tpu_custom_call" | custom-call | tf_op jit(solution)/shard_map/first_grad/pallas_call | solution.py:314
  18.2 2.6 %collective-permute-start.6 = (bf16[27,16,128]{2,1,0:T(8,128)(2,1)S(1)}, bf16[27,16,128]{2,1,0:T(8,128)(2,1)S(1)}, u32[]{:S(2)}, u32[]{:S(2)}) collective-permute-start(bf16[27,16,128]{2,1,0:T(8,128)(2,1)S(1)} %get-tuple-element.39), channel_id=1, source_target_pairs={{0,6},{1,7},{2,4},{3,5},{4,2},{5,3},{6,0},{7,1},{8,14},{9,15},{10,... | collective-permute-start | bytes 331784 | tf_op jit(solution)/shard_map/ppermute | solution.py:266
  20.7 0.5 %collective-permute-start.7 = (bf16[27,16,128]{2,1,0:T(8,128)(2,1)S(1)}, bf16[27,16,128]{2,1,0:T(8,128)(2,1)S(1)}, u32[]{:S(2)}, u32[]{:S(2)}) collective-permute-start(bf16[27,16,128]{2,1,0:T(8,128)(2,1)S(1)} %get-tuple-element.43), channel_id=1, source_target_pairs={{0,2},{1,3},{2,0},{3,1},{4,6},{5,7},{6,4},{7,5},{8,10},{9,11},{10,... | collective-permute-start | bytes 331784 | tf_op jit(solution)/shard_map/ppermute | solution.py:266
  21.2 0.5 %collective-permute-start.8 = (bf16[27,16,128]{2,1,0:T(8,128)(2,1)S(1)}, bf16[27,16,128]{2,1,0:T(8,128)(2,1)S(1)}, u32[]{:S(2)}, u32[]{:S(2)}) collective-permute-start(bf16[27,16,128]{2,1,0:T(8,128)(2,1)S(1)} %get-tuple-element.44), channel_id=1, source_target_pairs={{0,4},{1,5},{2,6},{3,7},{4,0},{5,1},{6,2},{7,3},{8,12},{9,13},{10,... | collective-permute-start | bytes 331784 | tf_op jit(solution)/shard_map/ppermute | solution.py:266
  21.7 0.6 %collective-permute-done.11.got_b = bf16[27,16,128]{2,1,0:T(8,128)(2,1)S(1)} collective-permute-done((bf16[27,16,128]{2,1,0:T(8,128)(2,1)S(1)}, bf16[27,16,128]{2,1,0:T(8,128)(2,1)S(1)}, u32[]{:S(2)}, u32[]{:S(2)}) %collective-permute-start.11) | collective-permute-done | bytes 110624 | tf_op jit(solution)/shard_map/ppermute | solution.py:266
  22.4 0.1 second_near_sum.1
  22.4 2.8 %collective-permute-start.13 = (bf16[224,128]{1,0:T(8,128)(2,1)S(1)}, bf16[224,128]{1,0:T(8,128)(2,1)S(1)}, u32[]{:S(2)}, u32[]{:S(2)}) collective-permute-start(bf16[224,128]{1,0:T(8,128)(2,1)S(1)} %get-tuple-element.52), channel_id=1, source_target_pairs={{0,8},{1,9},{2,10},{3,11},{4,12},{5,13},{6,14},{7,15},{8,0},{9,1},... | collective-permute-start | bytes 172040 | tf_op jit(solution)/shard_map/ppermute | solution.py:266
  25.2 2.5 %response.1 = bf16[2,16,16,128]{3,2,1,0:T(8,128)(2,1)} custom-call(bf16[4,16,16,128]{3,2,1,0:T(8,128)(2,1)S(1)} %get-tuple-element.40.near.four.act, bf16[4,16,16,128]{3,2,1,0:T(8,128)(2,1)S(1)} %collective-permute-done.4.near_sib.four_sib.sib, bf16[2,16,16,128]{3,2,1,0:T(8,128)(2,1)S(1)} %copy-done.4, ...), custom_call_target="tpu_custom_call" | custom-call | tf_op jit(solution)/shard_map/response/pallas_call | solution.py:360
  27.8 0.1 first_near_sum.1
  27.8 2.5 %collective-permute-start.9 = (bf16[224,128]{1,0:T(8,128)(2,1)S(1)}, bf16[224,128]{1,0:T(8,128)(2,1)S(1)}, u32[]{:S(2)}, u32[]{:S(2)}) collective-permute-start(bf16[224,128]{1,0:T(8,128)(2,1)S(1)} %get-tuple-element.46), channel_id=1, source_target_pairs={{0,8},{1,9},{2,10},{3,11},{4,12},{5,13},{6,14},{7,15},{8,0},{9,1},... | collective-permute-start | bytes 172040 | tf_op jit(solution)/shard_map/ppermute | solution.py:266
  30.4 0.7 %second_last_sum.1 = f32[216,128]{1,0:T(8,128)} custom-call(f32[216,128]{1,0:T(8,128)S(1)} %get-tuple-element.51.refs_0_, bf16[224,128]{1,0:T(8,128)(2,1)S(1)} %collective-permute-done.13.refs_1_), custom_call_target="tpu_custom_call" | custom-call | tf_op jit(solution)/shard_map/second_last_sum/pallas_call | solution.py:349
  31.0 2.1 %collective-permute-done.9.refs_1_ = bf16[224,128]{1,0:T(8,128)(2,1)S(1)} collective-permute-done((bf16[224,128]{1,0:T(8,128)(2,1)S(1)}, bf16[224,128]{1,0:T(8,128)(2,1)S(1)}, u32[]{:S(2)}, u32[]{:S(2)}) %collective-permute-start.9) | collective-permute-done | bytes 57376 | tf_op jit(solution)/shard_map/ppermute | solution.py:266
  33.1 0.7 %first_last_sum.1 = f32[216,128]{1,0:T(8,128)} custom-call(f32[216,128]{1,0:T(8,128)S(1)} %get-tuple-element.45.refs_0_, bf16[224,128]{1,0:T(8,128)(2,1)S(1)} %collective-permute-done.9.refs_1_), custom_call_target="tpu_custom_call" | custom-call | tf_op jit(solution)/shard_map/first_last_sum/pallas_call | solution.py:349
  (18 shorter events, 0.0 us)
Async XLA Ops:
  0.6 5.7 %copy-start.4 = (bf16[2,16,16,128]{3,2,1,0:T(8,128)(2,1)S(1)}, bf16[2,16,16,128]{3,2,1,0:T(8,128)(2,1)}, u32[]{:S(2)}) copy-start(bf16[2,16,16,128]{3,2,1,0:T(8,128)(2,1)} %vol.1) | copy-start | bytes 393220
  0.6 8.8 %collective-permute-start.2 = (bf16[2,16,16,128]{3,2,1,0:T(8,128)(2,1)}, bf16[2,16,16,128]{3,2,1,0:T(8,128)(2,1)S(1)}, u32[]{:S(2)}, u32[]{:S(2)}) collective-permute-start(bf16[2,16,16,128]{3,2,1,0:T(8,128)(2,1)} %vol.1), channel_id=1, source_target_pairs={{0,1},{1,0},{2,3},{3,2},{4,5},{5,4},{6,7},{7,6},{8,9},{9,8},{10,11... | collective-permute-start | bytes 393224 | tf_op jit(solution)/shard_map/ppermute | solution.py:266
  1.2 8.3 %collective-permute-start = (bf16[2,16,16,128]{3,2,1,0:T(8,128)(2,1)}, bf16[2,16,16,128]{3,2,1,0:T(8,128)(2,1)S(1)}, u32[]{:S(2)}, u32[]{:S(2)}) collective-permute-start(bf16[2,16,16,128]{3,2,1,0:T(8,128)(2,1)} %vol.1), channel_id=1, source_target_pairs={{1,2},{3,4},{5,6},{7,8},{9,10},{11,12},{13,14},{17,18},{19,20},{21... | collective-permute-start | bytes 393224 | tf_op jit(solution)/shard_map/ppermute | solution.py:269
  3.7 5.7 %collective-permute-start.3 = (bf16[2,16,16,128]{3,2,1,0:T(8,128)(2,1)}, bf16[2,16,16,128]{3,2,1,0:T(8,128)(2,1)S(1)}, u32[]{:S(2)}, u32[]{:S(2)}) collective-permute-start(bf16[2,16,16,128]{3,2,1,0:T(8,128)(2,1)} %own.6), channel_id=1, source_target_pairs={{0,1},{1,0},{2,3},{3,2},{4,5},{5,4},{6,7},{7,6},{8,9},{9,8},{10,11... | collective-permute-start | bytes 393224 | tf_op jit(solution)/shard_map/ppermute | solution.py:266
  4.7 4.7 %collective-permute-start.1 = (bf16[16,16,128]{2,1,0:T(8,128)(2,1)S(1)}, bf16[16,16,128]{2,1,0:T(8,128)(2,1)S(1)}, u32[]{:S(2)}, u32[]{:S(2)}) collective-permute-start(bf16[16,16,128]{2,1,0:T(8,128)(2,1)S(1)} %select_bitcast_fusion), channel_id=1, source_target_pairs={{1,2},{3,4},{5,6},{7,8},{9,10},{11,12},{13,14},{17,18},{19,20},{21... | collective-permute-start | bytes 196616 | tf_op jit(solution)/shard_map/ppermute | solution.py:269
  6.3 1.2 %copy-start = (bf16[3,3,3,128,128]{4,3,2,1,0:T(8,128)(2,1)S(1)}, bf16[3,3,3,128,128]{4,3,2,1,0:T(8,128)(2,1)}, u32[]{:S(2)}) copy-start(bf16[3,3,3,128,128]{4,3,2,1,0:T(8,128)(2,1)} %first.3) | copy-start | bytes 2654212
  7.5 1.2 %copy-start.2 = (bf16[3,3,3,128,128]{4,3,2,1,0:T(8,128)(2,1)S(1)}, bf16[3,3,3,128,128]{4,3,2,1,0:T(8,128)(2,1)}, u32[]{:S(2)}) copy-start(bf16[3,3,3,128,128]{4,3,2,1,0:T(8,128)(2,1)} %second.3) | copy-start | bytes 2654212
  7.5 1.2 %copy-start.3 = (bf16[2,16,16,128]{3,2,1,0:T(8,128)(2,1)S(1)}, bf16[2,16,16,128]{3,2,1,0:T(8,128)(2,1)}, u32[]{:S(2)}) copy-start(bf16[2,16,16,128]{3,2,1,0:T(8,128)(2,1)} %own.6) | copy-start | bytes 393220
  8.6 1.2 %copy-start.1 = (bf16[3,3,3,128,128]{4,3,2,1,0:T(8,128)(2,1)S(1)}, bf16[3,3,3,128,128]{4,3,2,1,0:T(8,128)(2,1)}, u32[]{:S(2)}) copy-start(bf16[3,3,3,128,128]{4,3,2,1,0:T(8,128)(2,1)} %first.3) | copy-start | bytes 2654212
  10.3 1.6 %collective-permute-start.4 = (bf16[4,16,16,128]{3,2,1,0:T(8,128)(2,1)S(1)}, bf16[4,16,16,128]{3,2,1,0:T(8,128)(2,1)S(1)}, u32[]{:S(2)}, u32[]{:S(2)}) collective-permute-start(bf16[4,16,16,128]{3,2,1,0:T(8,128)(2,1)S(1)} %get-tuple-element.40.near.four.act), channel_id=1, source_target_pairs={{0,1},{1,0},{2,3},{3,2},{4,5},{5,4},{6,7},{7,6},{8,9},{9,8},{10,11... | collective-permute-start | bytes 786440 | tf_op jit(solution)/shard_map/ppermute | solution.py:266
  11.0 5.8 %collective-permute-start.5 = (bf16[2,16,16,128]{3,2,1,0:T(8,128)(2,1)S(1)}, bf16[2,16,16,128]{3,2,1,0:T(8,128)(2,1)S(1)}, u32[]{:S(2)}, u32[]{:S(2)}) collective-permute-start(bf16[2,16,16,128]{3,2,1,0:T(8,128)(2,1)S(1)} %hidden_grad.1.four), channel_id=1, source_target_pairs={{0,1},{1,0},{2,3},{3,2},{4,5},{5,4},{6,7},{7,6},{8,9},{9,8},{10,11... | collective-permute-start | bytes 393224 | tf_op jit(solution)/shard_map/ppermute | solution.py:266
  13.3 8.0 %collective-permute-start.10 = (bf16[27,16,128]{2,1,0:T(8,128)(2,1)S(1)}, bf16[27,16,128]{2,1,0:T(8,128)(2,1)S(1)}, u32[]{:S(2)}, u32[]{:S(2)}) collective-permute-start(bf16[27,16,128]{2,1,0:T(8,128)(2,1)S(1)} %get-tuple-element.48), channel_id=1, source_target_pairs={{0,6},{1,7},{2,4},{3,5},{4,2},{5,3},{6,0},{7,1},{8,14},{9,15},{10,... | collective-permute-start | bytes 331784 | tf_op jit(solution)/shard_map/ppermute | solution.py:266
  15.8 6.5 %collective-permute-start.11 = (bf16[27,16,128]{2,1,0:T(8,128)(2,1)S(1)}, bf16[27,16,128]{2,1,0:T(8,128)(2,1)S(1)}, u32[]{:S(2)}, u32[]{:S(2)}) collective-permute-start(bf16[27,16,128]{2,1,0:T(8,128)(2,1)S(1)} %get-tuple-element.49), channel_id=1, source_target_pairs={{0,2},{1,3},{2,0},{3,1},{4,6},{5,7},{6,4},{7,5},{8,10},{9,11},{10,... | collective-permute-start | bytes 331784 | tf_op jit(solution)/shard_map/ppermute | solution.py:266
  16.3 6.1 %collective-permute-start.12 = (bf16[27,16,128]{2,1,0:T(8,128)(2,1)S(1)}, bf16[27,16,128]{2,1,0:T(8,128)(2,1)S(1)}, u32[]{:S(2)}, u32[]{:S(2)}) collective-permute-start(bf16[27,16,128]{2,1,0:T(8,128)(2,1)S(1)} %get-tuple-element.50), channel_id=1, source_target_pairs={{0,4},{1,5},{2,6},{3,7},{4,0},{5,1},{6,2},{7,3},{8,12},{9,13},{10,... | collective-permute-start | bytes 331784 | tf_op jit(solution)/shard_map/ppermute | solution.py:266
  18.2 7.1 %collective-permute-start.6 = (bf16[27,16,128]{2,1,0:T(8,128)(2,1)S(1)}, bf16[27,16,128]{2,1,0:T(8,128)(2,1)S(1)}, u32[]{:S(2)}, u32[]{:S(2)}) collective-permute-start(bf16[27,16,128]{2,1,0:T(8,128)(2,1)S(1)} %get-tuple-element.39), channel_id=1, source_target_pairs={{0,6},{1,7},{2,4},{3,5},{4,2},{5,3},{6,0},{7,1},{8,14},{9,15},{10,... | collective-permute-start | bytes 331784 | tf_op jit(solution)/shard_map/ppermute | solution.py:266
  20.7 7.0 %collective-permute-start.7 = (bf16[27,16,128]{2,1,0:T(8,128)(2,1)S(1)}, bf16[27,16,128]{2,1,0:T(8,128)(2,1)S(1)}, u32[]{:S(2)}, u32[]{:S(2)}) collective-permute-start(bf16[27,16,128]{2,1,0:T(8,128)(2,1)S(1)} %get-tuple-element.43), channel_id=1, source_target_pairs={{0,2},{1,3},{2,0},{3,1},{4,6},{5,7},{6,4},{7,5},{8,10},{9,11},{10,... | collective-permute-start | bytes 331784 | tf_op jit(solution)/shard_map/ppermute | solution.py:266
  21.2 6.5 %collective-permute-start.8 = (bf16[27,16,128]{2,1,0:T(8,128)(2,1)S(1)}, bf16[27,16,128]{2,1,0:T(8,128)(2,1)S(1)}, u32[]{:S(2)}, u32[]{:S(2)}) collective-permute-start(bf16[27,16,128]{2,1,0:T(8,128)(2,1)S(1)} %get-tuple-element.44), channel_id=1, source_target_pairs={{0,4},{1,5},{2,6},{3,7},{4,0},{5,1},{6,2},{7,3},{8,12},{9,13},{10,... | collective-permute-start | bytes 331784 | tf_op jit(solution)/shard_map/ppermute | solution.py:266
  22.4 7.9 %collective-permute-start.13 = (bf16[224,128]{1,0:T(8,128)(2,1)S(1)}, bf16[224,128]{1,0:T(8,128)(2,1)S(1)}, u32[]{:S(2)}, u32[]{:S(2)}) collective-permute-start(bf16[224,128]{1,0:T(8,128)(2,1)S(1)} %get-tuple-element.52), channel_id=1, source_target_pairs={{0,8},{1,9},{2,10},{3,11},{4,12},{5,13},{6,14},{7,15},{8,0},{9,1},... | collective-permute-start | bytes 172040 | tf_op jit(solution)/shard_map/ppermute | solution.py:266
  27.8 5.3 %collective-permute-start.9 = (bf16[224,128]{1,0:T(8,128)(2,1)S(1)}, bf16[224,128]{1,0:T(8,128)(2,1)S(1)}, u32[]{:S(2)}, u32[]{:S(2)}) collective-permute-start(bf16[224,128]{1,0:T(8,128)(2,1)S(1)} %get-tuple-element.46), channel_id=1, source_target_pairs={{0,8},{1,9},{2,10},{3,11},{4,12},{5,13},{6,14},{7,15},{8,0},{9,1},... | collective-permute-start | bytes 172040 | tf_op jit(solution)/shard_map/ppermute | solution.py:266

commit v5 on v4

--- a/solution.py
+++ b/solution.py
@@ -108,8 +108,8 @@
         part[plane] = middle[plane * voxels : (plane + 1) * voxels] + side
 
 
-def neighbours(size, back, part, sib, cross, weight, wide):
-    index, core = core_of(size)
+def neighbours(size, core, back, part, sib, cross, weight, wide):
+    index, _ = core_of(size)
     run = backward if back else forward
     edge_rows(wide)
     widen(wide, 0, cross.astype(F32) * within(index, size))
@@ -120,36 +120,33 @@
         yield at, part[at] + side
 
 
-def hidden_kernel(size, part, sib, cross, cot_cross, first, hidden, near, wide):
+def hidden_kernel(size, part, sib, cross, first, hidden, near, border, wide):
     index, core = core_of(size)
-    for at, held in neighbours(size, False, part, sib, cross[1 - core], first, wide):
+    for at, held in neighbours(size, core, False, part, sib, cross[0], first, wide):
         hidden[at] = held
-        near[at] = (held * jax.nn.sigmoid(held)).astype(BF16).reshape(near.shape[1:])
-    for i, plane in enumerate((cross[1 - core], cot_cross[...])):
-        near[2 + i] = (plane.astype(F32) * within(index, size)).astype(BF16)
+        act = (held * jax.nn.sigmoid(held)).astype(BF16).reshape(near.shape[1:])
+        near[at] = act
+        if at is core:
+            border[...] = act
+    for i in range(2):
+        near[2 + i] = (cross[i].astype(F32) * within(index, size)).astype(BF16)
 
 
 def hidden_grad_kernel(size, hidden, part, sib, cross, second, out, wide):
-    for at, act_grad in neighbours(size, True, part, sib, cross[...], second, wide):
+    for at, act_grad in neighbours(size, core_of(size)[1], True, part, sib, cross[1], second, wide):
         held = hidden[at]
         sigma = jax.nn.sigmoid(held)
         grad = act_grad * sigma * (1.0 + held * (1.0 - sigma))
         out[at] = grad.astype(BF16).reshape(out.shape[1:])
 
 
-def response_kernel(size, act, sib, vol, cross, first, second, out, vol_wide, wide):
+def response_kernel(size, near, near_sib, cross, second, out, wide):
     index, core = core_of(size)
-    edge_rows(vol_wide)
-    widen(vol_wide, 1, act[2])
-    widen(vol_wide, 2 * core, cross[core])
-    widen(vol_wide, 2 * (1 - core), vol[core])
-    hidden = convolve(vol_wide, first, 1)
-    outer = hidden * jax.nn.sigmoid(hidden) * within(index, size)
     edge_rows(wide)
-    widen(wide, 1, act[0])
-    widen(wide, 2, act[1])
-    widen(wide, 3 * core, outer.reshape(out.shape[1:]).astype(BF16))
-    widen(wide, 3 * (1 - core), sib[core])
+    widen(wide, 1, near[0])
+    widen(wide, 2, near[1])
+    widen(wide, 3 * core, cross[...].astype(F32) * within(index, size))
+    widen(wide, 3 * (1 - core), near_sib[core])
     out[...] = convolve(wide, second, 2).astype(BF16).reshape(out.shape)
 
 
@@ -174,7 +171,7 @@
 
 
 def turn(plane):
-    return plane.reshape(-1, plane.shape[-1]).astype(F32).T.astype(BF16)
+    return plane.reshape(-1, plane.shape[-1]).T
 
 
 def weight_kernel(size, which, own, sib, near, near_sib, four, four_sib, keep, *refs):
@@ -271,40 +268,45 @@
     def wide(count, wide_channels):
         return pltpu.VMEM((count, width + 2, height, wide_channels), BF16)
 
+    slab_type = jax.ShapeDtypeStruct(volume.shape, BF16)
+    sums_type = jax.ShapeDtypeStruct((planes, width * height, channels), F32)
+    pair_type = jax.ShapeDtypeStruct((2 * planes, width, height, channels), BF16)
+
     def hop(move):
         return pairs(lambda i: i ^ move)
 
-    slab_type = jax.ShapeDtypeStruct(volume.shape, BF16)
-    pair_type = jax.ShapeDtypeStruct((2 * planes, width, height, channels), BF16)
-    sums_type = jax.ShapeDtypeStruct((planes, width * height, channels), F32)
-
     core = lax.rem(lax.axis_index("space"), 2)
-    vol_cross = send_across(volume)
-    cot_cross = send_across(jnp.where(core == 0, cotangent[0], cotangent[1]))
-    vol_sib = send(volume, sibling)
-    cot_sib = send(cotangent, sibling)
+    edge = jnp.where(
+        core == 0,
+        jnp.stack([volume[0], cotangent[0]]),
+        jnp.stack([volume[1], cotangent[1]]),
+    )
+    edge, late_volume, late_cotangent = lax.optimization_barrier((edge, volume, cotangent))
+    cross = send_across(edge)
+    vol_sib = send(late_volume, sibling)
+    cot_sib = send(late_cotangent, sibling)
 
     def inner(back, own, weight, name):
         return call(functools.partial(inner_kernel, back), sums_type, [wide(2, 3 * channels)], name)(own, weight)
 
     part = inner(False, volume, first_filter, "inner")
     part_back = inner(True, cotangent, second_filter, "inner_back")
-    vol_cross, cot_cross, part, part_back, vol_sib, cot_sib = lax.optimization_barrier(
-        (vol_cross, cot_cross, part, part_back, vol_sib, cot_sib)
+    cross, part, part_back, vol_sib, cot_sib = lax.optimization_barrier(
+        (cross, part, part_back, vol_sib, cot_sib)
     )
-    hidden, near = call(
+    hidden, near, border = call(
         functools.partial(hidden_kernel, size),
-        (sums_type, pair_type),
+        (sums_type, pair_type, jax.ShapeDtypeStruct(volume.shape[1:], BF16)),
         [wide(2, 3 * channels)],
         "hidden",
-    )(part, vol_sib, vol_cross, cot_cross, first_filter)
+    )(part, vol_sib, cross, first_filter)
     near_sib = send(near, sibling)
     grad = call(
         functools.partial(hidden_grad_kernel, size),
         slab_type,
         [wide(2, 3 * channels)],
         "hidden_grad",
-    )(hidden, part_back, cot_sib, cot_cross, second_filter)
+    )(hidden, part_back, cot_sib, cross, second_filter)
     grad_sib = send(grad, sibling)
 
     block_type = jax.ShapeDtypeStruct((27, channels // 8, channels), BF16)
@@ -320,7 +322,10 @@
             ],
             name,
         )(*operands)
-        return keep, [send(blocks[d - 1], hop(2 * d)) for d in (3, 1, 2)]
+        return keep, blocks
+
+    def near_hop(blocks):
+        return [send(blocks[d - 1], hop(2 * d)) for d in (3, 1, 2)]
 
     def near_sum(keep, gots, name):
         if share % 8:
@@ -351,23 +356,28 @@
             )(own, *gots)
         return jnp.transpose(total.reshape(3, 3, 3, share, channels), (3, 0, 1, 2, 4))
 
-    keep_2, gots_2 = filter_grad(1, (cotangent, cot_sib, near, near_sib, near, near_sib), "second_grad")
+    keep_2, blocks_2 = filter_grad(1, (cotangent, cot_sib, near, near_sib, near, near_sib), "second_grad")
     grad_sib, keep_2 = lax.optimization_barrier((grad_sib, keep_2))
-    keep_1, gots_1 = filter_grad(0, (volume, vol_sib, near, near_sib, grad, grad_sib), "first_grad")
+    gots_2 = near_hop(blocks_2)
+    keep_1, blocks_1 = filter_grad(0, (volume, vol_sib, near, near_sib, grad, grad_sib), "first_grad")
+    gots_1 = near_hop(blocks_1)
     blocks_2 = near_sum(keep_2, gots_2, "second_near_sum")
     gots_2 = far_hop(blocks_2)
-    late_near, _ = lax.optimization_barrier((near, gots_1[0]))
+    border, _ = lax.optimization_barrier((border, blocks_2[0]))
+    act_cross = send_across(border)
+    keep_1, _ = lax.optimization_barrier((keep_1, blocks_2[0]))
+    blocks_1 = near_sum(keep_1, gots_1, "first_near_sum")
+    gots_1 = far_hop(blocks_1)
+    act_cross, _ = lax.optimization_barrier((act_cross, blocks_1[0]))
     response = call(
         functools.partial(response_kernel, size),
         slab_type,
-        [wide(3, 3 * channels), wide(4, 3 * channels)],
+        [wide(4, 3 * channels)],
         "response",
-    )(late_near, near_sib, volume, vol_cross, first_filter, second_filter)
-    keep_1, response = lax.optimization_barrier((keep_1, response))
-    blocks_1 = near_sum(keep_1, gots_1, "first_near_sum")
-    gots_1 = far_hop(blocks_1)
+    )(near, near_sib, act_cross, second_filter)
+    first_own, response = lax.optimization_barrier((blocks_1[0], response))
     second_grad = last_sum(blocks_2[0], gots_2, "second_last_sum")
-    first_grad = last_sum(blocks_1[0], gots_1, "first_last_sum")
+    first_grad = last_sum(first_own, gots_1, "first_last_sum")
     return response, first_grad, second_grad
 
 

time: 34.1 us -> 32.9 us (0.965)
  other arithmetic: 0.88 us -> 0.03 us
  Pallas kernels: 9.17 us -> 8.5 us
  waiting for transfers between devices: 3.24 us -> 3.68 us
    slice x0 -> x1, local copies, waits for them, and re-layouts: none -> 1.03 us  [per_device(): volume[1]]
    unnamed x10, local copies, waits for them, and re-layouts: 1.9 us -> 0.93 us
    select_n x1, other arithmetic: 0.88 us -> 0.03 us  [per_device(): jnp.where(core == 0, jnp.stack([volume[0], cotangent[0]]), jnp.stack([vol...]
    pallas_call x2, Pallas kernels: 2.98 us -> 2.37 us  [the longest x1 1.88 us: per_device(): call(functools.partial(response_kernel, size), slab_type, [wide(4, 3 * ch...]
    ppermute x12, starting transfers between devices: 13.7 us -> 13.3 us  [send(): return lax.ppermute(array, 'space', moves)]
    ppermute x2, starting transfers between devices: 4.12 us -> 4.57 us  [send_across(): return lax.ppermute(array, ('parts', 'space'), across)]
    ppermute x12, waiting for transfers between devices: 3.23 us -> 3.67 us  [send(): return lax.ppermute(array, 'space', moves)]
  transfers between devices with their start and end apart: 14 -> 14, of which waited for: 3 -> 8; matrix products, arithmetic and copies ran while one was open for 3% -> 0% of each run, Pallas kernels for 24% -> 22%
where the time goes in v5:
time: 32.9 us; the launch traced here: 32.8 us
  starting transfers between devices  17.8 us (54%)
  Pallas kernels  8.5 us (26%)
  waiting for transfers between devices  3.68 us (11%)
  local copies, waits for them, and re-layouts  1.96 us (6%)
  between operations  0.78 us (2%)
    ppermute x12, starting transfers between devices, send(): return lax.ppermute(array, 'space', moves)  13.3 us
    ppermute x2, starting transfers between devices, send_across(): return lax.ppermute(array, ('parts', 'space'), across)  4.57 us
    ppermute x12, waiting for transfers between devices, send(): return lax.ppermute(array, 'space', moves)  3.67 us
    pallas_call x2, Pallas kernels, filter_grad(): call(functools.partial(weight_kernel, size, which), (keep_type,) + (block...  2.64 us
    pallas_call x1, Pallas kernels, per_device(): call(functools.partial(response_kernel, size), slab_type, [wide(4, 3 * ch...  1.88 us
    pallas_call x2, Pallas kernels, inner(): call(functools.partial(inner_kernel, back), sums_type, [wide(2, 3 * chann...  1.55 us
    pallas_call x2, Pallas kernels, last_sum(): call(last_sum_kernel, jax.ShapeDtypeStruct(own.shape, F32), [], name)  1.32 us
    slice x1, local copies, waits for them, and re-layouts, per_device(): volume[1]  1.03 us
  transfers between devices with their start and end apart: 14, of which 8 were waited for; matrix products, arithmetic and copies ran while one was open for 0% of the time, Pallas kernels for 22%

profile of v5, /device:TPU:0, one launch (start us, length us, event | category | flops | bytes accessed | tf_op | source)
XLA Modules:
  0.0 32.8 jit_solution(2925432281375943610)
XLA Ops:
  0.6 1.0 %fusion = (bf16[1,16,16,128]{3,2,1,0:T(8,128)(2,1)S(1)}, bf16[1,16,16,128]{3,2,1,0:T(8,128)(2,1)S(1)}, bf16[1,16,16,128]{3,2,1,0:T(8,128)(2,1)S(1)}, bf16[1,16,16,128]{3,2,1,0:T(8,128)(2,1)S(1)}) fusion(bf16[2,16,16,128]{3,2,1,0:T(8,128)(2,1)} %own.7, bf16[2,16,16,128]{3,2,1,0:T(8,128)(2,1)} %own.6), kind=kLoop, calls=%fused_computation.1 | loop fusion | bytes 524288 | tf_op jit(solution)/shard_map/slice | solution.py:282
  1.7 3.0 %collective-permute-start = (bf16[2,16,16,128]{3,2,1,0:T(8,128)(2,1)S(1)}, bf16[2,16,16,128]{3,2,1,0:T(8,128)(2,1)S(1)}, u32[]{:S(2)}, u32[]{:S(2)}) collective-permute-start(bf16[2,16,16,128]{3,2,1,0:T(8,128)(2,1)S(1)} %maximum_select_fusion), channel_id=1, source_target_pairs={{1,2},{3,4},{5,6},{7,8},{9,10},{11,12},{13,14},{17,18},{19,20},{21... | collective-permute-start | bytes 393224 | tf_op jit(solution)/shard_map/ppermute | solution.py:266
  4.7 0.1 collective-permute-start.1
  4.9 0.4 %collective-permute-start.2 = (bf16[2,16,16,128]{3,2,1,0:T(8,128)(2,1)}, bf16[2,16,16,128]{3,2,1,0:T(8,128)(2,1)S(1)}, u32[]{:S(2)}, u32[]{:S(2)}) collective-permute-start(bf16[2,16,16,128]{3,2,1,0:T(8,128)(2,1)} %own.6), channel_id=1, source_target_pairs={{0,1},{1,0},{2,3},{3,2},{4,5},{5,4},{6,7},{7,6},{8,9},{9,8},{10,11... | collective-permute-start | bytes 393224 | tf_op jit(solution)/shard_map/ppermute | solution.py:263
  5.3 0.9 %copy-done.3 = bf16[2,16,16,128]{3,2,1,0:T(8,128)(2,1)S(1)} copy-done((bf16[2,16,16,128]{3,2,1,0:T(8,128)(2,1)S(1)}, bf16[2,16,16,128]{3,2,1,0:T(8,128)(2,1)}, u32[]{:S(2)}) %copy-start.3) | copy-done | bytes 131096
  6.2 0.8 %inner.1.part = f32[2,256,128]{2,1,0:T(8,128)S(1)} custom-call(bf16[2,16,16,128]{3,2,1,0:T(8,128)(2,1)S(1)} %copy-done.3, bf16[3,3,3,128,128]{4,3,2,1,0:T(8,128)(2,1)S(1)} %copy-done.1), custom_call_target="tpu_custom_call" | custom-call | tf_op jit(solution)/shard_map/inner/pallas_call | solution.py:290
  7.0 0.8 %inner_back.1.part = f32[2,256,128]{2,1,0:T(8,128)S(1)} custom-call(bf16[2,16,16,128]{3,2,1,0:T(8,128)(2,1)S(1)} %copy-done.2, bf16[3,3,3,128,128]{4,3,2,1,0:T(8,128)(2,1)S(1)} %copy-done), custom_call_target="tpu_custom_call" | custom-call | tf_op jit(solution)/shard_map/inner_back/pallas_call | solution.py:290
  7.8 0.5 %hidden.1 = (f32[2,256,128]{2,1,0:T(8,128)S(1)}, bf16[4,16,16,128]{3,2,1,0:T(8,128)(2,1)S(1)}, bf16[16,16,128]{2,1,0:T(8,128)(2,1)S(1)}) custom-call(f32[2,256,128]{2,1,0:T(8,128)S(1)} %inner.1.part, bf16[2,16,16,128]{3,2,1,0:T(8,128)(2,1)S(1)} %collective-permute-done.1.sib, bf16[2,16,16,128]{3,2,1,0:T(8,128)(2,1)S(1)} %collective-permute-done.cross, ...), custom_call_target="tpu_custom_call" | custom-call | tf_op jit(solution)/shard_map/hidden/pallas_call | solution.py:297
  8.3 0.5 %collective-permute-start.3 = (bf16[4,16,16,128]{3,2,1,0:T(8,128)(2,1)S(1)}, bf16[4,16,16,128]{3,2,1,0:T(8,128)(2,1)S(1)}, u32[]{:S(2)}, u32[]{:S(2)}) collective-permute-start(bf16[4,16,16,128]{3,2,1,0:T(8,128)(2,1)S(1)} %get-tuple-element.39.near.four), channel_id=1, source_target_pairs={{0,1},{1,0},{2,3},{3,2},{4,5},{5,4},{6,7},{7,6},{8,9},{9,8},{10,11... | collective-permute-start | bytes 786440 | tf_op jit(solution)/shard_map/ppermute | solution.py:263
  8.8 0.5 %hidden_grad.1.four = bf16[2,16,16,128]{3,2,1,0:T(8,128)(2,1)S(1)} custom-call(f32[2,256,128]{2,1,0:T(8,128)S(1)} %get-tuple-element.40.hidden, f32[2,256,128]{2,1,0:T(8,128)S(1)} %inner_back.1.part, bf16[2,16,16,128]{3,2,1,0:T(8,128)(2,1)S(1)} %collective-permute-done.2.sib, bf16[2,16,16,128]{3,2,1,0:T(8,128)(2,1)S(1)} %collective-permute-done.cross, ...), custom_call_target="tpu_custom_call" | custom-call | tf_op jit(solution)/shard_map/hidden_grad/pallas_call | solution.py:304
  9.3 0.2 collective-permute-start.4
  9.4 0.5 %collective-permute-done.3.near_sib.four_sib = bf16[4,16,16,128]{3,2,1,0:T(8,128)(2,1)S(1)} collective-permute-done((bf16[4,16,16,128]{3,2,1,0:T(8,128)(2,1)S(1)}, bf16[4,16,16,128]{3,2,1,0:T(8,128)(2,1)S(1)}, u32[]{:S(2)}, u32[]{:S(2)}) %collective-permute-start.3) | collective-permute-done | bytes 262176 | tf_op jit(solution)/shard_map/ppermute | solution.py:263
  9.9 1.3 %second_grad.1 = (f32[27,16,128]{2,1,0:T(8,128)S(1)}, bf16[27,16,128]{2,1,0:T(8,128)(2,1)S(1)}, bf16[27,16,128]{2,1,0:T(8,128)(2,1)S(1)}, bf16[27,16,128]{2,1,0:T(8,128)(2,1)S(1)}) custom-call(bf16[2,16,16,128]{3,2,1,0:T(8,128)(2,1)S(1)} %copy-done.2, bf16[2,16,16,128]{3,2,1,0:T(8,128)(2,1)S(1)} %collective-permute-done.2.sib, ...), custom_call_target="tpu_custom_call" | custom-call | tf_op jit(solution)/shard_map/second_grad/pallas_call | solution.py:316
  11.3 3.8 %collective-permute-start.5 = (bf16[27,16,128]{2,1,0:T(8,128)(2,1)S(1)}, bf16[27,16,128]{2,1,0:T(8,128)(2,1)S(1)}, u32[]{:S(2)}, u32[]{:S(2)}) collective-permute-start(bf16[27,16,128]{2,1,0:T(8,128)(2,1)S(1)} %get-tuple-element.47), channel_id=1, source_target_pairs={{0,6},{1,7},{2,4},{3,5},{4,2},{5,3},{6,0},{7,1},{8,14},{9,15},{10,... | collective-permute-start | bytes 331784 | tf_op jit(solution)/shard_map/ppermute | solution.py:263
  15.1 0.1 collective-permute-start.6
  15.2 0.5 %collective-permute-start.7 = (bf16[27,16,128]{2,1,0:T(8,128)(2,1)S(1)}, bf16[27,16,128]{2,1,0:T(8,128)(2,1)S(1)}, u32[]{:S(2)}, u32[]{:S(2)}) collective-permute-start(bf16[27,16,128]{2,1,0:T(8,128)(2,1)S(1)} %get-tuple-element.49), channel_id=1, source_target_pairs={{0,4},{1,5},{2,6},{3,7},{4,0},{5,1},{6,2},{7,3},{8,12},{9,13},{10,... | collective-permute-start | bytes 331784 | tf_op jit(solution)/shard_map/ppermute | solution.py:263
  15.7 1.3 %first_grad.1 = (f32[27,16,128]{2,1,0:T(8,128)S(1)}, bf16[27,16,128]{2,1,0:T(8,128)(2,1)S(1)}, bf16[27,16,128]{2,1,0:T(8,128)(2,1)S(1)}, bf16[27,16,128]{2,1,0:T(8,128)(2,1)S(1)}) custom-call(bf16[2,16,16,128]{3,2,1,0:T(8,128)(2,1)S(1)} %copy-done.4, bf16[2,16,16,128]{3,2,1,0:T(8,128)(2,1)S(1)} %collective-permute-done.1.sib, ...), custom_call_target="tpu_custom_call" | custom-call | tf_op jit(solution)/shard_map/first_grad/pallas_call | solution.py:316
  17.1 2.9 %collective-permute-start.8 = (bf16[27,16,128]{2,1,0:T(8,128)(2,1)S(1)}, bf16[27,16,128]{2,1,0:T(8,128)(2,1)S(1)}, u32[]{:S(2)}, u32[]{:S(2)}) collective-permute-start(bf16[27,16,128]{2,1,0:T(8,128)(2,1)S(1)} %get-tuple-element.52), channel_id=1, source_target_pairs={{0,6},{1,7},{2,4},{3,5},{4,2},{5,3},{6,0},{7,1},{8,14},{9,15},{10,... | collective-permute-start | bytes 331784 | tf_op jit(solution)/shard_map/ppermute | solution.py:263
  20.0 0.1 collective-permute-start.9
  20.1 0.5 %collective-permute-start.10 = (bf16[27,16,128]{2,1,0:T(8,128)(2,1)S(1)}, bf16[27,16,128]{2,1,0:T(8,128)(2,1)S(1)}, u32[]{:S(2)}, u32[]{:S(2)}) collective-permute-start(bf16[27,16,128]{2,1,0:T(8,128)(2,1)S(1)} %get-tuple-element.54), channel_id=1, source_target_pairs={{0,4},{1,5},{2,6},{3,7},{4,0},{5,1},{6,2},{7,3},{8,12},{9,13},{10,... | collective-permute-start | bytes 331784 | tf_op jit(solution)/shard_map/ppermute | solution.py:263
  20.6 0.8 %collective-permute-done.6.got_b = bf16[27,16,128]{2,1,0:T(8,128)(2,1)S(1)} collective-permute-done((bf16[27,16,128]{2,1,0:T(8,128)(2,1)S(1)}, bf16[27,16,128]{2,1,0:T(8,128)(2,1)S(1)}, u32[]{:S(2)}, u32[]{:S(2)}) %collective-permute-start.6) | collective-permute-done | bytes 110624 | tf_op jit(solution)/shard_map/ppermute | solution.py:263
  21.4 0.2 collective-permute-done.7.got_c
  21.6 1.6 %collective-permute-start.11 = (bf16[16,16,128]{2,1,0:T(8,128)(2,1)S(1)}, bf16[16,16,128]{2,1,0:T(8,128)(2,1)S(1)}, u32[]{:S(2)}, u32[]{:S(2)}) collective-permute-start(bf16[16,16,128]{2,1,0:T(8,128)(2,1)S(1)} %get-tuple-element.57), channel_id=1, source_target_pairs={{1,2},{3,4},{5,6},{7,8},{9,10},{11,12},{13,14},{17,18},{19,20},{21... | collective-permute-start | bytes 196616 | tf_op jit(solution)/shard_map/ppermute | solution.py:266
  23.2 1.2 %collective-permute-start.13 = (bf16[224,128]{1,0:T(8,128)(2,1)S(1)}, bf16[224,128]{1,0:T(8,128)(2,1)S(1)}, u32[]{:S(2)}, u32[]{:S(2)}) collective-permute-start(bf16[224,128]{1,0:T(8,128)(2,1)S(1)} %get-tuple-element.62), channel_id=1, source_target_pairs={{0,8},{1,9},{2,10},{3,11},{4,12},{5,13},{6,14},{7,15},{8,0},{9,1},... | collective-permute-start | bytes 172040 | tf_op jit(solution)/shard_map/ppermute | solution.py:263
  24.4 0.1 collective-permute-done.8.got_a
  24.5 1.1 %collective-permute-done.9.got_b = bf16[27,16,128]{2,1,0:T(8,128)(2,1)S(1)} collective-permute-done((bf16[27,16,128]{2,1,0:T(8,128)(2,1)S(1)}, bf16[27,16,128]{2,1,0:T(8,128)(2,1)S(1)}, u32[]{:S(2)}, u32[]{:S(2)}) %collective-permute-start.9) | collective-permute-done | bytes 110624 | tf_op jit(solution)/shard_map/ppermute | solution.py:263
  25.8 2.9 %collective-permute-start.12 = (bf16[224,128]{1,0:T(8,128)(2,1)S(1)}, bf16[224,128]{1,0:T(8,128)(2,1)S(1)}, u32[]{:S(2)}, u32[]{:S(2)}) collective-permute-start(bf16[224,128]{1,0:T(8,128)(2,1)S(1)} %get-tuple-element.61), channel_id=1, source_target_pairs={{0,8},{1,9},{2,10},{3,11},{4,12},{5,13},{6,14},{7,15},{8,0},{9,1},... | collective-permute-start | bytes 172040 | tf_op jit(solution)/shard_map/ppermute | solution.py:263
  28.7 0.1 collective-permute-done.13.refs_1_
  28.8 0.7 %second_last_sum.1 = f32[216,128]{1,0:T(8,128)} custom-call(f32[216,128]{1,0:T(8,128)S(1)} %get-tuple-element.50.refs_0_, bf16[224,128]{1,0:T(8,128)(2,1)S(1)} %collective-permute-done.13.refs_1_), custom_call_target="tpu_custom_call" | custom-call | tf_op jit(solution)/shard_map/second_last_sum/pallas_call | solution.py:354
  29.5 1.9 %response.1 = bf16[2,16,16,128]{3,2,1,0:T(8,128)(2,1)} custom-call(bf16[4,16,16,128]{3,2,1,0:T(8,128)(2,1)S(1)} %get-tuple-element.39.near.four, bf16[4,16,16,128]{3,2,1,0:T(8,128)(2,1)S(1)} %collective-permute-done.3.near_sib.four_sib, bf16[16,16,128]{2,1,0:T(8,128)(2,1)S(1)} %collective-permute-done.11.cross, bf16[3,3,3,128,128]{4,3,2,1,0:T(8,128)(2,1)S(1)} %copy-done), custom_call_target="tpu_custom_call" | custom-call | tf_op jit(solution)/shard_map/response/pallas_call | solution.py:372
  31.3 0.8 %collective-permute-done.12.refs_1_ = bf16[224,128]{1,0:T(8,128)(2,1)S(1)} collective-permute-done((bf16[224,128]{1,0:T(8,128)(2,1)S(1)}, bf16[224,128]{1,0:T(8,128)(2,1)S(1)}, u32[]{:S(2)}, u32[]{:S(2)}) %collective-permute-start.12) | collective-permute-done | bytes 57376 | tf_op jit(solution)/shard_map/ppermute | solution.py:263
  32.1 0.7 %first_last_sum.1 = f32[216,128]{1,0:T(8,128)} custom-call(f32[216,128]{1,0:T(8,128)S(1)} %get-tuple-element.60.refs_0_, bf16[224,128]{1,0:T(8,128)(2,1)S(1)} %collective-permute-done.12.refs_1_), custom_call_target="tpu_custom_call" | custom-call | tf_op jit(solution)/shard_map/first_last_sum/pallas_call | solution.py:354
  (19 shorter events, 0.3 us)
Async XLA Ops:
  0.6 4.6 %copy-start.1 = (bf16[3,3,3,128,128]{4,3,2,1,0:T(8,128)(2,1)S(1)}, bf16[3,3,3,128,128]{4,3,2,1,0:T(8,128)(2,1)}, u32[]{:S(2)}) copy-start(bf16[3,3,3,128,128]{4,3,2,1,0:T(8,128)(2,1)} %first.1) | copy-start | bytes 2654212
  1.7 5.3 %copy-start = (bf16[3,3,3,128,128]{4,3,2,1,0:T(8,128)(2,1)S(1)}, bf16[3,3,3,128,128]{4,3,2,1,0:T(8,128)(2,1)}, u32[]{:S(2)}) copy-start(bf16[3,3,3,128,128]{4,3,2,1,0:T(8,128)(2,1)} %second.3) | copy-start | bytes 2654212
  1.7 5.2 %copy-start.2 = (bf16[2,16,16,128]{3,2,1,0:T(8,128)(2,1)S(1)}, bf16[2,16,16,128]{3,2,1,0:T(8,128)(2,1)}, u32[]{:S(2)}) copy-start(bf16[2,16,16,128]{3,2,1,0:T(8,128)(2,1)} %own.6) | copy-start | bytes 393220
  1.7 6.0 %collective-permute-start = (bf16[2,16,16,128]{3,2,1,0:T(8,128)(2,1)S(1)}, bf16[2,16,16,128]{3,2,1,0:T(8,128)(2,1)S(1)}, u32[]{:S(2)}, u32[]{:S(2)}) collective-permute-start(bf16[2,16,16,128]{3,2,1,0:T(8,128)(2,1)S(1)} %maximum_select_fusion), channel_id=1, source_target_pairs={{1,2},{3,4},{5,6},{7,8},{9,10},{11,12},{13,14},{17,18},{19,20},{21... | collective-permute-start | bytes 393224 | tf_op jit(solution)/shard_map/ppermute | solution.py:266
  4.7 3.0 %collective-permute-start.1 = (bf16[2,16,16,128]{3,2,1,0:T(8,128)(2,1)}, bf16[2,16,16,128]{3,2,1,0:T(8,128)(2,1)S(1)}, u32[]{:S(2)}, u32[]{:S(2)}) collective-permute-start(bf16[2,16,16,128]{3,2,1,0:T(8,128)(2,1)} %own.7), channel_id=1, source_target_pairs={{0,1},{1,0},{2,3},{3,2},{4,5},{5,4},{6,7},{7,6},{8,9},{9,8},{10,11... | collective-permute-start | bytes 393224 | tf_op jit(solution)/shard_map/ppermute | solution.py:263
  4.9 2.9 %collective-permute-start.2 = (bf16[2,16,16,128]{3,2,1,0:T(8,128)(2,1)}, bf16[2,16,16,128]{3,2,1,0:T(8,128)(2,1)S(1)}, u32[]{:S(2)}, u32[]{:S(2)}) collective-permute-start(bf16[2,16,16,128]{3,2,1,0:T(8,128)(2,1)} %own.6), channel_id=1, source_target_pairs={{0,1},{1,0},{2,3},{3,2},{4,5},{5,4},{6,7},{7,6},{8,9},{9,8},{10,11... | collective-permute-start | bytes 393224 | tf_op jit(solution)/shard_map/ppermute | solution.py:263
  5.3 0.9 %copy-start.3 = (bf16[2,16,16,128]{3,2,1,0:T(8,128)(2,1)S(1)}, bf16[2,16,16,128]{3,2,1,0:T(8,128)(2,1)}, u32[]{:S(2)}) copy-start(bf16[2,16,16,128]{3,2,1,0:T(8,128)(2,1)} %own.7) | copy-start | bytes 393220
  8.3 1.7 %collective-permute-start.3 = (bf16[4,16,16,128]{3,2,1,0:T(8,128)(2,1)S(1)}, bf16[4,16,16,128]{3,2,1,0:T(8,128)(2,1)S(1)}, u32[]{:S(2)}, u32[]{:S(2)}) collective-permute-start(bf16[4,16,16,128]{3,2,1,0:T(8,128)(2,1)S(1)} %get-tuple-element.39.near.four), channel_id=1, source_target_pairs={{0,1},{1,0},{2,3},{3,2},{4,5},{5,4},{6,7},{7,6},{8,9},{9,8},{10,11... | collective-permute-start | bytes 786440 | tf_op jit(solution)/shard_map/ppermute | solution.py:263
  9.3 6.5 %copy-start.4 = (bf16[2,16,16,128]{3,2,1,0:T(8,128)(2,1)S(1)}, bf16[2,16,16,128]{3,2,1,0:T(8,128)(2,1)}, u32[]{:S(2)}) copy-start(bf16[2,16,16,128]{3,2,1,0:T(8,128)(2,1)} %own.7) | copy-start | bytes 393220
  9.3 6.4 %collective-permute-start.4 = (bf16[2,16,16,128]{3,2,1,0:T(8,128)(2,1)S(1)}, bf16[2,16,16,128]{3,2,1,0:T(8,128)(2,1)S(1)}, u32[]{:S(2)}, u32[]{:S(2)}) collective-permute-start(bf16[2,16,16,128]{3,2,1,0:T(8,128)(2,1)S(1)} %hidden_grad.1.four), channel_id=1, source_target_pairs={{0,1},{1,0},{2,3},{3,2},{4,5},{5,4},{6,7},{7,6},{8,9},{9,8},{10,11... | collective-permute-start | bytes 393224 | tf_op jit(solution)/shard_map/ppermute | solution.py:263
  11.3 8.8 %collective-permute-start.5 = (bf16[27,16,128]{2,1,0:T(8,128)(2,1)S(1)}, bf16[27,16,128]{2,1,0:T(8,128)(2,1)S(1)}, u32[]{:S(2)}, u32[]{:S(2)}) collective-permute-start(bf16[27,16,128]{2,1,0:T(8,128)(2,1)S(1)} %get-tuple-element.47), channel_id=1, source_target_pairs={{0,6},{1,7},{2,4},{3,5},{4,2},{5,3},{6,0},{7,1},{8,14},{9,15},{10,... | collective-permute-start | bytes 331784 | tf_op jit(solution)/shard_map/ppermute | solution.py:263
  15.1 6.3 %collective-permute-start.6 = (bf16[27,16,128]{2,1,0:T(8,128)(2,1)S(1)}, bf16[27,16,128]{2,1,0:T(8,128)(2,1)S(1)}, u32[]{:S(2)}, u32[]{:S(2)}) collective-permute-start(bf16[27,16,128]{2,1,0:T(8,128)(2,1)S(1)} %get-tuple-element.48), channel_id=1, source_target_pairs={{0,2},{1,3},{2,0},{3,1},{4,6},{5,7},{6,4},{7,5},{8,10},{9,11},{10,... | collective-permute-start | bytes 331784 | tf_op jit(solution)/shard_map/ppermute | solution.py:263
  15.2 6.4 %collective-permute-start.7 = (bf16[27,16,128]{2,1,0:T(8,128)(2,1)S(1)}, bf16[27,16,128]{2,1,0:T(8,128)(2,1)S(1)}, u32[]{:S(2)}, u32[]{:S(2)}) collective-permute-start(bf16[27,16,128]{2,1,0:T(8,128)(2,1)S(1)} %get-tuple-element.49), channel_id=1, source_target_pairs={{0,4},{1,5},{2,6},{3,7},{4,0},{5,1},{6,2},{7,3},{8,12},{9,13},{10,... | collective-permute-start | bytes 331784 | tf_op jit(solution)/shard_map/ppermute | solution.py:263
  17.1 7.4 %collective-permute-start.8 = (bf16[27,16,128]{2,1,0:T(8,128)(2,1)S(1)}, bf16[27,16,128]{2,1,0:T(8,128)(2,1)S(1)}, u32[]{:S(2)}, u32[]{:S(2)}) collective-permute-start(bf16[27,16,128]{2,1,0:T(8,128)(2,1)S(1)} %get-tuple-element.52), channel_id=1, source_target_pairs={{0,6},{1,7},{2,4},{3,5},{4,2},{5,3},{6,0},{7,1},{8,14},{9,15},{10,... | collective-permute-start | bytes 331784 | tf_op jit(solution)/shard_map/ppermute | solution.py:263
  20.0 5.7 %collective-permute-start.9 = (bf16[27,16,128]{2,1,0:T(8,128)(2,1)S(1)}, bf16[27,16,128]{2,1,0:T(8,128)(2,1)S(1)}, u32[]{:S(2)}, u32[]{:S(2)}) collective-permute-start(bf16[27,16,128]{2,1,0:T(8,128)(2,1)S(1)} %get-tuple-element.53), channel_id=1, source_target_pairs={{0,2},{1,3},{2,0},{3,1},{4,6},{5,7},{6,4},{7,5},{8,10},{9,11},{10,... | collective-permute-start | bytes 331784 | tf_op jit(solution)/shard_map/ppermute | solution.py:263
  20.1 5.6 %collective-permute-start.10 = (bf16[27,16,128]{2,1,0:T(8,128)(2,1)S(1)}, bf16[27,16,128]{2,1,0:T(8,128)(2,1)S(1)}, u32[]{:S(2)}, u32[]{:S(2)}) collective-permute-start(bf16[27,16,128]{2,1,0:T(8,128)(2,1)S(1)} %get-tuple-element.54), channel_id=1, source_target_pairs={{0,4},{1,5},{2,6},{3,7},{4,0},{5,1},{6,2},{7,3},{8,12},{9,13},{10,... | collective-permute-start | bytes 331784 | tf_op jit(solution)/shard_map/ppermute | solution.py:263
  21.6 7.8 %collective-permute-start.11 = (bf16[16,16,128]{2,1,0:T(8,128)(2,1)S(1)}, bf16[16,16,128]{2,1,0:T(8,128)(2,1)S(1)}, u32[]{:S(2)}, u32[]{:S(2)}) collective-permute-start(bf16[16,16,128]{2,1,0:T(8,128)(2,1)S(1)} %get-tuple-element.57), channel_id=1, source_target_pairs={{1,2},{3,4},{5,6},{7,8},{9,10},{11,12},{13,14},{17,18},{19,20},{21... | collective-permute-start | bytes 196616 | tf_op jit(solution)/shard_map/ppermute | solution.py:266
  23.2 5.6 %collective-permute-start.13 = (bf16[224,128]{1,0:T(8,128)(2,1)S(1)}, bf16[224,128]{1,0:T(8,128)(2,1)S(1)}, u32[]{:S(2)}, u32[]{:S(2)}) collective-permute-start(bf16[224,128]{1,0:T(8,128)(2,1)S(1)} %get-tuple-element.62), channel_id=1, source_target_pairs={{0,8},{1,9},{2,10},{3,11},{4,12},{5,13},{6,14},{7,15},{8,0},{9,1},... | collective-permute-start | bytes 172040 | tf_op jit(solution)/shard_map/ppermute | solution.py:263
  25.8 6.3 %collective-permute-start.12 = (bf16[224,128]{1,0:T(8,128)(2,1)S(1)}, bf16[224,128]{1,0:T(8,128)(2,1)S(1)}, u32[]{:S(2)}, u32[]{:S(2)}) collective-permute-start(bf16[224,128]{1,0:T(8,128)(2,1)S(1)} %get-tuple-element.61), channel_id=1, source_target_pairs={{0,8},{1,9},{2,10},{3,11},{4,12},{5,13},{6,14},{7,15},{8,0},{9,1},... | collective-permute-start | bytes 172040 | tf_op jit(solution)/shard_map/ppermute | solution.py:263

commit v6 on v5

--- a/solution.py
+++ b/solution.py
@@ -219,6 +219,51 @@
                     target[tap + lane] = rows[d * block : (d + 1) * block].astype(BF16)
 
 
+def half_products(size, index, away, slab, other, border, input_planes, wide, turned):
+    channels = slab.shape[-1]
+    side = jnp.bitwise_xor(lax.rem(index, 2), away)
+    choice = channel_choice(size, channels, index)
+    edge_rows(wide)
+    for i in range(2):
+        narrow(wide, i, input_planes[i], choice)
+        turned[1 + i] = turn(slab[i])
+    turned[3 * side] = turn(border)
+    turned[3 * (1 - side)] = turn(other[side])
+    left = jnp.concatenate(
+        [jnp.concatenate([turned[i + 2 - a] for a in range(3)], axis=0) for i in range(2)], axis=1
+    )
+    return [
+        jnp.dot(left, patch(wide, 0, 2, column), preferred_element_type=F32) for column in range(3)
+    ]
+
+
+def second_own_kernel(size, cot, cot_sib, near, out, wide, turned):
+    index, _ = core_of(size)
+    sums = half_products(size, index, 0, cot, cot_sib, near[3], near, wide, turned)
+    for column in range(3):
+        out[column] = sums[column]
+
+
+def second_rest_kernel(size, cot, cot_sib, near_sib, own, keep, *refs):
+    sends, wide, turned = refs[:-2], refs[-2], refs[-1]
+    index, _ = core_of(size)
+    channels = cot.shape[-1]
+    sums = half_products(size, index, 1, cot_sib, cot, near_sib[3], near_sib, wide, turned)
+    half = channels // 2
+    block = half // 4
+    for column in range(3):
+        total = sums[column] + own[column]
+        for a in range(3):
+            rows_a = total[a * channels : (a + 1) * channels]
+            first = rows_a[:, :channels].T
+            second = rows_a[:, channels:].T
+            tap = (a * 3 + column) * 3
+            for lane, rows in enumerate((first[:half], first[half:], second[:half])):
+                keep[tap + lane] = rows[:block]
+                for d, target in enumerate(sends, 1):
+                    target[tap + lane] = rows[d * block : (d + 1) * block].astype(BF16)
+
+
 def near_sum_kernel(share, keep, got_a, got_b, got_c, own, *sends):
     total = keep[...]
     for got in (got_a, got_b, got_c):
@@ -356,7 +401,19 @@
             )(own, *gots)
         return jnp.transpose(total.reshape(3, 3, 3, share, channels), (3, 0, 1, 2, 4))
 
-    keep_2, blocks_2 = filter_grad(1, (cotangent, cot_sib, near, near_sib, near, near_sib), "second_grad")
+    halves = [wide(2, 2 * channels), pltpu.VMEM((4, channels, width * height), BF16)]
+    own_2 = call(
+        functools.partial(second_own_kernel, size),
+        jax.ShapeDtypeStruct((3, 3 * channels, 2 * channels), F32),
+        halves,
+        "second_own",
+    )(cotangent, cot_sib, near)
+    keep_2, *blocks_2 = call(
+        functools.partial(second_rest_kernel, size),
+        (keep_type,) + (block_type,) * 3,
+        halves,
+        "second_rest",
+    )(cotangent, cot_sib, near_sib, own_2)
     grad_sib, keep_2 = lax.optimization_barrier((grad_sib, keep_2))
     gots_2 = near_hop(blocks_2)
     keep_1, blocks_1 = filter_grad(0, (volume, vol_sib, near, near_sib, grad, grad_sib), "first_grad")

time: 32.9 us -> 32.7 us (level)
  waiting for transfers between devices: 3.68 us -> 2.97 us
    pallas_call x0 -> x2, Pallas kernels: none -> 1.52 us  [the longest x1 0.84 us: per_device(): call(functools.partial(second_rest_kernel, size), (keep_type,) + (block_t...]
    pallas_call x2 -> x1, Pallas kernels: 2.64 us -> 1.32 us  [filter_grad(): call(functools.partial(weight_kernel, size, which), (keep_type,) + (block...]
    ppermute x12, waiting for transfers between devices: 3.67 us -> 2.97 us  [send(): return lax.ppermute(array, 'space', moves)]
  transfers between devices with their start and end apart: 14 -> 14, of which waited for: 8 -> 6; matrix products, arithmetic and copies ran while one was open for 0% -> 0% of each run, Pallas kernels for 22% -> 23%
where the time goes in v6:
time: 32.7 us; the launch traced here: 32.5 us
  starting transfers between devices  18 us (55%)
  Pallas kernels  8.72 us (27%)
  waiting for transfers between devices  2.97 us (9%)
  local copies, waits for them, and re-layouts  2.01 us (6%)
  between operations  0.79 us (2%)
    ppermute x12, starting transfers between devices, send(): return lax.ppermute(array, 'space', moves)  13.4 us
    ppermute x2, starting transfers between devices, send_across(): return lax.ppermute(array, ('parts', 'space'), across)  4.56 us
    ppermute x12, waiting for transfers between devices, send(): return lax.ppermute(array, 'space', moves)  2.97 us
    pallas_call x1, Pallas kernels, per_device(): call(functools.partial(response_kernel, size), slab_type, [wide(4, 3 * ch...  1.89 us
    pallas_call x2, Pallas kernels, inner(): call(functools.partial(inner_kernel, back), sums_type, [wide(2, 3 * chann...  1.55 us
    pallas_call x1, Pallas kernels, filter_grad(): call(functools.partial(weight_kernel, size, which), (keep_type,) + (block...  1.32 us
    pallas_call x2, Pallas kernels, last_sum(): call(last_sum_kernel, jax.ShapeDtypeStruct(own.shape, F32), [], name)  1.32 us
    slice x1, local copies, waits for them, and re-layouts, per_device(): volume[1]  1.09 us
  transfers between devices with their start and end apart: 14, of which 6 were waited for; matrix products, arithmetic and copies ran while one was open for 0% of the time, Pallas kernels for 23%

profile of v6, /device:TPU:0, one launch (start us, length us, event | category | flops | bytes accessed | tf_op | source)
XLA Modules:
  0.0 32.5 jit_solution(3628785532148290248)
XLA Ops:
  0.7 1.1 %fusion = (bf16[1,16,16,128]{3,2,1,0:T(8,128)(2,1)S(1)}, bf16[1,16,16,128]{3,2,1,0:T(8,128)(2,1)S(1)}, bf16[1,16,16,128]{3,2,1,0:T(8,128)(2,1)S(1)}, bf16[1,16,16,128]{3,2,1,0:T(8,128)(2,1)S(1)}) fusion(bf16[2,16,16,128]{3,2,1,0:T(8,128)(2,1)} %own.5, bf16[2,16,16,128]{3,2,1,0:T(8,128)(2,1)} %cot.3), kind=kLoop, calls=%fused_computation.1 | loop fusion | bytes 524288 | tf_op jit(solution)/shard_map/slice | solution.py:327
  1.8 3.0 %collective-permute-start = (bf16[2,16,16,128]{3,2,1,0:T(8,128)(2,1)S(1)}, bf16[2,16,16,128]{3,2,1,0:T(8,128)(2,1)S(1)}, u32[]{:S(2)}, u32[]{:S(2)}) collective-permute-start(bf16[2,16,16,128]{3,2,1,0:T(8,128)(2,1)S(1)} %maximum_select_fusion), channel_id=1, source_target_pairs={{1,2},{3,4},{5,6},{7,8},{9,10},{11,12},{13,14},{17,18},{19,20},{21... | collective-permute-start | bytes 393224 | tf_op jit(solution)/shard_map/ppermute | solution.py:311
  4.8 0.1 collective-permute-start.1
  4.9 0.4 %collective-permute-start.2 = (bf16[2,16,16,128]{3,2,1,0:T(8,128)(2,1)}, bf16[2,16,16,128]{3,2,1,0:T(8,128)(2,1)S(1)}, u32[]{:S(2)}, u32[]{:S(2)}) collective-permute-start(bf16[2,16,16,128]{3,2,1,0:T(8,128)(2,1)} %cot.3), channel_id=1, source_target_pairs={{0,1},{1,0},{2,3},{3,2},{4,5},{5,4},{6,7},{7,6},{8,9},{9,8},{10,11... | collective-permute-start | bytes 393224 | tf_op jit(solution)/shard_map/ppermute | solution.py:308
  5.3 0.9 %copy-done.3 = bf16[2,16,16,128]{3,2,1,0:T(8,128)(2,1)S(1)} copy-done((bf16[2,16,16,128]{3,2,1,0:T(8,128)(2,1)S(1)}, bf16[2,16,16,128]{3,2,1,0:T(8,128)(2,1)}, u32[]{:S(2)}) %copy-start.3) | copy-done | bytes 131096
  6.2 0.8 %inner.1.part = f32[2,256,128]{2,1,0:T(8,128)S(1)} custom-call(bf16[2,16,16,128]{3,2,1,0:T(8,128)(2,1)S(1)} %copy-done.3, bf16[3,3,3,128,128]{4,3,2,1,0:T(8,128)(2,1)S(1)} %copy-done.1), custom_call_target="tpu_custom_call" | custom-call | tf_op jit(solution)/shard_map/inner/pallas_call | solution.py:335
  7.0 0.8 %inner_back.1.part = f32[2,256,128]{2,1,0:T(8,128)S(1)} custom-call(bf16[2,16,16,128]{3,2,1,0:T(8,128)(2,1)S(1)} %copy-done.2, bf16[3,3,3,128,128]{4,3,2,1,0:T(8,128)(2,1)S(1)} %copy-done), custom_call_target="tpu_custom_call" | custom-call | tf_op jit(solution)/shard_map/inner_back/pallas_call | solution.py:335
  7.8 0.5 %hidden.1 = (f32[2,256,128]{2,1,0:T(8,128)S(1)}, bf16[4,16,16,128]{3,2,1,0:T(8,128)(2,1)S(1)}, bf16[16,16,128]{2,1,0:T(8,128)(2,1)S(1)}) custom-call(f32[2,256,128]{2,1,0:T(8,128)S(1)} %inner.1.part, bf16[2,16,16,128]{3,2,1,0:T(8,128)(2,1)S(1)} %collective-permute-done.1.sib, bf16[2,16,16,128]{3,2,1,0:T(8,128)(2,1)S(1)} %collective-permute-done.cross, ...), custom_call_target="tpu_custom_call" | custom-call | tf_op jit(solution)/shard_map/hidden/pallas_call | solution.py:342
  8.3 0.5 %collective-permute-start.3 = (bf16[4,16,16,128]{3,2,1,0:T(8,128)(2,1)S(1)}, bf16[4,16,16,128]{3,2,1,0:T(8,128)(2,1)S(1)}, u32[]{:S(2)}, u32[]{:S(2)}) collective-permute-start(bf16[4,16,16,128]{3,2,1,0:T(8,128)(2,1)S(1)} %get-tuple-element.39.near), channel_id=1, source_target_pairs={{0,1},{1,0},{2,3},{3,2},{4,5},{5,4},{6,7},{7,6},{8,9},{9,8},{10,11... | collective-permute-start | bytes 786440 | tf_op jit(solution)/shard_map/ppermute | solution.py:308
  8.8 0.5 %hidden_grad.1.four = bf16[2,16,16,128]{3,2,1,0:T(8,128)(2,1)S(1)} custom-call(f32[2,256,128]{2,1,0:T(8,128)S(1)} %get-tuple-element.40.hidden, f32[2,256,128]{2,1,0:T(8,128)S(1)} %inner_back.1.part, bf16[2,16,16,128]{3,2,1,0:T(8,128)(2,1)S(1)} %collective-permute-done.2.sib.cot_sib, bf16[2,16,16,128]{3,2,1,0:T(8,128)(2,1)S(1)} %collective-permute-done.cross, ...), custom_call_target="tpu_custom_call" | custom-call | tf_op jit(solution)/shard_map/hidden_grad/pallas_call | solution.py:349
  9.3 0.1 collective-permute-start.4
  9.5 0.7 %second_own.1.own = f32[3,384,256]{2,1,0:T(8,128)S(1)} custom-call(bf16[2,16,16,128]{3,2,1,0:T(8,128)(2,1)S(1)} %copy-done.2, bf16[2,16,16,128]{3,2,1,0:T(8,128)(2,1)S(1)} %collective-permute-done.2.sib.cot_sib, bf16[4,16,16,128]{3,2,1,0:T(8,128)(2,1)S(1)} %get-tuple-element.39.near), custom_call_target="tpu_custom_call" | custom-call | tf_op jit(solution)/shard_map/second_own/pallas_call | solution.py:405
  10.2 0.8 %second_rest.1 = (f32[27,16,128]{2,1,0:T(8,128)S(1)}, bf16[27,16,128]{2,1,0:T(8,128)(2,1)S(1)}, bf16[27,16,128]{2,1,0:T(8,128)(2,1)S(1)}, bf16[27,16,128]{2,1,0:T(8,128)(2,1)S(1)}) custom-call(bf16[2,16,16,128]{3,2,1,0:T(8,128)(2,1)S(1)} %copy-done.2, bf16[2,16,16,128]{3,2,1,0:T(8,128)(2,1)S(1)} %collective-permute-done.2.sib.cot_sib, ...), custom_call_target="tpu_custom_call" | custom-call | tf_op jit(solution)/shard_map/second_rest/pallas_call | solution.py:411
  11.0 3.9 %collective-permute-start.5 = (bf16[27,16,128]{2,1,0:T(8,128)(2,1)S(1)}, bf16[27,16,128]{2,1,0:T(8,128)(2,1)S(1)}, u32[]{:S(2)}, u32[]{:S(2)}) collective-permute-start(bf16[27,16,128]{2,1,0:T(8,128)(2,1)S(1)} %get-tuple-element.47), channel_id=1, source_target_pairs={{0,6},{1,7},{2,4},{3,5},{4,2},{5,3},{6,0},{7,1},{8,14},{9,15},{10,... | collective-permute-start | bytes 331784 | tf_op jit(solution)/shard_map/ppermute | solution.py:308
  14.9 0.1 collective-permute-start.6
  15.0 0.5 %collective-permute-start.7 = (bf16[27,16,128]{2,1,0:T(8,128)(2,1)S(1)}, bf16[27,16,128]{2,1,0:T(8,128)(2,1)S(1)}, u32[]{:S(2)}, u32[]{:S(2)}) collective-permute-start(bf16[27,16,128]{2,1,0:T(8,128)(2,1)S(1)} %get-tuple-element.49), channel_id=1, source_target_pairs={{0,4},{1,5},{2,6},{3,7},{4,0},{5,1},{6,2},{7,3},{8,12},{9,13},{10,... | collective-permute-start | bytes 331784 | tf_op jit(solution)/shard_map/ppermute | solution.py:308
  15.6 1.3 %first_grad.1 = (f32[27,16,128]{2,1,0:T(8,128)S(1)}, bf16[27,16,128]{2,1,0:T(8,128)(2,1)S(1)}, bf16[27,16,128]{2,1,0:T(8,128)(2,1)S(1)}, bf16[27,16,128]{2,1,0:T(8,128)(2,1)S(1)}) custom-call(bf16[2,16,16,128]{3,2,1,0:T(8,128)(2,1)S(1)} %copy-done.4, bf16[2,16,16,128]{3,2,1,0:T(8,128)(2,1)S(1)} %collective-permute-done.1.sib, ...), custom_call_target="tpu_custom_call" | custom-call | tf_op jit(solution)/shard_map/first_grad/pallas_call | solution.py:361
  16.9 2.9 %collective-permute-start.8 = (bf16[27,16,128]{2,1,0:T(8,128)(2,1)S(1)}, bf16[27,16,128]{2,1,0:T(8,128)(2,1)S(1)}, u32[]{:S(2)}, u32[]{:S(2)}) collective-permute-start(bf16[27,16,128]{2,1,0:T(8,128)(2,1)S(1)} %get-tuple-element.52), channel_id=1, source_target_pairs={{0,6},{1,7},{2,4},{3,5},{4,2},{5,3},{6,0},{7,1},{8,14},{9,15},{10,... | collective-permute-start | bytes 331784 | tf_op jit(solution)/shard_map/ppermute | solution.py:308
  19.8 0.1 collective-permute-start.9
  19.9 0.5 %collective-permute-start.10 = (bf16[27,16,128]{2,1,0:T(8,128)(2,1)S(1)}, bf16[27,16,128]{2,1,0:T(8,128)(2,1)S(1)}, u32[]{:S(2)}, u32[]{:S(2)}) collective-permute-start(bf16[27,16,128]{2,1,0:T(8,128)(2,1)S(1)} %get-tuple-element.54), channel_id=1, source_target_pairs={{0,4},{1,5},{2,6},{3,7},{4,0},{5,1},{6,2},{7,3},{8,12},{9,13},{10,... | collective-permute-start | bytes 331784 | tf_op jit(solution)/shard_map/ppermute | solution.py:308
  20.4 0.7 %collective-permute-done.6.got_b = bf16[27,16,128]{2,1,0:T(8,128)(2,1)S(1)} collective-permute-done((bf16[27,16,128]{2,1,0:T(8,128)(2,1)S(1)}, bf16[27,16,128]{2,1,0:T(8,128)(2,1)S(1)}, u32[]{:S(2)}, u32[]{:S(2)}) %collective-permute-start.6) | collective-permute-done | bytes 110624 | tf_op jit(solution)/shard_map/ppermute | solution.py:308
  21.1 0.2 collective-permute-done.7.got_c
  21.4 1.6 %collective-permute-start.11 = (bf16[16,16,128]{2,1,0:T(8,128)(2,1)S(1)}, bf16[16,16,128]{2,1,0:T(8,128)(2,1)S(1)}, u32[]{:S(2)}, u32[]{:S(2)}) collective-permute-start(bf16[16,16,128]{2,1,0:T(8,128)(2,1)S(1)} %get-tuple-element.57), channel_id=1, source_target_pairs={{1,2},{3,4},{5,6},{7,8},{9,10},{11,12},{13,14},{17,18},{19,20},{21... | collective-permute-start | bytes 196616 | tf_op jit(solution)/shard_map/ppermute | solution.py:311
  22.9 1.2 %collective-permute-start.13 = (bf16[224,128]{1,0:T(8,128)(2,1)S(1)}, bf16[224,128]{1,0:T(8,128)(2,1)S(1)}, u32[]{:S(2)}, u32[]{:S(2)}) collective-permute-start(bf16[224,128]{1,0:T(8,128)(2,1)S(1)} %get-tuple-element.62), channel_id=1, source_target_pairs={{0,8},{1,9},{2,10},{3,11},{4,12},{5,13},{6,14},{7,15},{8,0},{9,1},... | collective-permute-start | bytes 172040 | tf_op jit(solution)/shard_map/ppermute | solution.py:308
  24.1 0.3 collective-permute-done.8.got_a
  24.4 1.0 %collective-permute-done.9.got_b = bf16[27,16,128]{2,1,0:T(8,128)(2,1)S(1)} collective-permute-done((bf16[27,16,128]{2,1,0:T(8,128)(2,1)S(1)}, bf16[27,16,128]{2,1,0:T(8,128)(2,1)S(1)}, u32[]{:S(2)}, u32[]{:S(2)}) %collective-permute-start.9) | collective-permute-done | bytes 110624 | tf_op jit(solution)/shard_map/ppermute | solution.py:308
  25.4 0.1 collective-permute-done.10.got_c
  25.5 3.0 %collective-permute-start.12 = (bf16[224,128]{1,0:T(8,128)(2,1)S(1)}, bf16[224,128]{1,0:T(8,128)(2,1)S(1)}, u32[]{:S(2)}, u32[]{:S(2)}) collective-permute-start(bf16[224,128]{1,0:T(8,128)(2,1)S(1)} %get-tuple-element.61), channel_id=1, source_target_pairs={{0,8},{1,9},{2,10},{3,11},{4,12},{5,13},{6,14},{7,15},{8,0},{9,1},... | collective-permute-start | bytes 172040 | tf_op jit(solution)/shard_map/ppermute | solution.py:308
  28.5 0.7 %second_last_sum.1 = f32[216,128]{1,0:T(8,128)} custom-call(f32[216,128]{1,0:T(8,128)S(1)} %get-tuple-element.50.refs_0_, bf16[224,128]{1,0:T(8,128)(2,1)S(1)} %collective-permute-done.13.refs_1_), custom_call_target="tpu_custom_call" | custom-call | tf_op jit(solution)/shard_map/second_last_sum/pallas_call | solution.py:399
  29.2 1.9 %response.1 = bf16[2,16,16,128]{3,2,1,0:T(8,128)(2,1)} custom-call(bf16[4,16,16,128]{3,2,1,0:T(8,128)(2,1)S(1)} %get-tuple-element.39.near, bf16[4,16,16,128]{3,2,1,0:T(8,128)(2,1)S(1)} %collective-permute-done.3.near_sib, bf16[16,16,128]{2,1,0:T(8,128)(2,1)S(1)} %collective-permute-done.11.cross, bf16[3,3,3,128,128]{4,3,2,1,0:T(8,128)(2,1)S(1)} %copy-done), custom_call_target="tpu_custom_call" | custom-call | tf_op jit(solution)/shard_map/response/pallas_call | solution.py:429
  31.1 0.8 %collective-permute-done.12.refs_1_ = bf16[224,128]{1,0:T(8,128)(2,1)S(1)} collective-permute-done((bf16[224,128]{1,0:T(8,128)(2,1)S(1)}, bf16[224,128]{1,0:T(8,128)(2,1)S(1)}, u32[]{:S(2)}, u32[]{:S(2)}) %collective-permute-start.12) | collective-permute-done | bytes 57376 | tf_op jit(solution)/shard_map/ppermute | solution.py:308
  31.9 0.7 %first_last_sum.1 = f32[216,128]{1,0:T(8,128)} custom-call(f32[216,128]{1,0:T(8,128)S(1)} %get-tuple-element.60.refs_0_, bf16[224,128]{1,0:T(8,128)(2,1)S(1)} %collective-permute-done.12.refs_1_), custom_call_target="tpu_custom_call" | custom-call | tf_op jit(solution)/shard_map/first_last_sum/pallas_call | solution.py:399
  (20 shorter events, 0.2 us)
Async XLA Ops:
  0.6 4.7 %copy-start.1 = (bf16[3,3,3,128,128]{4,3,2,1,0:T(8,128)(2,1)S(1)}, bf16[3,3,3,128,128]{4,3,2,1,0:T(8,128)(2,1)}, u32[]{:S(2)}) copy-start(bf16[3,3,3,128,128]{4,3,2,1,0:T(8,128)(2,1)} %first.1) | copy-start | bytes 2654212
  0.6 6.4 %copy-start.2 = (bf16[2,16,16,128]{3,2,1,0:T(8,128)(2,1)S(1)}, bf16[2,16,16,128]{3,2,1,0:T(8,128)(2,1)}, u32[]{:S(2)}) copy-start(bf16[2,16,16,128]{3,2,1,0:T(8,128)(2,1)} %cot.3) | copy-start | bytes 393220
  0.7 6.4 %copy-start = (bf16[3,3,3,128,128]{4,3,2,1,0:T(8,128)(2,1)S(1)}, bf16[3,3,3,128,128]{4,3,2,1,0:T(8,128)(2,1)}, u32[]{:S(2)}) copy-start(bf16[3,3,3,128,128]{4,3,2,1,0:T(8,128)(2,1)} %second.3) | copy-start | bytes 2654212
  1.8 6.0 %collective-permute-start = (bf16[2,16,16,128]{3,2,1,0:T(8,128)(2,1)S(1)}, bf16[2,16,16,128]{3,2,1,0:T(8,128)(2,1)S(1)}, u32[]{:S(2)}, u32[]{:S(2)}) collective-permute-start(bf16[2,16,16,128]{3,2,1,0:T(8,128)(2,1)S(1)} %maximum_select_fusion), channel_id=1, source_target_pairs={{1,2},{3,4},{5,6},{7,8},{9,10},{11,12},{13,14},{17,18},{19,20},{21... | collective-permute-start | bytes 393224 | tf_op jit(solution)/shard_map/ppermute | solution.py:311
  4.8 3.0 %collective-permute-start.1 = (bf16[2,16,16,128]{3,2,1,0:T(8,128)(2,1)}, bf16[2,16,16,128]{3,2,1,0:T(8,128)(2,1)S(1)}, u32[]{:S(2)}, u32[]{:S(2)}) collective-permute-start(bf16[2,16,16,128]{3,2,1,0:T(8,128)(2,1)} %own.5), channel_id=1, source_target_pairs={{0,1},{1,0},{2,3},{3,2},{4,5},{5,4},{6,7},{7,6},{8,9},{9,8},{10,11... | collective-permute-start | bytes 393224 | tf_op jit(solution)/shard_map/ppermute | solution.py:308
  4.9 2.9 %collective-permute-start.2 = (bf16[2,16,16,128]{3,2,1,0:T(8,128)(2,1)}, bf16[2,16,16,128]{3,2,1,0:T(8,128)(2,1)S(1)}, u32[]{:S(2)}, u32[]{:S(2)}) collective-permute-start(bf16[2,16,16,128]{3,2,1,0:T(8,128)(2,1)} %cot.3), channel_id=1, source_target_pairs={{0,1},{1,0},{2,3},{3,2},{4,5},{5,4},{6,7},{7,6},{8,9},{9,8},{10,11... | collective-permute-start | bytes 393224 | tf_op jit(solution)/shard_map/ppermute | solution.py:308
  5.3 0.9 %copy-start.3 = (bf16[2,16,16,128]{3,2,1,0:T(8,128)(2,1)S(1)}, bf16[2,16,16,128]{3,2,1,0:T(8,128)(2,1)}, u32[]{:S(2)}) copy-start(bf16[2,16,16,128]{3,2,1,0:T(8,128)(2,1)} %own.5) | copy-start | bytes 393220
  8.3 1.9 %collective-permute-start.3 = (bf16[4,16,16,128]{3,2,1,0:T(8,128)(2,1)S(1)}, bf16[4,16,16,128]{3,2,1,0:T(8,128)(2,1)S(1)}, u32[]{:S(2)}, u32[]{:S(2)}) collective-permute-start(bf16[4,16,16,128]{3,2,1,0:T(8,128)(2,1)S(1)} %get-tuple-element.39.near), channel_id=1, source_target_pairs={{0,1},{1,0},{2,3},{3,2},{4,5},{5,4},{6,7},{7,6},{8,9},{9,8},{10,11... | collective-permute-start | bytes 786440 | tf_op jit(solution)/shard_map/ppermute | solution.py:308
  9.3 6.2 %collective-permute-start.4 = (bf16[2,16,16,128]{3,2,1,0:T(8,128)(2,1)S(1)}, bf16[2,16,16,128]{3,2,1,0:T(8,128)(2,1)S(1)}, u32[]{:S(2)}, u32[]{:S(2)}) collective-permute-start(bf16[2,16,16,128]{3,2,1,0:T(8,128)(2,1)S(1)} %hidden_grad.1.four), channel_id=1, source_target_pairs={{0,1},{1,0},{2,3},{3,2},{4,5},{5,4},{6,7},{7,6},{8,9},{9,8},{10,11... | collective-permute-start | bytes 393224 | tf_op jit(solution)/shard_map/ppermute | solution.py:308
  10.2 5.4 %copy-start.4 = (bf16[2,16,16,128]{3,2,1,0:T(8,128)(2,1)S(1)}, bf16[2,16,16,128]{3,2,1,0:T(8,128)(2,1)}, u32[]{:S(2)}) copy-start(bf16[2,16,16,128]{3,2,1,0:T(8,128)(2,1)} %own.5) | copy-start | bytes 393220
  11.0 8.9 %collective-permute-start.5 = (bf16[27,16,128]{2,1,0:T(8,128)(2,1)S(1)}, bf16[27,16,128]{2,1,0:T(8,128)(2,1)S(1)}, u32[]{:S(2)}, u32[]{:S(2)}) collective-permute-start(bf16[27,16,128]{2,1,0:T(8,128)(2,1)S(1)} %get-tuple-element.47), channel_id=1, source_target_pairs={{0,6},{1,7},{2,4},{3,5},{4,2},{5,3},{6,0},{7,1},{8,14},{9,15},{10,... | collective-permute-start | bytes 331784 | tf_op jit(solution)/shard_map/ppermute | solution.py:308
  14.9 6.2 %collective-permute-start.6 = (bf16[27,16,128]{2,1,0:T(8,128)(2,1)S(1)}, bf16[27,16,128]{2,1,0:T(8,128)(2,1)S(1)}, u32[]{:S(2)}, u32[]{:S(2)}) collective-permute-start(bf16[27,16,128]{2,1,0:T(8,128)(2,1)S(1)} %get-tuple-element.48), channel_id=1, source_target_pairs={{0,2},{1,3},{2,0},{3,1},{4,6},{5,7},{6,4},{7,5},{8,10},{9,11},{10,... | collective-permute-start | bytes 331784 | tf_op jit(solution)/shard_map/ppermute | solution.py:308
  15.0 6.3 %collective-permute-start.7 = (bf16[27,16,128]{2,1,0:T(8,128)(2,1)S(1)}, bf16[27,16,128]{2,1,0:T(8,128)(2,1)S(1)}, u32[]{:S(2)}, u32[]{:S(2)}) collective-permute-start(bf16[27,16,128]{2,1,0:T(8,128)(2,1)S(1)} %get-tuple-element.49), channel_id=1, source_target_pairs={{0,4},{1,5},{2,6},{3,7},{4,0},{5,1},{6,2},{7,3},{8,12},{9,13},{10,... | collective-permute-start | bytes 331784 | tf_op jit(solution)/shard_map/ppermute | solution.py:308
  16.9 7.5 %collective-permute-start.8 = (bf16[27,16,128]{2,1,0:T(8,128)(2,1)S(1)}, bf16[27,16,128]{2,1,0:T(8,128)(2,1)S(1)}, u32[]{:S(2)}, u32[]{:S(2)}) collective-permute-start(bf16[27,16,128]{2,1,0:T(8,128)(2,1)S(1)} %get-tuple-element.52), channel_id=1, source_target_pairs={{0,6},{1,7},{2,4},{3,5},{4,2},{5,3},{6,0},{7,1},{8,14},{9,15},{10,... | collective-permute-start | bytes 331784 | tf_op jit(solution)/shard_map/ppermute | solution.py:308
  19.8 5.6 %collective-permute-start.9 = (bf16[27,16,128]{2,1,0:T(8,128)(2,1)S(1)}, bf16[27,16,128]{2,1,0:T(8,128)(2,1)S(1)}, u32[]{:S(2)}, u32[]{:S(2)}) collective-permute-start(bf16[27,16,128]{2,1,0:T(8,128)(2,1)S(1)} %get-tuple-element.53), channel_id=1, source_target_pairs={{0,2},{1,3},{2,0},{3,1},{4,6},{5,7},{6,4},{7,5},{8,10},{9,11},{10,... | collective-permute-start | bytes 331784 | tf_op jit(solution)/shard_map/ppermute | solution.py:308
  19.9 5.5 %collective-permute-start.10 = (bf16[27,16,128]{2,1,0:T(8,128)(2,1)S(1)}, bf16[27,16,128]{2,1,0:T(8,128)(2,1)S(1)}, u32[]{:S(2)}, u32[]{:S(2)}) collective-permute-start(bf16[27,16,128]{2,1,0:T(8,128)(2,1)S(1)} %get-tuple-element.54), channel_id=1, source_target_pairs={{0,4},{1,5},{2,6},{3,7},{4,0},{5,1},{6,2},{7,3},{8,12},{9,13},{10,... | collective-permute-start | bytes 331784 | tf_op jit(solution)/shard_map/ppermute | solution.py:308
  21.4 7.8 %collective-permute-start.11 = (bf16[16,16,128]{2,1,0:T(8,128)(2,1)S(1)}, bf16[16,16,128]{2,1,0:T(8,128)(2,1)S(1)}, u32[]{:S(2)}, u32[]{:S(2)}) collective-permute-start(bf16[16,16,128]{2,1,0:T(8,128)(2,1)S(1)} %get-tuple-element.57), channel_id=1, source_target_pairs={{1,2},{3,4},{5,6},{7,8},{9,10},{11,12},{13,14},{17,18},{19,20},{21... | collective-permute-start | bytes 196616 | tf_op jit(solution)/shard_map/ppermute | solution.py:311
  22.9 5.6 %collective-permute-start.13 = (bf16[224,128]{1,0:T(8,128)(2,1)S(1)}, bf16[224,128]{1,0:T(8,128)(2,1)S(1)}, u32[]{:S(2)}, u32[]{:S(2)}) collective-permute-start(bf16[224,128]{1,0:T(8,128)(2,1)S(1)} %get-tuple-element.62), channel_id=1, source_target_pairs={{0,8},{1,9},{2,10},{3,11},{4,12},{5,13},{6,14},{7,15},{8,0},{9,1},... | collective-permute-start | bytes 172040 | tf_op jit(solution)/shard_map/ppermute | solution.py:308
  25.5 6.4 %collective-permute-start.12 = (bf16[224,128]{1,0:T(8,128)(2,1)S(1)}, bf16[224,128]{1,0:T(8,128)(2,1)S(1)}, u32[]{:S(2)}, u32[]{:S(2)}) collective-permute-start(bf16[224,128]{1,0:T(8,128)(2,1)S(1)} %get-tuple-element.61), channel_id=1, source_target_pairs={{0,8},{1,9},{2,10},{3,11},{4,12},{5,13},{6,14},{7,15},{8,0},{9,1},... | collective-permute-start | bytes 172040 | tf_op jit(solution)/shard_map/ppermute | solution.py:308

commit v7 on v6

--- a/solution.py
+++ b/solution.py
@@ -95,11 +95,12 @@
     return total
 
 
-def inner_kernel(back, own, weight, part, wide):
+def inner_kernel(size, back, edge, rest, weight, part, wide):
     run = backward if back else forward
     edge_rows(wide)
-    widen(wide, 0, own[0])
-    widen(wide, 1, own[1])
+    _, core = core_of(size)
+    widen(wide, core, edge[int(back)])
+    widen(wide, 1 - core, rest[int(back)])
     middle = run(lambda column: patch(wide, 0, 2, column), lambda column: weight[1, column])
     voxels = middle.shape[0] // 2
     for plane in range(2):
@@ -326,16 +327,22 @@
         jnp.stack([volume[0], cotangent[0]]),
         jnp.stack([volume[1], cotangent[1]]),
     )
-    edge, late_volume, late_cotangent = lax.optimization_barrier((edge, volume, cotangent))
+    rest = jnp.where(
+        core == 0,
+        jnp.stack([volume[1], cotangent[1]]),
+        jnp.stack([volume[0], cotangent[0]]),
+    )
     cross = send_across(edge)
+
+    def inner(back, weight, name):
+        body = functools.partial(inner_kernel, size, back)
+        return call(body, sums_type, [wide(2, 3 * channels)], name)(edge, rest, weight)
+
+    part = inner(False, first_filter, "inner")
+    part_back = inner(True, second_filter, "inner_back")
+    late_volume, late_cotangent, part = lax.optimization_barrier((volume, cotangent, part))
     vol_sib = send(late_volume, sibling)
     cot_sib = send(late_cotangent, sibling)
-
-    def inner(back, own, weight, name):
-        return call(functools.partial(inner_kernel, back), sums_type, [wide(2, 3 * channels)], name)(own, weight)
-
-    part = inner(False, volume, first_filter, "inner")
-    part_back = inner(True, cotangent, second_filter, "inner_back")
     cross, part, part_back, vol_sib, cot_sib = lax.optimization_barrier(
         (cross, part, part_back, vol_sib, cot_sib)
     )

time: 32.7 us -> 32.7 us (level)
  local copies, waits for them, and re-layouts: 2.01 us -> 1.11 us
  waiting for transfers between devices: 2.97 us -> 3.6 us
    unnamed x10 -> x8, local copies, waits for them, and re-layouts: 0.93 us -> 0.02 us
    ppermute x2, waiting for transfers between devices: 0.01 us -> 0.62 us  [send_across(): return lax.ppermute(array, ('parts', 'space'), across)]
  transfers between devices with their start and end apart: 14 -> 14, of which waited for: 6 -> 7; matrix products, arithmetic and copies ran while one was open for 0% -> 0% of each run, Pallas kernels for 23% -> 24%
where the time goes in v7:
time: 32.7 us; the launch traced here: 32.5 us
  starting transfers between devices  18.1 us (55%)
  Pallas kernels  8.88 us (27%)
  waiting for transfers between devices  3.6 us (11%)
  local copies, waits for them, and re-layouts  1.11 us (3%)
  between operations  0.76 us (2%)
    ppermute x12, starting transfers between devices, send(): return lax.ppermute(array, 'space', moves)  13.6 us
    ppermute x2, starting transfers between devices, send_across(): return lax.ppermute(array, ('parts', 'space'), across)  4.56 us
    ppermute x12, waiting for transfers between devices, send(): return lax.ppermute(array, 'space', moves)  2.98 us
    pallas_call x1, Pallas kernels, per_device(): call(functools.partial(response_kernel, size), slab_type, [wide(4, 3 * ch...  1.89 us
    pallas_call x2, Pallas kernels, inner(): call(body, sums_type, [wide(2, 3 * channels)], name)(edge, rest, weight)  1.72 us
    pallas_call x1, Pallas kernels, filter_grad(): call(functools.partial(weight_kernel, size, which), (keep_type,) + (block...  1.32 us
    pallas_call x2, Pallas kernels, last_sum(): call(last_sum_kernel, jax.ShapeDtypeStruct(own.shape, F32), [], name)  1.32 us
    slice x1, local copies, waits for them, and re-layouts, per_device(): volume[0]  1.09 us
  transfers between devices with their start and end apart: 14, of which 7 were waited for; matrix products, arithmetic and copies ran while one was open for 0% of the time, Pallas kernels for 24%

profile of v7, /device:TPU:0, one launch (start us, length us, event | category | flops | bytes accessed | tf_op | source)
XLA Modules:
  0.0 32.5 jit_solution(12727324270312649165)
XLA Ops:
  0.7 1.1 %fusion = (bf16[1,16,16,128]{3,2,1,0:T(8,128)(2,1)S(1)}, bf16[1,16,16,128]{3,2,1,0:T(8,128)(2,1)S(1)}, bf16[1,16,16,128]{3,2,1,0:T(8,128)(2,1)S(1)}, bf16[1,16,16,128]{3,2,1,0:T(8,128)(2,1)S(1)}) fusion(bf16[2,16,16,128]{3,2,1,0:T(8,128)(2,1)} %own.1, bf16[2,16,16,128]{3,2,1,0:T(8,128)(2,1)} %cot.3), kind=kLoop, calls=%fused_computation.4 | loop fusion | bytes 524288 | tf_op jit(solution)/shard_map/slice | solution.py:327
  1.8 3.0 %collective-permute-start = (bf16[2,16,16,128]{3,2,1,0:T(8,128)(2,1)S(1)}, bf16[2,16,16,128]{3,2,1,0:T(8,128)(2,1)S(1)}, u32[]{:S(2)}, u32[]{:S(2)}) collective-permute-start(bf16[2,16,16,128]{3,2,1,0:T(8,128)(2,1)S(1)} %get-tuple-element.64.edge), channel_id=1, source_target_pairs={{1,2},{3,4},{5,6},{7,8},{9,10},{11,12},{13,14},{17,18},{19,20},{21... | collective-permute-start | bytes 393224 | tf_op jit(solution)/shard_map/ppermute | solution.py:312
  4.8 0.9 %inner.1.part = f32[2,256,128]{2,1,0:T(8,128)S(1)} custom-call(bf16[2,16,16,128]{3,2,1,0:T(8,128)(2,1)S(1)} %get-tuple-element.64.edge, bf16[2,16,16,128]{3,2,1,0:T(8,128)(2,1)S(1)} %get-tuple-element.63.rest, bf16[3,3,3,128,128]{4,3,2,1,0:T(8,128)(2,1)S(1)} %copy-done.1), custom_call_target="tpu_custom_call" | custom-call | tf_op jit(solution)/shard_map/inner/pallas_call | solution.py:339
  5.7 0.2 collective-permute-start.1
  5.9 0.4 %collective-permute-start.2 = (bf16[2,16,16,128]{3,2,1,0:T(8,128)(2,1)S(1)}, bf16[2,16,16,128]{3,2,1,0:T(8,128)(2,1)S(1)}, u32[]{:S(2)}, u32[]{:S(2)}) collective-permute-start(bf16[2,16,16,128]{3,2,1,0:T(8,128)(2,1)S(1)} %copy-done.2), channel_id=1, source_target_pairs={{0,1},{1,0},{2,3},{3,2},{4,5},{5,4},{6,7},{7,6},{8,9},{9,8},{10,11... | collective-permute-start | bytes 393224 | tf_op jit(solution)/shard_map/ppermute | solution.py:309
  6.3 0.9 %inner_back.1.part = f32[2,256,128]{2,1,0:T(8,128)S(1)} custom-call(bf16[2,16,16,128]{3,2,1,0:T(8,128)(2,1)S(1)} %get-tuple-element.64.edge, bf16[2,16,16,128]{3,2,1,0:T(8,128)(2,1)S(1)} %get-tuple-element.63.rest, bf16[3,3,3,128,128]{4,3,2,1,0:T(8,128)(2,1)S(1)} %copy-done), custom_call_target="tpu_custom_call" | custom-call | tf_op jit(solution)/shard_map/inner_back/pallas_call | solution.py:339
  7.1 0.6 %collective-permute-done.cross = bf16[2,16,16,128]{3,2,1,0:T(8,128)(2,1)S(1)} collective-permute-done((bf16[2,16,16,128]{3,2,1,0:T(8,128)(2,1)S(1)}, bf16[2,16,16,128]{3,2,1,0:T(8,128)(2,1)S(1)}, u32[]{:S(2)}, u32[]{:S(2)}) %collective-permute-start) | collective-permute-done | bytes 131104 | tf_op jit(solution)/shard_map/ppermute | solution.py:312
  7.8 0.5 %hidden.1 = (f32[2,256,128]{2,1,0:T(8,128)S(1)}, bf16[4,16,16,128]{3,2,1,0:T(8,128)(2,1)S(1)}, bf16[16,16,128]{2,1,0:T(8,128)(2,1)S(1)}) custom-call(f32[2,256,128]{2,1,0:T(8,128)S(1)} %inner.1.part, bf16[2,16,16,128]{3,2,1,0:T(8,128)(2,1)S(1)} %collective-permute-done.1.sib, bf16[2,16,16,128]{3,2,1,0:T(8,128)(2,1)S(1)} %collective-permute-done.cross, ...), custom_call_target="tpu_custom_call" | custom-call | tf_op jit(solution)/shard_map/hidden/pallas_call | solution.py:349
  8.3 0.6 %collective-permute-start.3 = (bf16[4,16,16,128]{3,2,1,0:T(8,128)(2,1)S(1)}, bf16[4,16,16,128]{3,2,1,0:T(8,128)(2,1)S(1)}, u32[]{:S(2)}, u32[]{:S(2)}) collective-permute-start(bf16[4,16,16,128]{3,2,1,0:T(8,128)(2,1)S(1)} %get-tuple-element.39.near), channel_id=1, source_target_pairs={{0,1},{1,0},{2,3},{3,2},{4,5},{5,4},{6,7},{7,6},{8,9},{9,8},{10,11... | collective-permute-start | bytes 786440 | tf_op jit(solution)/shard_map/ppermute | solution.py:309
  8.8 0.5 %hidden_grad.1.four = bf16[2,16,16,128]{3,2,1,0:T(8,128)(2,1)S(1)} custom-call(f32[2,256,128]{2,1,0:T(8,128)S(1)} %get-tuple-element.40.hidden, f32[2,256,128]{2,1,0:T(8,128)S(1)} %inner_back.1.part, bf16[2,16,16,128]{3,2,1,0:T(8,128)(2,1)S(1)} %collective-permute-done.2.sib.cot_sib, bf16[2,16,16,128]{3,2,1,0:T(8,128)(2,1)S(1)} %collective-permute-done.cross, ...), custom_call_target="tpu_custom_call" | custom-call | tf_op jit(solution)/shard_map/hidden_grad/pallas_call | solution.py:356
  9.4 0.1 collective-permute-start.4
  9.4 0.7 %second_own.1.own = f32[3,384,256]{2,1,0:T(8,128)S(1)} custom-call(bf16[2,16,16,128]{3,2,1,0:T(8,128)(2,1)S(1)} %copy-done.2, bf16[2,16,16,128]{3,2,1,0:T(8,128)(2,1)S(1)} %collective-permute-done.2.sib.cot_sib, bf16[4,16,16,128]{3,2,1,0:T(8,128)(2,1)S(1)} %get-tuple-element.39.near), custom_call_target="tpu_custom_call" | custom-call | tf_op jit(solution)/shard_map/second_own/pallas_call | solution.py:412
  10.1 0.8 %second_rest.1 = (f32[27,16,128]{2,1,0:T(8,128)S(1)}, bf16[27,16,128]{2,1,0:T(8,128)(2,1)S(1)}, bf16[27,16,128]{2,1,0:T(8,128)(2,1)S(1)}, bf16[27,16,128]{2,1,0:T(8,128)(2,1)S(1)}) custom-call(bf16[2,16,16,128]{3,2,1,0:T(8,128)(2,1)S(1)} %copy-done.2, bf16[2,16,16,128]{3,2,1,0:T(8,128)(2,1)S(1)} %collective-permute-done.2.sib.cot_sib, ...), custom_call_target="tpu_custom_call" | custom-call | tf_op jit(solution)/shard_map/second_rest/pallas_call | solution.py:418
  11.0 3.9 %collective-permute-start.5 = (bf16[27,16,128]{2,1,0:T(8,128)(2,1)S(1)}, bf16[27,16,128]{2,1,0:T(8,128)(2,1)S(1)}, u32[]{:S(2)}, u32[]{:S(2)}) collective-permute-start(bf16[27,16,128]{2,1,0:T(8,128)(2,1)S(1)} %get-tuple-element.47), channel_id=1, source_target_pairs={{0,6},{1,7},{2,4},{3,5},{4,2},{5,3},{6,0},{7,1},{8,14},{9,15},{10,... | collective-permute-start | bytes 331784 | tf_op jit(solution)/shard_map/ppermute | solution.py:309
  14.9 0.1 collective-permute-start.6
  15.0 0.5 %collective-permute-start.7 = (bf16[27,16,128]{2,1,0:T(8,128)(2,1)S(1)}, bf16[27,16,128]{2,1,0:T(8,128)(2,1)S(1)}, u32[]{:S(2)}, u32[]{:S(2)}) collective-permute-start(bf16[27,16,128]{2,1,0:T(8,128)(2,1)S(1)} %get-tuple-element.49), channel_id=1, source_target_pairs={{0,4},{1,5},{2,6},{3,7},{4,0},{5,1},{6,2},{7,3},{8,12},{9,13},{10,... | collective-permute-start | bytes 331784 | tf_op jit(solution)/shard_map/ppermute | solution.py:309
  15.6 1.3 %first_grad.1 = (f32[27,16,128]{2,1,0:T(8,128)S(1)}, bf16[27,16,128]{2,1,0:T(8,128)(2,1)S(1)}, bf16[27,16,128]{2,1,0:T(8,128)(2,1)S(1)}, bf16[27,16,128]{2,1,0:T(8,128)(2,1)S(1)}) custom-call(bf16[2,16,16,128]{3,2,1,0:T(8,128)(2,1)S(1)} %copy-done.3, bf16[2,16,16,128]{3,2,1,0:T(8,128)(2,1)S(1)} %collective-permute-done.1.sib, ...), custom_call_target="tpu_custom_call" | custom-call | tf_op jit(solution)/shard_map/first_grad/pallas_call | solution.py:368
  16.9 2.9 %collective-permute-start.8 = (bf16[27,16,128]{2,1,0:T(8,128)(2,1)S(1)}, bf16[27,16,128]{2,1,0:T(8,128)(2,1)S(1)}, u32[]{:S(2)}, u32[]{:S(2)}) collective-permute-start(bf16[27,16,128]{2,1,0:T(8,128)(2,1)S(1)} %get-tuple-element.52), channel_id=1, source_target_pairs={{0,6},{1,7},{2,4},{3,5},{4,2},{5,3},{6,0},{7,1},{8,14},{9,15},{10,... | collective-permute-start | bytes 331784 | tf_op jit(solution)/shard_map/ppermute | solution.py:309
  19.8 0.1 collective-permute-start.9
  19.9 0.5 %collective-permute-start.10 = (bf16[27,16,128]{2,1,0:T(8,128)(2,1)S(1)}, bf16[27,16,128]{2,1,0:T(8,128)(2,1)S(1)}, u32[]{:S(2)}, u32[]{:S(2)}) collective-permute-start(bf16[27,16,128]{2,1,0:T(8,128)(2,1)S(1)} %get-tuple-element.54), channel_id=1, source_target_pairs={{0,4},{1,5},{2,6},{3,7},{4,0},{5,1},{6,2},{7,3},{8,12},{9,13},{10,... | collective-permute-start | bytes 331784 | tf_op jit(solution)/shard_map/ppermute | solution.py:309
  20.5 0.7 %collective-permute-done.6.got_b = bf16[27,16,128]{2,1,0:T(8,128)(2,1)S(1)} collective-permute-done((bf16[27,16,128]{2,1,0:T(8,128)(2,1)S(1)}, bf16[27,16,128]{2,1,0:T(8,128)(2,1)S(1)}, u32[]{:S(2)}, u32[]{:S(2)}) %collective-permute-start.6) | collective-permute-done | bytes 110624 | tf_op jit(solution)/shard_map/ppermute | solution.py:309
  21.2 0.2 collective-permute-done.7.got_c
  21.4 1.6 %collective-permute-start.11 = (bf16[16,16,128]{2,1,0:T(8,128)(2,1)S(1)}, bf16[16,16,128]{2,1,0:T(8,128)(2,1)S(1)}, u32[]{:S(2)}, u32[]{:S(2)}) collective-permute-start(bf16[16,16,128]{2,1,0:T(8,128)(2,1)S(1)} %get-tuple-element.57), channel_id=1, source_target_pairs={{1,2},{3,4},{5,6},{7,8},{9,10},{11,12},{13,14},{17,18},{19,20},{21... | collective-permute-start | bytes 196616 | tf_op jit(solution)/shard_map/ppermute | solution.py:312
  22.9 1.2 %collective-permute-start.13 = (bf16[224,128]{1,0:T(8,128)(2,1)S(1)}, bf16[224,128]{1,0:T(8,128)(2,1)S(1)}, u32[]{:S(2)}, u32[]{:S(2)}) collective-permute-start(bf16[224,128]{1,0:T(8,128)(2,1)S(1)} %get-tuple-element.62), channel_id=1, source_target_pairs={{0,8},{1,9},{2,10},{3,11},{4,12},{5,13},{6,14},{7,15},{8,0},{9,1},... | collective-permute-start | bytes 172040 | tf_op jit(solution)/shard_map/ppermute | solution.py:309
  24.1 0.3 collective-permute-done.8.got_a
  24.4 1.0 %collective-permute-done.9.got_b = bf16[27,16,128]{2,1,0:T(8,128)(2,1)S(1)} collective-permute-done((bf16[27,16,128]{2,1,0:T(8,128)(2,1)S(1)}, bf16[27,16,128]{2,1,0:T(8,128)(2,1)S(1)}, u32[]{:S(2)}, u32[]{:S(2)}) %collective-permute-start.9) | collective-permute-done | bytes 110624 | tf_op jit(solution)/shard_map/ppermute | solution.py:309
  25.4 0.1 collective-permute-done.10.got_c
  25.5 3.0 %collective-permute-start.12 = (bf16[224,128]{1,0:T(8,128)(2,1)S(1)}, bf16[224,128]{1,0:T(8,128)(2,1)S(1)}, u32[]{:S(2)}, u32[]{:S(2)}) collective-permute-start(bf16[224,128]{1,0:T(8,128)(2,1)S(1)} %get-tuple-element.61), channel_id=1, source_target_pairs={{0,8},{1,9},{2,10},{3,11},{4,12},{5,13},{6,14},{7,15},{8,0},{9,1},... | collective-permute-start | bytes 172040 | tf_op jit(solution)/shard_map/ppermute | solution.py:309
  28.5 0.7 %second_last_sum.1 = f32[216,128]{1,0:T(8,128)} custom-call(f32[216,128]{1,0:T(8,128)S(1)} %get-tuple-element.50.refs_0_, bf16[224,128]{1,0:T(8,128)(2,1)S(1)} %collective-permute-done.13.refs_1_), custom_call_target="tpu_custom_call" | custom-call | tf_op jit(solution)/shard_map/second_last_sum/pallas_call | solution.py:406
  29.2 1.9 %response.1 = bf16[2,16,16,128]{3,2,1,0:T(8,128)(2,1)} custom-call(bf16[4,16,16,128]{3,2,1,0:T(8,128)(2,1)S(1)} %get-tuple-element.39.near, bf16[4,16,16,128]{3,2,1,0:T(8,128)(2,1)S(1)} %collective-permute-done.3.near_sib, bf16[16,16,128]{2,1,0:T(8,128)(2,1)S(1)} %collective-permute-done.11.cross, bf16[3,3,3,128,128]{4,3,2,1,0:T(8,128)(2,1)S(1)} %copy-done), custom_call_target="tpu_custom_call" | custom-call | tf_op jit(solution)/shard_map/response/pallas_call | solution.py:436
  31.1 0.8 %collective-permute-done.12.refs_1_ = bf16[224,128]{1,0:T(8,128)(2,1)S(1)} collective-permute-done((bf16[224,128]{1,0:T(8,128)(2,1)S(1)}, bf16[224,128]{1,0:T(8,128)(2,1)S(1)}, u32[]{:S(2)}, u32[]{:S(2)}) %collective-permute-start.12) | collective-permute-done | bytes 57376 | tf_op jit(solution)/shard_map/ppermute | solution.py:309
  31.9 0.7 %first_last_sum.1 = f32[216,128]{1,0:T(8,128)} custom-call(f32[216,128]{1,0:T(8,128)S(1)} %get-tuple-element.60.refs_0_, bf16[224,128]{1,0:T(8,128)(2,1)S(1)} %collective-permute-done.12.refs_1_), custom_call_target="tpu_custom_call" | custom-call | tf_op jit(solution)/shard_map/first_last_sum/pallas_call | solution.py:406
  (18 shorter events, 0.2 us)
Async XLA Ops:
  0.6 4.2 %copy-start.1 = (bf16[3,3,3,128,128]{4,3,2,1,0:T(8,128)(2,1)S(1)}, bf16[3,3,3,128,128]{4,3,2,1,0:T(8,128)(2,1)}, u32[]{:S(2)}) copy-start(bf16[3,3,3,128,128]{4,3,2,1,0:T(8,128)(2,1)} %first.1) | copy-start | bytes 2654212
  0.6 5.0 %copy-start.3 = (bf16[2,16,16,128]{3,2,1,0:T(8,128)(2,1)S(1)}, bf16[2,16,16,128]{3,2,1,0:T(8,128)(2,1)}, u32[]{:S(2)}) copy-start(bf16[2,16,16,128]{3,2,1,0:T(8,128)(2,1)} %own.1) | copy-start | bytes 393220
  0.7 5.3 %copy-start.2 = (bf16[2,16,16,128]{3,2,1,0:T(8,128)(2,1)S(1)}, bf16[2,16,16,128]{3,2,1,0:T(8,128)(2,1)}, u32[]{:S(2)}) copy-start(bf16[2,16,16,128]{3,2,1,0:T(8,128)(2,1)} %cot.3) | copy-start | bytes 393220
  0.7 5.6 %copy-start = (bf16[3,3,3,128,128]{4,3,2,1,0:T(8,128)(2,1)S(1)}, bf16[3,3,3,128,128]{4,3,2,1,0:T(8,128)(2,1)}, u32[]{:S(2)}) copy-start(bf16[3,3,3,128,128]{4,3,2,1,0:T(8,128)(2,1)} %second.3) | copy-start | bytes 2654212
  1.8 6.0 %collective-permute-start = (bf16[2,16,16,128]{3,2,1,0:T(8,128)(2,1)S(1)}, bf16[2,16,16,128]{3,2,1,0:T(8,128)(2,1)S(1)}, u32[]{:S(2)}, u32[]{:S(2)}) collective-permute-start(bf16[2,16,16,128]{3,2,1,0:T(8,128)(2,1)S(1)} %get-tuple-element.64.edge), channel_id=1, source_target_pairs={{1,2},{3,4},{5,6},{7,8},{9,10},{11,12},{13,14},{17,18},{19,20},{21... | collective-permute-start | bytes 393224 | tf_op jit(solution)/shard_map/ppermute | solution.py:312
  5.7 2.1 %collective-permute-start.1 = (bf16[2,16,16,128]{3,2,1,0:T(8,128)(2,1)S(1)}, bf16[2,16,16,128]{3,2,1,0:T(8,128)(2,1)S(1)}, u32[]{:S(2)}, u32[]{:S(2)}) collective-permute-start(bf16[2,16,16,128]{3,2,1,0:T(8,128)(2,1)S(1)} %copy-done.3), channel_id=1, source_target_pairs={{0,1},{1,0},{2,3},{3,2},{4,5},{5,4},{6,7},{7,6},{8,9},{9,8},{10,11... | collective-permute-start | bytes 393224 | tf_op jit(solution)/shard_map/ppermute | solution.py:309
  5.9 1.9 %collective-permute-start.2 = (bf16[2,16,16,128]{3,2,1,0:T(8,128)(2,1)S(1)}, bf16[2,16,16,128]{3,2,1,0:T(8,128)(2,1)S(1)}, u32[]{:S(2)}, u32[]{:S(2)}) collective-permute-start(bf16[2,16,16,128]{3,2,1,0:T(8,128)(2,1)S(1)} %copy-done.2), channel_id=1, source_target_pairs={{0,1},{1,0},{2,3},{3,2},{4,5},{5,4},{6,7},{7,6},{8,9},{9,8},{10,11... | collective-permute-start | bytes 393224 | tf_op jit(solution)/shard_map/ppermute | solution.py:309
  8.3 1.9 %collective-permute-start.3 = (bf16[4,16,16,128]{3,2,1,0:T(8,128)(2,1)S(1)}, bf16[4,16,16,128]{3,2,1,0:T(8,128)(2,1)S(1)}, u32[]{:S(2)}, u32[]{:S(2)}) collective-permute-start(bf16[4,16,16,128]{3,2,1,0:T(8,128)(2,1)S(1)} %get-tuple-element.39.near), channel_id=1, source_target_pairs={{0,1},{1,0},{2,3},{3,2},{4,5},{5,4},{6,7},{7,6},{8,9},{9,8},{10,11... | collective-permute-start | bytes 786440 | tf_op jit(solution)/shard_map/ppermute | solution.py:309
  9.4 6.2 %collective-permute-start.4 = (bf16[2,16,16,128]{3,2,1,0:T(8,128)(2,1)S(1)}, bf16[2,16,16,128]{3,2,1,0:T(8,128)(2,1)S(1)}, u32[]{:S(2)}, u32[]{:S(2)}) collective-permute-start(bf16[2,16,16,128]{3,2,1,0:T(8,128)(2,1)S(1)} %hidden_grad.1.four), channel_id=1, source_target_pairs={{0,1},{1,0},{2,3},{3,2},{4,5},{5,4},{6,7},{7,6},{8,9},{9,8},{10,11... | collective-permute-start | bytes 393224 | tf_op jit(solution)/shard_map/ppermute | solution.py:309
  11.0 8.9 %collective-permute-start.5 = (bf16[27,16,128]{2,1,0:T(8,128)(2,1)S(1)}, bf16[27,16,128]{2,1,0:T(8,128)(2,1)S(1)}, u32[]{:S(2)}, u32[]{:S(2)}) collective-permute-start(bf16[27,16,128]{2,1,0:T(8,128)(2,1)S(1)} %get-tuple-element.47), channel_id=1, source_target_pairs={{0,6},{1,7},{2,4},{3,5},{4,2},{5,3},{6,0},{7,1},{8,14},{9,15},{10,... | collective-permute-start | bytes 331784 | tf_op jit(solution)/shard_map/ppermute | solution.py:309
  14.9 6.3 %collective-permute-start.6 = (bf16[27,16,128]{2,1,0:T(8,128)(2,1)S(1)}, bf16[27,16,128]{2,1,0:T(8,128)(2,1)S(1)}, u32[]{:S(2)}, u32[]{:S(2)}) collective-permute-start(bf16[27,16,128]{2,1,0:T(8,128)(2,1)S(1)} %get-tuple-element.48), channel_id=1, source_target_pairs={{0,2},{1,3},{2,0},{3,1},{4,6},{5,7},{6,4},{7,5},{8,10},{9,11},{10,... | collective-permute-start | bytes 331784 | tf_op jit(solution)/shard_map/ppermute | solution.py:309
  15.0 6.3 %collective-permute-start.7 = (bf16[27,16,128]{2,1,0:T(8,128)(2,1)S(1)}, bf16[27,16,128]{2,1,0:T(8,128)(2,1)S(1)}, u32[]{:S(2)}, u32[]{:S(2)}) collective-permute-start(bf16[27,16,128]{2,1,0:T(8,128)(2,1)S(1)} %get-tuple-element.49), channel_id=1, source_target_pairs={{0,4},{1,5},{2,6},{3,7},{4,0},{5,1},{6,2},{7,3},{8,12},{9,13},{10,... | collective-permute-start | bytes 331784 | tf_op jit(solution)/shard_map/ppermute | solution.py:309
  16.9 7.5 %collective-permute-start.8 = (bf16[27,16,128]{2,1,0:T(8,128)(2,1)S(1)}, bf16[27,16,128]{2,1,0:T(8,128)(2,1)S(1)}, u32[]{:S(2)}, u32[]{:S(2)}) collective-permute-start(bf16[27,16,128]{2,1,0:T(8,128)(2,1)S(1)} %get-tuple-element.52), channel_id=1, source_target_pairs={{0,6},{1,7},{2,4},{3,5},{4,2},{5,3},{6,0},{7,1},{8,14},{9,15},{10,... | collective-permute-start | bytes 331784 | tf_op jit(solution)/shard_map/ppermute | solution.py:309
  19.8 5.6 %collective-permute-start.9 = (bf16[27,16,128]{2,1,0:T(8,128)(2,1)S(1)}, bf16[27,16,128]{2,1,0:T(8,128)(2,1)S(1)}, u32[]{:S(2)}, u32[]{:S(2)}) collective-permute-start(bf16[27,16,128]{2,1,0:T(8,128)(2,1)S(1)} %get-tuple-element.53), channel_id=1, source_target_pairs={{0,2},{1,3},{2,0},{3,1},{4,6},{5,7},{6,4},{7,5},{8,10},{9,11},{10,... | collective-permute-start | bytes 331784 | tf_op jit(solution)/shard_map/ppermute | solution.py:309
  19.9 5.5 %collective-permute-start.10 = (bf16[27,16,128]{2,1,0:T(8,128)(2,1)S(1)}, bf16[27,16,128]{2,1,0:T(8,128)(2,1)S(1)}, u32[]{:S(2)}, u32[]{:S(2)}) collective-permute-start(bf16[27,16,128]{2,1,0:T(8,128)(2,1)S(1)} %get-tuple-element.54), channel_id=1, source_target_pairs={{0,4},{1,5},{2,6},{3,7},{4,0},{5,1},{6,2},{7,3},{8,12},{9,13},{10,... | collective-permute-start | bytes 331784 | tf_op jit(solution)/shard_map/ppermute | solution.py:309
  21.4 7.8 %collective-permute-start.11 = (bf16[16,16,128]{2,1,0:T(8,128)(2,1)S(1)}, bf16[16,16,128]{2,1,0:T(8,128)(2,1)S(1)}, u32[]{:S(2)}, u32[]{:S(2)}) collective-permute-start(bf16[16,16,128]{2,1,0:T(8,128)(2,1)S(1)} %get-tuple-element.57), channel_id=1, source_target_pairs={{1,2},{3,4},{5,6},{7,8},{9,10},{11,12},{13,14},{17,18},{19,20},{21... | collective-permute-start | bytes 196616 | tf_op jit(solution)/shard_map/ppermute | solution.py:312
  22.9 5.6 %collective-permute-start.13 = (bf16[224,128]{1,0:T(8,128)(2,1)S(1)}, bf16[224,128]{1,0:T(8,128)(2,1)S(1)}, u32[]{:S(2)}, u32[]{:S(2)}) collective-permute-start(bf16[224,128]{1,0:T(8,128)(2,1)S(1)} %get-tuple-element.62), channel_id=1, source_target_pairs={{0,8},{1,9},{2,10},{3,11},{4,12},{5,13},{6,14},{7,15},{8,0},{9,1},... | collective-permute-start | bytes 172040 | tf_op jit(solution)/shard_map/ppermute | solution.py:309
  25.5 6.3 %collective-permute-start.12 = (bf16[224,128]{1,0:T(8,128)(2,1)S(1)}, bf16[224,128]{1,0:T(8,128)(2,1)S(1)}, u32[]{:S(2)}, u32[]{:S(2)}) collective-permute-start(bf16[224,128]{1,0:T(8,128)(2,1)S(1)} %get-tuple-element.61), channel_id=1, source_target_pairs={{0,8},{1,9},{2,10},{3,11},{4,12},{5,13},{6,14},{7,15},{8,0},{9,1},... | collective-permute-start | bytes 172040 | tf_op jit(solution)/shard_map/ppermute | solution.py:309
